TPU v7x, 32 devices: a whole 2x2x4 slice. The times are simulated.
32 devices in a mesh: span: 4 (over y, x), ty: 2 (over core), tx: 4 (over z).
Axes of the slice: x: 2, y: 2, z: 4, core: 2. Of those that a mesh axis runs over, the one named last changes fastest.
Arguments:
- queries: bfloat16 [4, 2, 4, 128, 1536], P('span', 'ty', 'tx'), may hold values from -125 to 125
- key_value: bfloat16 [4, 2, 4, 128, 1024], P('span', 'ty', 'tx'), may hold values from -5 to 5
- pattern: int32 [4, 2, 4, 5], P('span', 'ty', 'tx'), may hold values from 0 to 1
- counts: int32 [4, 2, 4], replicated, may hold values from 64 to 128, as said below
- span_mask: int32 [4, 4], replicated, may hold values from 0 to 1, as said below
Outputs:
- attended: bfloat16 [4, 2, 4, 128, 1536], P('span', 'ty', 'tx')
Inputs may be any that keep to these rules, and one draw needn't show every extreme that they name: `counts`: in every span some tile has all 128 slots valid. span_mask[c, c] is 1 and span_mask[c, c'] is 0 for c' > c.
All inputs are finite; a program needn't handle non-finite values.
Results may differ from a plain program's by a relative error of at most 0.006.
Values may be sent and summed in bfloat16 or wider, within the bound.
No kernel may reach another device: no remote copies, remote signals or barrier semaphores. Data moves between devices by JAX's collectives and lax.ppermute only.
A program may use at most 64 MiB of HBM per device.

v0:
```python
import jax
import jax.numpy as jnp
from jax import lax
from jax.sharding import PartitionSpec as P

HEAD_SIZE = 128
NEIGH = 5


def padded(block, sides, width):
    for axis, dim in sides:
        count = lax.axis_size(axis)
        forward = [(i, i + 1) for i in range(count - 1)]
        backward = [(target, source) for source, target in forward]
        low = lax.ppermute(
            lax.slice_in_dim(block, block.shape[dim] - width, None, axis=dim), axis, forward
        )
        high = lax.ppermute(lax.slice_in_dim(block, 0, width, axis=dim), axis, backward)
        block = jnp.concatenate([low, block, high], axis=dim)
    return block


def cross_tiles(extended):
    return jnp.stack(
        [
            extended[:, 1, 1],
            extended[:, 0, 1],
            extended[:, 2, 1],
            extended[:, 1, 0],
            extended[:, 1, 2],
        ],
        axis=1,
    )


def shards(queries, key_value, pattern, counts, span_mask):
    tok_rows = queries.shape[3]
    kv_width = key_value.shape[4] // 2
    kv_heads = kv_width // HEAD_SIZE
    groups = queries.shape[4] // kv_width
    scale = HEAD_SIZE ** (-0.5)
    my_span = lax.axis_index("span")
    my_row = lax.axis_index("ty")
    my_col = lax.axis_index("tx")
    zero_index = jnp.asarray(0).astype(jnp.int32)
    padded_counts = jnp.pad(counts, ((0, 0), (1, 1), (1, 1)))
    window = lax.dynamic_slice(padded_counts, (zero_index, my_row, my_col), (counts.shape[0], 3, 3))
    near_counts = cross_tiles(window)
    own_count = lax.dynamic_index_in_dim(window[:, 1, 1], my_span, 0, keepdims=False)
    allowed = pattern.reshape(NEIGH) > 0
    span_row = lax.dynamic_index_in_dim(span_mask, my_span, 0, keepdims=False) > 0
    query_rows = queries.reshape(tok_rows, kv_heads, groups, HEAD_SIZE)
    row_ids = jnp.arange(tok_rows, dtype=jnp.int32)
    initial = (
        jnp.full((tok_rows, kv_heads, groups), -1e30, jnp.float32),
        jnp.zeros((tok_rows, kv_heads, groups), jnp.float32),
        jnp.zeros((tok_rows, kv_heads, groups, HEAD_SIZE), jnp.float32),
    )
    cached = lax.all_gather(key_value, "span", axis=0, tiled=True)
    extended = padded(cached, (("ty", 1), ("tx", 2)), 1)
    state_now = initial
    kv_piece = cross_tiles(extended)
    for offset in range(kv_piece.shape[0]):
        key_value_block = kv_piece[offset]
        source_span = 0 + offset
        attend_run_max, attend_run_sum, attend_accumulated = state_now
        key_matrix = key_value_block[:, :, :kv_width].reshape(-1, kv_heads, HEAD_SIZE)
        value_rows = key_value_block[:, :, kv_width:].reshape(-1, kv_heads, HEAD_SIZE)
        near_count = lax.dynamic_index_in_dim(near_counts, source_span, 0, keepdims=False)
        open_span = lax.dynamic_index_in_dim(span_row, source_span, 0, keepdims=False)
        live_keys = (
            (row_ids[None, :] < near_count[:, None]) & allowed[:, None] & open_span
        ).reshape(-1)
        scores = (
            jnp.einsum("tkgd,lkd->tkgl", query_rows, key_matrix, preferred_element_type=jnp.float32)
            * scale
        )
        scores = jnp.where(live_keys, scores, -1e30)
        new_max = jnp.maximum(attend_run_max, jnp.max(scores, axis=-1))
        weights = jnp.where(live_keys, jnp.exp(scores - new_max[..., None]), 0.0)
        fade_factor = jnp.exp(attend_run_max - new_max)
        attend_run_sum = attend_run_sum * fade_factor + jnp.sum(weights, axis=-1)
        update = jnp.einsum(
            "tkgl,lkd->tkgd",
            weights.astype(jnp.bfloat16),
            value_rows,
            preferred_element_type=jnp.float32,
        )
        attend_accumulated = attend_accumulated * fade_factor[..., None] + update
        final_output = (new_max, attend_run_sum, attend_accumulated)
        state_now = final_output
    run_max, run_sum, accumulated = state_now
    attended = jnp.where(
        row_ids[:, None, None, None] < own_count, accumulated / run_sum[..., None], 0.0
    )
    return attended.reshape(1, 1, 1, tok_rows, -1).astype(jnp.bfloat16)


def solution(mesh):
    return jax.shard_map(
        shards,
        mesh=mesh,
        in_specs=(
            P("span", "ty", "tx", None, None),
            P("span", "ty", "tx", None, None),
            P("span", "ty", "tx", None),
            P(),
            P(),
        ),
        out_specs=P("span", "ty", "tx", None, None),
        check_vma=False,
    )
```

profile of v0, /device:TPU:0, one launch (start us, length us, event | category | flops | bytes accessed | tf_op | source)
XLA Modules:
  0.0 171.8 jit_solution(7512742476200297336)
XLA Ops:
  7.3 31.3 %all-gather.2.cloned.1.call-done = bf16[4,1,1,128,1024]{4,3,2,1,0:T(8,128)(2,1)} async-done(((bf16[1,1,1,128,1024]{4,3,2,1,0:T(8,128)(2,1)}), bf16[4,1,1,128,1024]{4,3,2,1,0:T(8,128)(2,1)}) %all-gather.2.cloned.1.call-update) | async-done | bytes 1048592 | tf_op jit(solution)/shard_map/all_gather | solution.py:59
  39.8 3.2 %collective-permute-start = (bf16[4,1,1,128,1024]{4,3,0,2,1:T(8,128)(2,1)}, bf16[4,1,1,128,1024]{4,3,0,2,1:T(8,128)(2,1)S(1)}, u32[]{:S(2)}, u32[]{:S(2)}) collective-permute-start(bf16[4,1,1,128,1024]{4,3,0,2,1:T(8,128)(2,1)} %bitcast.169), channel_id=1, source_target_pairs={{0,4},{1,5},{2,6},{3,7},{8,12},{9,13},{10,14},{11,15},{16,20},{17,... | collective-permute-start | bytes 3145736 | tf_op jit(solution)/shard_map/ppermute | solution.py:15
  43.3 2.1 %collective-permute-done = bf16[4,1,1,128,1024]{4,3,0,2,1:T(8,128)(2,1)S(1)} collective-permute-done((bf16[4,1,1,128,1024]{4,3,0,2,1:T(8,128)(2,1)}, bf16[4,1,1,128,1024]{4,3,0,2,1:T(8,128)(2,1)S(1)}, u32[]{:S(2)}, u32[]{:S(2)}) %collective-permute-start) | collective-permute-done | bytes 1048608 | tf_op jit(solution)/shard_map/ppermute | solution.py:15
  45.4 1.9 %pad_maximum_fusion = bf16[4,3,1,128,1024]{4,3,2,1,0:T(8,128)(2,1)S(1)} fusion(bf16[4,1,1,128,1024]{4,3,2,1,0:T(8,128)(2,1)S(1)} %bitcast.170, bf16[4,1,1,128,1024]{4,3,2,1,0:T(8,128)(2,1)} %all-gather.2.cloned.1.call-done, bf16[4,1,1,128,1024]{4,3,2,1,0:T(8,128)(2,1)S(1)} %bitcast.171), kind=kLoop, calls=%fused_computation.20 | loop fusion | flops 3145728 | bytes 6291456 | tf_op jit(solution)/shard_map/concatenate | solution.py:19
  47.4 2.2 %copy.51 = bf16[4,3,1,128,1024]{4,3,0,2,1:T(8,128)(2,1)} copy(bf16[4,3,1,128,1024]{4,3,2,1,0:T(8,128)(2,1)S(1)} %pad_maximum_fusion) | data formatting | bytes 6291456 | tf_op jit(solution)/shard_map/concatenate | solution.py:19
  49.6 5.1 %collective-permute-start.2 = (bf16[4,3,1,128,1024]{4,3,0,2,1:T(8,128)(2,1)}, bf16[4,3,1,128,1024]{4,3,0,2,1:T(8,128)(2,1)}, u32[]{:S(2)}, u32[]{:S(2)}) collective-permute-start(bf16[4,3,1,128,1024]{4,3,0,2,1:T(8,128)(2,1)} %copy.51), channel_id=1, source_target_pairs={{0,1},{1,2},{2,3},{4,5},{5,6},{6,7},{8,9},{9,10},{10,11},{12,13},{... | collective-permute-start | bytes 9437192 | tf_op jit(solution)/shard_map/ppermute | solution.py:15
  59.7 1.3 iota_compare_fusion.4
  63.2 2.7 %fusion.93 = (pred[640]{0:T(1024)(128)(4,1)S(1)}, pred[640]{0:T(1024)(128)(4,1)S(1)}, pred[640]{0:T(1024)(128)(4,1)S(1)}, pred[640]{0:T(1024)(128)(4,1)S(1)}) fusion(s32[5]{0:T(128)S(1)} %get-tuple-element.7, pred[]{:T(512)} %bitcast.19, pred[5]{0:T(512)(128)(4,1)S(1)} %compare_bitcast_fusion, pred[]{:T(512)} %bitcast.26, s32[5]{0:T(128)S(1)} %get-tuple-element.6, ...), kind=kLoop, calls=%fused_computation.103 | loop fusion | flops 7680 | bytes 2649 | tf_op jit(solution)/shard_map/and | solution.py:72
  68.6 52.6 %collective-permute-done.2 = bf16[4,3,1,128,1024]{4,3,0,2,1:T(8,128)(2,1)} collective-permute-done((bf16[4,3,1,128,1024]{4,3,0,2,1:T(8,128)(2,1)}, bf16[4,3,1,128,1024]{4,3,0,2,1:T(8,128)(2,1)}, u32[]{:S(2)}, u32[]{:S(2)}) %collective-permute-start.2) | collective-permute-done | bytes 3145760 | tf_op jit(solution)/shard_map/ppermute | solution.py:15
  122.5 4.3 %collective-permute-done.3 = bf16[4,3,1,128,1024]{4,3,2,1,0:T(8,128)(2,1)} collective-permute-done((bf16[4,3,1,128,1024]{4,3,2,1,0:T(8,128)(2,1)S(1)}, bf16[4,3,1,128,1024]{4,3,2,1,0:T(8,128)(2,1)}, u32[]{:S(2)}, u32[]{:S(2)}) %collective-permute-start.3) | collective-permute-done | bytes 3145760 | tf_op jit(solution)/shard_map/ppermute | solution.py:18
  128.1 1.6 slice_bitcast_fusion.2
  131.0 2.3 %reshape.186 = bf16[640,4,128]{2,1,0:T(4,128)(2,1)} reshape(bf16[5,128,512]{2,1,0:T(8,128)(2,1)} %get-tuple-element.29) | data formatting | bytes 1310720 | tf_op jit(solution)/shard_map/reshape | solution.py:68
  133.3 2.3 %reshape.185 = bf16[640,4,128]{2,1,0:T(4,128)(2,1)} reshape(bf16[5,128,512]{2,1,0:T(8,128)(2,1)} %get-tuple-element.30) | data formatting | bytes 1310720 | tf_op jit(solution)/shard_map/reshape | solution.py:67
  135.6 2.4 %fusion.121 = (bf16[5,128,512]{2,1,0:T(8,128)(2,1)}, bf16[5,128,512]{2,1,0:T(8,128)(2,1)}) fusion(bf16[5,128,1024]{2,1,0:T(8,128)(2,1)} %get-tuple-element.22), kind=kLoop, calls=%fused_computation.133 | loop fusion | bytes 2621440 | tf_op jit(solution)/shard_map/slice | solution.py:68
  138.1 2.3 %reshape.190 = bf16[640,4,128]{2,1,0:T(4,128)(2,1)} reshape(bf16[5,128,512]{2,1,0:T(8,128)(2,1)} %get-tuple-element.25) | data formatting | bytes 1310720 | tf_op jit(solution)/shard_map/reshape | solution.py:68
  140.4 2.3 %reshape.189 = bf16[640,4,128]{2,1,0:T(4,128)(2,1)} reshape(bf16[5,128,512]{2,1,0:T(8,128)(2,1)} %get-tuple-element.26) | data formatting | bytes 1310720 | tf_op jit(solution)/shard_map/reshape | solution.py:67
  143.9 2.3 %reshape.188 = bf16[640,4,128]{2,1,0:T(4,128)(2,1)} reshape(bf16[5,128,512]{2,1,0:T(8,128)(2,1)} %get-tuple-element.27) | data formatting | bytes 1310720 | tf_op jit(solution)/shard_map/reshape | solution.py:68
  146.3 2.3 %reshape.187 = bf16[640,4,128]{2,1,0:T(4,128)(2,1)} reshape(bf16[5,128,512]{2,1,0:T(8,128)(2,1)} %get-tuple-element.28) | data formatting | bytes 1310720 | tf_op jit(solution)/shard_map/reshape | solution.py:67
  153.1 2.5 %fusion.8 = (f32[128,4,3]{0,2,1:T(4,128)S(1)}, f32[128,4,3]{0,2,1:T(4,128)S(1)}) fusion(f32[4,640,128,3]{2,1,3,0:T(8,128)S(1)} %get-tuple-element.50, f32[128,4,3]{0,2,1:T(4,128)S(1)} %get-tuple-element.34, pred[640]{0:T(1024)(128)(4,1)S(1)} %get-tuple-element.38, f32[128,4,3]{0,2,1:T(4,128)S(1)} %get-tuple-element.20, ...), kind=kLoop, calls=%fused_computation.21 | loop fusion | flops 9827328 | bytes 7890176 | tf_op jit(solution)/shard_map/reduce_sum | solution.py:82
  155.7 2.7 %fusion.12 = (f32[128,4,3]{0,2,1:T(4,128)S(1)}, f32[128,4,3]{0,2,1:T(4,128)S(1)}) fusion(f32[4,640,128,3]{2,1,3,0:T(8,128)S(1)} %get-tuple-element.46, f32[128,4,3]{0,2,1:T(4,128)S(1)} %get-tuple-element.19, pred[640]{0:T(1024)(128)(4,1)S(1)} %get-tuple-element.36, f32[128,4,3]{0,2,1:T(4,128)S(1)} %get-tuple-element.18, ...), kind=kLoop, calls=%fused_computation.25 | loop fusion | flops 9827328 | bytes 7890176 | tf_op jit(solution)/shard_map/reduce_sum | solution.py:82
  158.5 1.4 fusion.56
  159.9 1.4 fusion.59
  161.3 1.4 fusion.62
  162.6 1.4 fusion.73
  (54 shorter events, 22.6 us)
Async XLA Ops:
  6.5 32.0 %all-gather.2.cloned.1.call-start = ((), (), s32[]{:S(2)}) async-start(), calls=%async_computation | async-start | bytes 1310720 | tf_op jit(solution)/shard_map/all_gather | solution.py:59
  38.6 4.8 %collective-permute-start.1 = (bf16[4,1,1,128,1024]{4,3,0,2,1:T(8,128)(2,1)}, bf16[4,1,1,128,1024]{4,3,0,2,1:T(8,128)(2,1)S(1)}, u32[]{:S(2)}, u32[]{:S(2)}) collective-permute-start(bf16[4,1,1,128,1024]{4,3,0,2,1:T(8,128)(2,1)} %bitcast.168), channel_id=1, source_target_pairs={{4,0},{5,1},{6,2},{7,3},{12,8},{13,9},{14,10},{15,11},{20,16},{21,... | collective-permute-start | bytes 3145736 | tf_op jit(solution)/shard_map/ppermute | solution.py:18
  39.8 5.6 %collective-permute-start = (bf16[4,1,1,128,1024]{4,3,0,2,1:T(8,128)(2,1)}, bf16[4,1,1,128,1024]{4,3,0,2,1:T(8,128)(2,1)S(1)}, u32[]{:S(2)}, u32[]{:S(2)}) collective-permute-start(bf16[4,1,1,128,1024]{4,3,0,2,1:T(8,128)(2,1)} %bitcast.169), channel_id=1, source_target_pairs={{0,4},{1,5},{2,6},{3,7},{8,12},{9,13},{10,14},{11,15},{16,20},{17,... | collective-permute-start | bytes 3145736 | tf_op jit(solution)/shard_map/ppermute | solution.py:15
  43.3 6.3 %copy-start = (bf16[4,1,1,128,1024]{4,3,0,2,1:T(8,128)(2,1)}, bf16[4,1,1,128,1024]{4,3,0,2,1:T(8,128)(2,1)S(1)}, u32[]{:S(2)}) copy-start(bf16[4,1,1,128,1024]{4,3,0,2,1:T(8,128)(2,1)S(1)} %collective-permute-done.1) | copy-start | bytes 3145732
  45.4 4.2 %copy-start.2 = (bf16[4,1,1,128,1024]{4,3,0,2,1:T(8,128)(2,1)}, bf16[4,1,1,128,1024]{4,3,0,2,1:T(8,128)(2,1)S(1)}, u32[]{:S(2)}) copy-start(bf16[4,1,1,128,1024]{4,3,0,2,1:T(8,128)(2,1)S(1)} %collective-permute-done) | copy-start | bytes 3145732
  47.4 9.9 %copy-start.10 = (s32[4,2,4]{2,1,0:T(2,128)S(1)}, s32[4,2,4]{2,1,0:T(2,128)}, u32[]{:S(2)}) copy-start(s32[4,2,4]{2,1,0:T(2,128)} %param.8) | copy-start | bytes 388
  49.6 71.6 %collective-permute-start.2 = (bf16[4,3,1,128,1024]{4,3,0,2,1:T(8,128)(2,1)}, bf16[4,3,1,128,1024]{4,3,0,2,1:T(8,128)(2,1)}, u32[]{:S(2)}, u32[]{:S(2)}) collective-permute-start(bf16[4,3,1,128,1024]{4,3,0,2,1:T(8,128)(2,1)} %copy.51), channel_id=1, source_target_pairs={{0,1},{1,2},{2,3},{4,5},{5,6},{6,7},{8,9},{9,10},{10,11},{12,13},{... | collective-permute-start | bytes 9437192 | tf_op jit(solution)/shard_map/ppermute | solution.py:15
  54.7 72.1 %collective-permute-start.3 = (bf16[4,3,1,128,1024]{4,3,2,1,0:T(8,128)(2,1)S(1)}, bf16[4,3,1,128,1024]{4,3,2,1,0:T(8,128)(2,1)}, u32[]{:S(2)}, u32[]{:S(2)}) collective-permute-start(bf16[4,3,1,128,1024]{4,3,2,1,0:T(8,128)(2,1)S(1)} %pad_maximum_fusion), channel_id=1, source_target_pairs={{1,0},{2,1},{3,2},{5,4},{6,5},{7,6},{9,8},{10,9},{11,10},{13,12},{... | collective-permute-start | bytes 9437192 | tf_op jit(solution)/shard_map/ppermute | solution.py:18
  59.7 8.8 %copy-start.1 = (bf16[4,1,1,128,1024]{4,3,0,2,1:T(8,128)(2,1)S(1)}, bf16[4,1,1,128,1024]{4,3,0,2,1:T(8,128)(2,1)}, u32[]{:S(2)}) copy-start(bf16[4,1,1,128,1024]{4,3,0,2,1:T(8,128)(2,1)} %copy-done) | copy-start | bytes 3145732
  148.7 2.0 %copy-start.5 = (bf16[640,4,128]{2,1,0:T(4,128)(2,1)S(1)}, bf16[640,4,128]{2,1,0:T(4,128)(2,1)}, u32[]{:S(2)}) copy-start(bf16[640,4,128]{2,1,0:T(4,128)(2,1)} %reshape.187) | copy-start | bytes 1966084
  149.9 1.6 copy-start.4
  150.7 1.6 copy-start.3
  155.7 2.8 %copy-start.9 = (bf16[640,4,128]{2,1,0:T(4,128)(2,1)S(1)}, bf16[640,4,128]{2,1,0:T(4,128)(2,1)}, u32[]{:S(2)}) copy-start(bf16[640,4,128]{2,1,0:T(4,128)(2,1)} %reshape.184) | copy-start | bytes 1966084
  158.5 1.4 copy-start.7
  159.9 1.4 copy-start.8
  161.2 1.4 copy-start.6
  161.2 1.4 copy-start.11
Sparse Core Ops, SparseCore 0:
  9.2 29.3 all-gather.1
where the time goes:
time: 172 us
  waiting for transfers between devices  91.3 us (53%)
  local copies, waits for them, and re-layouts  34.7 us (20%)
  between operations  13.7 us (8%)
  other arithmetic  12.6 us (7%)
  starting transfers between devices  10.8 us (6%)
  matrix products  8.64 us (5%)
    ppermute x2, waiting for transfers between devices, padded(): lax.ppermute(lax.slice_in_dim(block, block.shape[dim] - width, None, axis...  54.7 us
    all_gather x1, waiting for transfers between devices, shards(): cached = lax.all_gather(key_value, 'span', axis=0, tiled=True)  31.3 us
    ppermute x2, starting transfers between devices, padded(): lax.ppermute(lax.slice_in_dim(block, block.shape[dim] - width, None, axis...  8.26 us
    reshape x4, local copies, waits for them, and re-layouts, shards(): key_value_block[:, :, kv_width:].reshape(-1, kv_heads, HEAD_SIZE)  7.99 us
    reshape x4, local copies, waits for them, and re-layouts, shards(): key_value_block[:, :, :kv_width].reshape(-1, kv_heads, HEAD_SIZE)  7.14 us
    dot_general x4, matrix products, shards(): jnp.einsum('tkgl,lkd->tkgd', weights.astype(jnp.bfloat16), value_rows, pr...  5.44 us
    reduce_sum x2, other arithmetic, shards(): attend_run_sum = attend_run_sum * fade_factor + jnp.sum(weights, axis=-1)  5.27 us
    unnamed x29, local copies, waits for them, and re-layouts  5.22 us
  transfers between devices with their start and end apart: 5, of which 5 were waited for; matrix products, arithmetic and copies ran while one was open for 8% of the time, Pallas kernels for 0%

commit v1 on v0

v1 whole, which is shorter than its diff:
```python
import functools

import jax
import jax.numpy as jnp
from jax import lax
from jax.experimental import pallas as pl
from jax.experimental.pallas import tpu as pltpu
from jax.sharding import PartitionSpec as P

HEAD_SIZE = 128
NEIGH = 5
EXTRA = 16
DEAD = -1e30
VMEM_LIMIT = 40 * 1024 * 1024


def vmem():
    return pl.BlockSpec(memory_space=pltpu.VMEM)


def smem():
    return pl.BlockSpec(memory_space=pltpu.SMEM)


def pairings(count):
    found = []
    for first in (0, 1):
        pairs = [(i, i + 1) for i in range(first, count - 1, 2)]
        if pairs:
            found.append(pairs)
    return found


def swap(block, axis, pairs):
    return lax.ppermute(block, axis, pairs + [(b, a) for a, b in pairs])


def partner(place, count, first):
    low = lax.rem(place + first, 2) == 0
    step = jnp.where(low, 1, -1)
    other = place + step
    return jnp.where((other >= 0) & (other < count), step, 0)


def split_kv(spans, kv_ref, *piece_refs):
    me = lax.axis_index("span")
    kv_width = kv_ref.shape[1] // 2
    for k in range(spans):
        head = me ^ k
        for part in range(2):
            start = pl.multiple_of(part * kv_width + head * HEAD_SIZE, HEAD_SIZE)
            piece_refs[k][part] = kv_ref[:, pl.ds(start, HEAD_SIZE)]


def split_q(spans, pattern_ref, q_ref, *piece_refs):
    me = lax.axis_index("span")
    rows = q_ref.shape[0]
    width = q_ref.shape[1] // spans
    row_ids = lax.broadcasted_iota(jnp.int32, (EXTRA, width), 0)
    extra = jnp.zeros((EXTRA, width), jnp.float32)
    for o in range(NEIGH):
        value = pattern_ref[o].astype(jnp.float32)
        extra = jnp.where(row_ids == o, value, extra)
    extra = extra.astype(jnp.bfloat16)
    for k in range(spans):
        start = pl.multiple_of((me ^ k) * width, HEAD_SIZE)
        piece_refs[k][:rows] = q_ref[:, pl.ds(start, width)]
        piece_refs[k][rows:] = extra


def attend(spans, ty_count, tx_count, ways, *refs):
    counts_ref, mask_ref = refs[:2]
    q_refs = refs[2 : 2 + spans]
    tile_refs = refs[2 + spans : 3 + spans + len(ways)]
    out_refs = refs[3 + spans + len(ways) : 3 + 2 * spans + len(ways)]
    score_ref, top_ref, sum_ref, acc_ref = refs[3 + 2 * spans + len(ways) :]
    me, row, col = (lax.axis_index(a) for a in ("span", "ty", "tx"))
    tok_rows = out_refs[0].shape[0]
    groups = out_refs[0].shape[1] // HEAD_SIZE
    scale = HEAD_SIZE ** (-0.5)
    slots = tile_refs[0].shape[2]
    lanes = lax.broadcasted_iota(jnp.int32, (1, slots), 1)

    steps = []
    for axis, first in ways:
        place, count = (row, ty_count) if axis == "ty" else (col, tx_count)
        steps.append(partner(place, count, first))

    def tile_count(span, step_row, step_col):
        index = (span * ty_count + row + step_row) * tx_count + col + step_col
        return counts_ref[index]

    def bias_of(k, other):
        span = me ^ other
        extra = q_refs[k][tok_rows:, :HEAD_SIZE].astype(jnp.float32)
        parts = [jnp.where((lanes < tile_count(span, 0, 0)) & (extra[0:1] > 0), 0.0, DEAD)]
        for (axis, _), step in zip(ways, steps, strict=True):
            base = 1 if axis == "ty" else 3
            chosen = jnp.where(step > 0, extra[base + 1 : base + 2], extra[base : base + 1])
            near = tile_count(span, *((step, 0) if axis == "ty" else (0, step)))
            near = jnp.where(step == 0, 0, near)
            parts.append(jnp.where((lanes < near) & (chosen > 0), 0.0, DEAD))
        return jnp.concatenate(parts, axis=1)

    tiles = 1 + len(ways)
    for k in range(spans):
        span = me ^ k
        query = jnp.concatenate(
            [q_refs[k][:tok_rows, g * HEAD_SIZE : (g + 1) * HEAD_SIZE] for g in range(groups)], axis=0
        )
        top_ref[...] = jnp.full(top_ref.shape, DEAD, jnp.float32)
        sum_ref[...] = jnp.zeros(sum_ref.shape, jnp.float32)
        acc_ref[...] = jnp.zeros(acc_ref.shape, jnp.float32)
        for other in range(spans):

            @pl.when(mask_ref[span * spans + (me ^ other)] > 0)
            def _(other=other):
                keys = jnp.concatenate([t[other, 0] for t in tile_refs], axis=0)
                scores = lax.dot_general(
                    query, keys, (((1,), (1,)), ((), ())), preferred_element_type=jnp.float32
                )
                scores = scores * scale + bias_of(k, other)
                score_ref[other] = scores
                top = top_ref[...]
                for t in range(tiles):
                    top = jnp.maximum(top, scores[:, t * slots : (t + 1) * slots])
                top_ref[...] = top

        top = jnp.max(top_ref[...], axis=1, keepdims=True)
        for other in range(spans):

            @pl.when(mask_ref[span * spans + (me ^ other)] > 0)
            def _(other=other):
                values = jnp.concatenate([t[other, 1] for t in tile_refs], axis=0)
                weights = jnp.exp(score_ref[other] - top)
                total = sum_ref[...]
                for t in range(tiles):
                    total = total + weights[:, t * slots : (t + 1) * slots]
                sum_ref[...] = total
                acc_ref[...] += jnp.dot(
                    weights.astype(jnp.bfloat16), values, preferred_element_type=jnp.float32
                )

        total = jnp.sum(sum_ref[...], axis=1, keepdims=True)
        result = acc_ref[...] / jnp.where(top > 0.5 * DEAD, total, jnp.nan)
        valid = lax.broadcasted_iota(jnp.int32, (tok_rows, HEAD_SIZE), 0) < tile_count(span, 0, 0)
        for g in range(groups):
            part = jnp.where(valid, result[g * tok_rows : (g + 1) * tok_rows], 0.0)
            out_refs[k][:, g * HEAD_SIZE : (g + 1) * HEAD_SIZE] = part.astype(jnp.bfloat16)


def join(spans, *refs):
    me = lax.axis_index("span")
    out_ref = refs[spans]
    width = refs[0].shape[1]
    for k in range(spans):
        start = pl.multiple_of((me ^ k) * width, HEAD_SIZE)
        out_ref[:, pl.ds(start, width)] = refs[k][...]


def shards(queries, key_value, pattern, counts, span_mask):
    spans, ty_count, tx_count = (lax.axis_size(a) for a in ("span", "ty", "tx"))
    tok_rows = queries.shape[3]
    kv_heads = key_value.shape[4] // (2 * HEAD_SIZE)
    assert kv_heads == spans and spans & (spans - 1) == 0
    width = queries.shape[4] // spans
    groups = width // HEAD_SIZE
    bf16 = jnp.bfloat16
    params = pltpu.CompilerParams(vmem_limit_bytes=VMEM_LIMIT)

    def exchange(block, k):
        return lax.ppermute(block, "span", [(i, i ^ k) for i in range(spans)])

    order = sorted(range(1, spans), key=lambda k: -bin(k).count("1"))

    kv_pieces = pl.pallas_call(
        functools.partial(split_kv, spans),
        out_shape=[jax.ShapeDtypeStruct((2, tok_rows, HEAD_SIZE), bf16)] * spans,
        in_specs=[vmem()],
        out_specs=[vmem()] * spans,
        compiler_params=params,
        name="split_kv",
    )(key_value.reshape(tok_rows, -1))
    q_pieces = pl.pallas_call(
        functools.partial(split_q, spans),
        out_shape=[jax.ShapeDtypeStruct((tok_rows + EXTRA, width), bf16)] * spans,
        in_specs=[smem(), vmem()],
        out_specs=[vmem()] * spans,
        compiler_params=params,
        name="split_q",
    )(pattern.reshape(NEIGH), queries.reshape(tok_rows, -1))

    column = [kv_pieces[0]] + [None] * (spans - 1)
    for k in order:
        column[k] = exchange(kv_pieces[k], k)
    own = jnp.stack(column)
    q_here = [q_pieces[0]] + [None] * (spans - 1)
    for k in order:
        q_here[k] = exchange(q_pieces[k], k)

    ways, tiles = [], [own]
    for axis, count in (("tx", tx_count), ("ty", ty_count)):
        for first, pairs in enumerate(pairings(count)):
            ways.append((axis, first))
            tiles.append(swap(own, axis, pairs))

    keys = len(tiles) * tok_rows
    outs = pl.pallas_call(
        functools.partial(attend, spans, ty_count, tx_count, tuple(ways)),
        out_shape=[jax.ShapeDtypeStruct((tok_rows, width), bf16)] * spans,
        in_specs=[smem(), smem()] + [vmem()] * (spans + len(tiles)),
        out_specs=[vmem()] * spans,
        scratch_shapes=[
            pltpu.VMEM((spans, groups * tok_rows, keys), jnp.float32),
            pltpu.VMEM((groups * tok_rows, tok_rows), jnp.float32),
            pltpu.VMEM((groups * tok_rows, tok_rows), jnp.float32),
            pltpu.VMEM((groups * tok_rows, HEAD_SIZE), jnp.float32),
        ],
        compiler_params=params,
        name="attend",
    )(counts.reshape(-1), span_mask.reshape(-1), *q_here, *tiles)

    home = [outs[0]] + [None] * (spans - 1)
    for k in order:
        home[k] = exchange(outs[k], k)
    attended = pl.pallas_call(
        functools.partial(join, spans),
        out_shape=jax.ShapeDtypeStruct((tok_rows, spans * width), bf16),
        in_specs=[vmem()] * spans,
        out_specs=vmem(),
        compiler_params=params,
        name="join",
    )(*home)
    return attended.reshape(1, 1, 1, tok_rows, -1)


def solution(mesh):
    return jax.shard_map(
        shards,
        mesh=mesh,
        in_specs=(
            P("span", "ty", "tx", None, None),
            P("span", "ty", "tx", None, None),
            P("span", "ty", "tx", None),
            P(),
            P(),
        ),
        out_specs=P("span", "ty", "tx", None, None),
        check_vma=False,
    )
```

time: 172 us -> 41.8 us (0.24)
  waiting for transfers between devices: 91.3 us -> 17 us
  local copies, waits for them, and re-layouts: 34.7 us -> 1.89 us
  between operations: 13.7 us -> 0.07 us
  other arithmetic: 12.6 us -> 0.04 us
  matrix products: 8.64 us -> 0 us
  Pallas kernels: 0 us -> 7.99 us
  starting transfers between devices: 10.8 us -> 14.9 us
    ppermute x4 -> x12, waiting for transfers between devices: 59.3 us -> 17 us  [the longest x9 17 us: exchange(): return lax.ppermute(block, 'span', [(i, i ^ k) for i in range(spans)])]
    all_gather x1 -> x0, waiting for transfers between devices: 31.3 us -> none  [shards(): cached = lax.all_gather(key_value, 'span', axis=0, tiled=True)]
    reshape x8 -> x2, local copies, waits for them, and re-layouts: 15.1 us -> 0.17 us  [the longest x1 0.08 us: shards(): counts.reshape(-1)]
    dot_general x8 -> x0, matrix products: 8.64 us -> none  [the longest x4 5.44 us: shards(): jnp.einsum('tkgl,lkd->tkgd', weights.astype(jnp.bfloat16), value_rows, pr...]
    pallas_call x0 -> x4, Pallas kernels: none -> 7.99 us  [the longest x1 6.54 us: shards(): pl.pallas_call(functools.partial(attend, spans, ty_count, tx_count, tuple...]
    slice x5 -> x0, local copies, waits for them, and re-layouts: 6.06 us -> none  [the longest x4 4.96 us: shards(): key_value_block[:, :, kv_width:].reshape(-1, kv_heads, HEAD_SIZE)]
    reduce_sum x2 -> x0, other arithmetic: 5.27 us -> none  [shards(): attend_run_sum = attend_run_sum * fade_factor + jnp.sum(weights, axis=-1)]
    ppermute x4 -> x12, starting transfers between devices: 10.8 us -> 14.9 us  [the longest x9 9.68 us: exchange(): return lax.ppermute(block, 'span', [(i, i ^ k) for i in range(spans)])]
  transfers between devices with their start and end apart: 5 -> 12, of which waited for: 5 -> 8; matrix products, arithmetic and copies ran while one was open for 8% -> 0% of each run, Pallas kernels for 0% -> 1%
where the time goes in v1:
time: 41.8 us; the launch traced here: 41.9 us
  waiting for transfers between devices  17 us (41%)
  starting transfers between devices  14.9 us (36%)
  Pallas kernels  7.99 us (19%)
  local copies, waits for them, and re-layouts  1.89 us (5%)
    ppermute x9, waiting for transfers between devices, exchange(): return lax.ppermute(block, 'span', [(i, i ^ k) for i in range(spans)])  17 us
    ppermute x9, starting transfers between devices, exchange(): return lax.ppermute(block, 'span', [(i, i ^ k) for i in range(spans)])  9.68 us
    pallas_call x1, Pallas kernels, shards(): pl.pallas_call(functools.partial(attend, spans, ty_count, tx_count, tuple...  6.54 us
    ppermute x3, starting transfers between devices, swap(): return lax.ppermute(block, axis, pairs + [(b, a) for a, b in pairs])  5.2 us
    unnamed x10, local copies, waits for them, and re-layouts  1.73 us
  transfers between devices with their start and end apart: 12, of which 8 were waited for; matrix products, arithmetic and copies ran while one was open for 0% of the time, Pallas kernels for 1%

profile of v1, /device:TPU:0, one launch (start us, length us, event | category | flops | bytes accessed | tf_op | source)
XLA Modules:
  0.0 41.9 jit_solution(1331756155093008628)
XLA Ops:
  0.0 0.9 %copy-done.1 = bf16[1,1,1,128,1024]{4,3,2,1,0:T(8,128)(2,1)S(1)} copy-done((bf16[1,1,1,128,1024]{4,3,2,1,0:T(8,128)(2,1)S(1)}, bf16[1,1,1,128,1024]{4,3,2,1,0:T(8,128)(2,1)}, u32[]{:S(2)}) %copy-start.1) | copy-done | bytes 262168
  1.0 3.0 %collective-permute-start.3 = (bf16[2,128,128]{2,1,0:T(8,128)(2,1)S(1)}, bf16[2,128,128]{2,1,0:T(8,128)(2,1)S(1)}, u32[]{:S(2)}, u32[]{:S(2)}) collective-permute-start(bf16[2,128,128]{2,1,0:T(8,128)(2,1)S(1)} %get-tuple-element.22), channel_id=1, source_target_pairs={{0,8},{8,0},{16,24},{24,16},{1,9},{9,1},{17,25},{25,17},{2,10},{10... | collective-permute-start | bytes 196616 | tf_op jit(solution)/shard_map/ppermute | solution.py:172
  4.0 1.5 %collective-permute-start.4 = (bf16[2,128,128]{2,1,0:T(8,128)(2,1)S(1)}, bf16[2,128,128]{2,1,0:T(8,128)(2,1)S(1)}, u32[]{:S(2)}, u32[]{:S(2)}) collective-permute-start(bf16[2,128,128]{2,1,0:T(8,128)(2,1)S(1)} %get-tuple-element.23), channel_id=1, source_target_pairs={{0,16},{8,24},{16,0},{24,8},{1,17},{9,25},{17,1},{25,9},{2,18},{10... | collective-permute-start | bytes 196616 | tf_op jit(solution)/shard_map/ppermute | solution.py:172
  5.6 0.8 %collective-permute-done.3 = bf16[2,128,128]{2,1,0:T(8,128)(2,1)S(1)} collective-permute-done((bf16[2,128,128]{2,1,0:T(8,128)(2,1)S(1)}, bf16[2,128,128]{2,1,0:T(8,128)(2,1)S(1)}, u32[]{:S(2)}, u32[]{:S(2)}) %collective-permute-start.3) | collective-permute-done | bytes 65568 | tf_op jit(solution)/shard_map/ppermute | solution.py:172
  6.4 1.9 %collective-permute-done.4 = bf16[2,128,128]{2,1,0:T(8,128)(2,1)S(1)} collective-permute-done((bf16[2,128,128]{2,1,0:T(8,128)(2,1)S(1)}, bf16[2,128,128]{2,1,0:T(8,128)(2,1)S(1)}, u32[]{:S(2)}, u32[]{:S(2)}) %collective-permute-start.4) | collective-permute-done | bytes 65568 | tf_op jit(solution)/shard_map/ppermute | solution.py:172
  8.3 2.4 %collective-permute-done.5 = bf16[2,128,128]{2,1,0:T(8,128)(2,1)S(1)} collective-permute-done((bf16[2,128,128]{2,1,0:T(8,128)(2,1)S(1)}, bf16[2,128,128]{2,1,0:T(8,128)(2,1)S(1)}, u32[]{:S(2)}, u32[]{:S(2)}) %collective-permute-start.5) | collective-permute-done | bytes 65568 | tf_op jit(solution)/shard_map/ppermute | solution.py:172
  10.8 0.7 %collective-permute-start.7 = (bf16[4,2,128,128]{3,2,1,0:T(8,128)(2,1)S(1)}, bf16[4,2,128,128]{3,2,1,0:T(8,128)(2,1)S(1)}, u32[]{:S(2)}, u32[]{:S(2)}) collective-permute-start(bf16[4,2,128,128]{3,2,1,0:T(8,128)(2,1)S(1)} %pad_maximum_fusion.refs_6_), channel_id=1, source_target_pairs={{1,2},{2,1},{5,6},{6,5},{9,10},{10,9},{13,14},{14,13},{17,18},{18,... | collective-permute-start | bytes 786440 | tf_op jit(solution)/shard_map/ppermute | solution.py:35
  11.5 4.4 %collective-permute-start.6 = (bf16[4,2,128,128]{3,2,1,0:T(8,128)(2,1)S(1)}, bf16[4,2,128,128]{3,2,1,0:T(8,128)(2,1)S(1)}, u32[]{:S(2)}, u32[]{:S(2)}) collective-permute-start(bf16[4,2,128,128]{3,2,1,0:T(8,128)(2,1)S(1)} %pad_maximum_fusion.refs_6_), channel_id=1, source_target_pairs={{0,1},{2,3},{1,0},{3,2},{4,5},{6,7},{5,4},{7,6},{8,9},{10,11},{9,8... | collective-permute-start | bytes 786440 | tf_op jit(solution)/shard_map/ppermute | solution.py:35
  16.0 0.7 %copy-done.2 = s32[1,1,1,5]{3,2,1,0:T(1,128)S(1)} copy-done((s32[1,1,1,5]{3,2,1,0:T(1,128)S(1)}, s32[1,1,1,5]{3,2,1,0:T(1,128)}, u32[]{:S(2)}) %copy-start.2) | copy-done | bytes 44
  16.6 0.6 %split_q.1 = (bf16[144,384]{1,0:T(8,128)(2,1)S(1)}, bf16[144,384]{1,0:T(8,128)(2,1)S(1)}, bf16[144,384]{1,0:T(8,128)(2,1)S(1)}, bf16[144,384]{1,0:T(8,128)(2,1)S(1)}) custom-call(s32[5]{0:T(128)S(1)} %bitcast.11, bf16[128,1536]{1,0:T(8,128)(2,1)S(1)} %bitcast.8), custom_call_target="tpu_custom_call" | custom-call | tf_op jit(solution)/shard_map/split_q/pallas_call | solution.py:184
  17.2 0.6 %collective-permute-start = (bf16[144,384]{1,0:T(8,128)(2,1)S(1)}, bf16[144,384]{1,0:T(8,128)(2,1)S(1)}, u32[]{:S(2)}, u32[]{:S(2)}) collective-permute-start(bf16[144,384]{1,0:T(8,128)(2,1)S(1)} %get-tuple-element.18), channel_id=1, source_target_pairs={{0,8},{8,0},{16,24},{24,16},{1,9},{9,1},{17,25},{25,17},{2,10},{10... | collective-permute-start | bytes 331784 | tf_op jit(solution)/shard_map/ppermute | solution.py:172
  17.8 0.5 %collective-permute-start.1 = (bf16[144,384]{1,0:T(8,128)(2,1)S(1)}, bf16[144,384]{1,0:T(8,128)(2,1)S(1)}, u32[]{:S(2)}, u32[]{:S(2)}) collective-permute-start(bf16[144,384]{1,0:T(8,128)(2,1)S(1)} %get-tuple-element.19), channel_id=1, source_target_pairs={{0,16},{8,24},{16,0},{24,8},{1,17},{9,25},{17,1},{25,9},{2,18},{10... | collective-permute-start | bytes 331784 | tf_op jit(solution)/shard_map/ppermute | solution.py:172
  18.3 3.8 %collective-permute-done.refs_3_ = bf16[144,384]{1,0:T(8,128)(2,1)S(1)} collective-permute-done((bf16[144,384]{1,0:T(8,128)(2,1)S(1)}, bf16[144,384]{1,0:T(8,128)(2,1)S(1)}, u32[]{:S(2)}, u32[]{:S(2)}) %collective-permute-start) | collective-permute-done | bytes 110624 | tf_op jit(solution)/shard_map/ppermute | solution.py:172
  22.2 0.5 %collective-permute-start.2 = (bf16[144,384]{1,0:T(8,128)(2,1)S(1)}, bf16[144,384]{1,0:T(8,128)(2,1)S(1)}, u32[]{:S(2)}, u32[]{:S(2)}) collective-permute-start(bf16[144,384]{1,0:T(8,128)(2,1)S(1)} %get-tuple-element.20), channel_id=1, source_target_pairs={{0,24},{8,16},{16,8},{24,0},{1,25},{9,17},{17,9},{25,1},{2,26},{10... | collective-permute-start | bytes 331784 | tf_op jit(solution)/shard_map/ppermute | solution.py:172
  22.8 0.1 copy-done.4
  23.0 4.9 %collective-permute-done.2.refs_5_ = bf16[144,384]{1,0:T(8,128)(2,1)S(1)} collective-permute-done((bf16[144,384]{1,0:T(8,128)(2,1)S(1)}, bf16[144,384]{1,0:T(8,128)(2,1)S(1)}, u32[]{:S(2)}, u32[]{:S(2)}) %collective-permute-start.2) | collective-permute-done | bytes 110624 | tf_op jit(solution)/shard_map/ppermute | solution.py:172
  27.8 6.5 %attend.1 = (bf16[128,384]{1,0:T(8,128)(2,1)S(1)}, bf16[128,384]{1,0:T(8,128)(2,1)S(1)}, bf16[128,384]{1,0:T(8,128)(2,1)S(1)}, bf16[128,384]{1,0:T(8,128)(2,1)S(1)}) custom-call(s32[32]{0:T(128)S(1)} %reshape.18.refs_0_, s32[16]{0:T(128)S(1)} %reshape.19.refs_1_, bf16[144,384]{1,0:T(8,128)(2,1)S(1)} %get-tuple-element.17.refs_2_, ...), custom_call_target="tpu_custom_call" | custom-call | tf_op jit(solution)/shard_map/attend/pallas_call | solution.py:208
  34.4 0.6 %collective-permute-start.9 = (bf16[128,384]{1,0:T(8,128)(2,1)S(1)}, bf16[128,384]{1,0:T(8,128)(2,1)S(1)}, u32[]{:S(2)}, u32[]{:S(2)}) collective-permute-start(bf16[128,384]{1,0:T(8,128)(2,1)S(1)} %get-tuple-element.26), channel_id=1, source_target_pairs={{0,8},{8,0},{16,24},{24,16},{1,9},{9,1},{17,25},{25,17},{2,10},{10... | collective-permute-start | bytes 294920 | tf_op jit(solution)/shard_map/ppermute | solution.py:172
  35.0 0.5 %collective-permute-start.10 = (bf16[128,384]{1,0:T(8,128)(2,1)S(1)}, bf16[128,384]{1,0:T(8,128)(2,1)S(1)}, u32[]{:S(2)}, u32[]{:S(2)}) collective-permute-start(bf16[128,384]{1,0:T(8,128)(2,1)S(1)} %get-tuple-element.27), channel_id=1, source_target_pairs={{0,16},{8,24},{16,0},{24,8},{1,17},{9,25},{17,1},{25,9},{2,18},{10... | collective-permute-start | bytes 294920 | tf_op jit(solution)/shard_map/ppermute | solution.py:172
  35.5 2.4 %collective-permute-start.11 = (bf16[128,384]{1,0:T(8,128)(2,1)S(1)}, bf16[128,384]{1,0:T(8,128)(2,1)S(1)}, u32[]{:S(2)}, u32[]{:S(2)}) collective-permute-start(bf16[128,384]{1,0:T(8,128)(2,1)S(1)} %get-tuple-element.28), channel_id=1, source_target_pairs={{0,24},{8,16},{16,8},{24,0},{1,25},{9,17},{17,9},{25,1},{2,26},{10... | collective-permute-start | bytes 294920 | tf_op jit(solution)/shard_map/ppermute | solution.py:172
  37.9 1.1 %collective-permute-done.9.refs_1_ = bf16[128,384]{1,0:T(8,128)(2,1)S(1)} collective-permute-done((bf16[128,384]{1,0:T(8,128)(2,1)S(1)}, bf16[128,384]{1,0:T(8,128)(2,1)S(1)}, u32[]{:S(2)}, u32[]{:S(2)}) %collective-permute-start.9) | collective-permute-done | bytes 98336 | tf_op jit(solution)/shard_map/ppermute | solution.py:172
  39.1 0.6 %collective-permute-done.10.refs_2_ = bf16[128,384]{1,0:T(8,128)(2,1)S(1)} collective-permute-done((bf16[128,384]{1,0:T(8,128)(2,1)S(1)}, bf16[128,384]{1,0:T(8,128)(2,1)S(1)}, u32[]{:S(2)}, u32[]{:S(2)}) %collective-permute-start.10) | collective-permute-done | bytes 98336 | tf_op jit(solution)/shard_map/ppermute | solution.py:172
  39.6 1.4 %collective-permute-done.11.refs_3_ = bf16[128,384]{1,0:T(8,128)(2,1)S(1)} collective-permute-done((bf16[128,384]{1,0:T(8,128)(2,1)S(1)}, bf16[128,384]{1,0:T(8,128)(2,1)S(1)}, u32[]{:S(2)}, u32[]{:S(2)}) %collective-permute-start.11) | collective-permute-done | bytes 98336 | tf_op jit(solution)/shard_map/ppermute | solution.py:172
  41.1 0.8 %join.1 = bf16[128,1536]{1,0:T(8,128)(2,1)} custom-call(bf16[128,384]{1,0:T(8,128)(2,1)S(1)} %get-tuple-element.25.refs_0_, bf16[128,384]{1,0:T(8,128)(2,1)S(1)} %collective-permute-done.9.refs_1_, bf16[128,384]{1,0:T(8,128)(2,1)S(1)} %collective-permute-done.10.refs_2_, bf16[128,384]{1,0:T(8,128)(2,1)S(1)} %collective-permute-done.11.refs_3_), custom_call_target="tpu_custom_call" | custom-call | tf_op jit(solution)/shard_map/join/pallas_call | solution.py:226
  (17 shorter events, 0.4 us)
Async XLA Ops:
  0.0 0.9 %copy-start.1 = (bf16[1,1,1,128,1024]{4,3,2,1,0:T(8,128)(2,1)S(1)}, bf16[1,1,1,128,1024]{4,3,2,1,0:T(8,128)(2,1)}, u32[]{:S(2)}) copy-start(bf16[1,1,1,128,1024]{4,3,2,1,0:T(8,128)(2,1)} %param.6) | copy-start | bytes 786436
  1.0 15.0 %copy-start = (bf16[1,1,1,128,1536]{4,3,2,1,0:T(8,128)(2,1)S(1)}, bf16[1,1,1,128,1536]{4,3,2,1,0:T(8,128)(2,1)}, u32[]{:S(2)}) copy-start(bf16[1,1,1,128,1536]{4,3,2,1,0:T(8,128)(2,1)} %param.5) | copy-start | bytes 1179652
  1.0 5.4 %collective-permute-start.3 = (bf16[2,128,128]{2,1,0:T(8,128)(2,1)S(1)}, bf16[2,128,128]{2,1,0:T(8,128)(2,1)S(1)}, u32[]{:S(2)}, u32[]{:S(2)}) collective-permute-start(bf16[2,128,128]{2,1,0:T(8,128)(2,1)S(1)} %get-tuple-element.22), channel_id=1, source_target_pairs={{0,8},{8,0},{16,24},{24,16},{1,9},{9,1},{17,25},{25,17},{2,10},{10... | collective-permute-start | bytes 196616 | tf_op jit(solution)/shard_map/ppermute | solution.py:172
  4.0 4.3 %collective-permute-start.4 = (bf16[2,128,128]{2,1,0:T(8,128)(2,1)S(1)}, bf16[2,128,128]{2,1,0:T(8,128)(2,1)S(1)}, u32[]{:S(2)}, u32[]{:S(2)}) collective-permute-start(bf16[2,128,128]{2,1,0:T(8,128)(2,1)S(1)} %get-tuple-element.23), channel_id=1, source_target_pairs={{0,16},{8,24},{16,0},{24,8},{1,17},{9,25},{17,1},{25,9},{2,18},{10... | collective-permute-start | bytes 196616 | tf_op jit(solution)/shard_map/ppermute | solution.py:172
  5.5 5.2 %collective-permute-start.5 = (bf16[2,128,128]{2,1,0:T(8,128)(2,1)S(1)}, bf16[2,128,128]{2,1,0:T(8,128)(2,1)S(1)}, u32[]{:S(2)}, u32[]{:S(2)}) collective-permute-start(bf16[2,128,128]{2,1,0:T(8,128)(2,1)S(1)} %get-tuple-element.24), channel_id=1, source_target_pairs={{0,24},{8,16},{16,8},{24,0},{1,25},{9,17},{17,9},{25,1},{2,26},{10... | collective-permute-start | bytes 196616 | tf_op jit(solution)/shard_map/ppermute | solution.py:172
  10.8 17.1 %collective-permute-start.8 = (bf16[4,2,128,128]{3,2,1,0:T(8,128)(2,1)S(1)}, bf16[4,2,128,128]{3,2,1,0:T(8,128)(2,1)S(1)}, u32[]{:S(2)}, u32[]{:S(2)}) collective-permute-start(bf16[4,2,128,128]{3,2,1,0:T(8,128)(2,1)S(1)} %pad_maximum_fusion.refs_6_), channel_id=1, source_target_pairs={{0,4},{4,0},{1,5},{5,1},{2,6},{6,2},{3,7},{7,3},{8,12},{12,8},{9,1... | collective-permute-start | bytes 786440 | tf_op jit(solution)/shard_map/ppermute | solution.py:35
  10.8 17.0 %collective-permute-start.7 = (bf16[4,2,128,128]{3,2,1,0:T(8,128)(2,1)S(1)}, bf16[4,2,128,128]{3,2,1,0:T(8,128)(2,1)S(1)}, u32[]{:S(2)}, u32[]{:S(2)}) collective-permute-start(bf16[4,2,128,128]{3,2,1,0:T(8,128)(2,1)S(1)} %pad_maximum_fusion.refs_6_), channel_id=1, source_target_pairs={{1,2},{2,1},{5,6},{6,5},{9,10},{10,9},{13,14},{14,13},{17,18},{18,... | collective-permute-start | bytes 786440 | tf_op jit(solution)/shard_map/ppermute | solution.py:35
  11.5 16.3 %collective-permute-start.6 = (bf16[4,2,128,128]{3,2,1,0:T(8,128)(2,1)S(1)}, bf16[4,2,128,128]{3,2,1,0:T(8,128)(2,1)S(1)}, u32[]{:S(2)}, u32[]{:S(2)}) collective-permute-start(bf16[4,2,128,128]{3,2,1,0:T(8,128)(2,1)S(1)} %pad_maximum_fusion.refs_6_), channel_id=1, source_target_pairs={{0,1},{2,3},{1,0},{3,2},{4,5},{6,7},{5,4},{7,6},{8,9},{10,11},{9,8... | collective-permute-start | bytes 786440 | tf_op jit(solution)/shard_map/ppermute | solution.py:35
  16.0 0.7 %copy-start.2 = (s32[1,1,1,5]{3,2,1,0:T(1,128)S(1)}, s32[1,1,1,5]{3,2,1,0:T(1,128)}, u32[]{:S(2)}) copy-start(s32[1,1,1,5]{3,2,1,0:T(1,128)} %param.7) | copy-start | bytes 64
  17.2 5.4 %copy-start.3 = (s32[4,2,4]{2,1,0:T(2,128)S(1)}, s32[4,2,4]{2,1,0:T(2,128)}, u32[]{:S(2)}) copy-start(s32[4,2,4]{2,1,0:T(2,128)} %param.8) | copy-start | bytes 388
  17.2 5.0 %collective-permute-start = (bf16[144,384]{1,0:T(8,128)(2,1)S(1)}, bf16[144,384]{1,0:T(8,128)(2,1)S(1)}, u32[]{:S(2)}, u32[]{:S(2)}) collective-permute-start(bf16[144,384]{1,0:T(8,128)(2,1)S(1)} %get-tuple-element.18), channel_id=1, source_target_pairs={{0,8},{8,0},{16,24},{24,16},{1,9},{9,1},{17,25},{25,17},{2,10},{10... | collective-permute-start | bytes 331784 | tf_op jit(solution)/shard_map/ppermute | solution.py:172
  17.8 5.1 %collective-permute-start.1 = (bf16[144,384]{1,0:T(8,128)(2,1)S(1)}, bf16[144,384]{1,0:T(8,128)(2,1)S(1)}, u32[]{:S(2)}, u32[]{:S(2)}) collective-permute-start(bf16[144,384]{1,0:T(8,128)(2,1)S(1)} %get-tuple-element.19), channel_id=1, source_target_pairs={{0,16},{8,24},{16,0},{24,8},{1,17},{9,25},{17,1},{25,9},{2,18},{10... | collective-permute-start | bytes 331784 | tf_op jit(solution)/shard_map/ppermute | solution.py:172
  22.2 0.7 %copy-start.4 = (s32[4,4]{1,0:T(4,128)S(1)}, s32[4,4]{1,0:T(4,128)}, u32[]{:S(2)}) copy-start(s32[4,4]{1,0:T(4,128)} %param.9) | copy-start | bytes 196
  22.2 5.6 %collective-permute-start.2 = (bf16[144,384]{1,0:T(8,128)(2,1)S(1)}, bf16[144,384]{1,0:T(8,128)(2,1)S(1)}, u32[]{:S(2)}, u32[]{:S(2)}) collective-permute-start(bf16[144,384]{1,0:T(8,128)(2,1)S(1)} %get-tuple-element.20), channel_id=1, source_target_pairs={{0,24},{8,16},{16,8},{24,0},{1,25},{9,17},{17,9},{25,1},{2,26},{10... | collective-permute-start | bytes 331784 | tf_op jit(solution)/shard_map/ppermute | solution.py:172
  34.4 4.7 %collective-permute-start.9 = (bf16[128,384]{1,0:T(8,128)(2,1)S(1)}, bf16[128,384]{1,0:T(8,128)(2,1)S(1)}, u32[]{:S(2)}, u32[]{:S(2)}) collective-permute-start(bf16[128,384]{1,0:T(8,128)(2,1)S(1)} %get-tuple-element.26), channel_id=1, source_target_pairs={{0,8},{8,0},{16,24},{24,16},{1,9},{9,1},{17,25},{25,17},{2,10},{10... | collective-permute-start | bytes 294920 | tf_op jit(solution)/shard_map/ppermute | solution.py:172
  35.0 4.6 %collective-permute-start.10 = (bf16[128,384]{1,0:T(8,128)(2,1)S(1)}, bf16[128,384]{1,0:T(8,128)(2,1)S(1)}, u32[]{:S(2)}, u32[]{:S(2)}) collective-permute-start(bf16[128,384]{1,0:T(8,128)(2,1)S(1)} %get-tuple-element.27), channel_id=1, source_target_pairs={{0,16},{8,24},{16,0},{24,8},{1,17},{9,25},{17,1},{25,9},{2,18},{10... | collective-permute-start | bytes 294920 | tf_op jit(solution)/shard_map/ppermute | solution.py:172
  35.5 5.5 %collective-permute-start.11 = (bf16[128,384]{1,0:T(8,128)(2,1)S(1)}, bf16[128,384]{1,0:T(8,128)(2,1)S(1)}, u32[]{:S(2)}, u32[]{:S(2)}) collective-permute-start(bf16[128,384]{1,0:T(8,128)(2,1)S(1)} %get-tuple-element.28), channel_id=1, source_target_pairs={{0,24},{8,16},{16,8},{24,0},{1,25},{9,17},{17,9},{25,1},{2,26},{10... | collective-permute-start | bytes 294920 | tf_op jit(solution)/shard_map/ppermute | solution.py:172

commit v2 on v1

v2 whole, which is shorter than its diff:
```python
import functools
import math

import jax
import jax.numpy as jnp
from jax import lax
from jax.experimental import pallas as pl
from jax.experimental.pallas import tpu as pltpu
from jax.sharding import PartitionSpec as P

HEAD_SIZE = 128
NEIGH = 5
EXTRA = 16
CHUNK = 64
NEAR_FLOPS = 1_000_000_000
DEAD = -1e30
VMEM_LIMIT = 40 * 1024 * 1024


def vmem():
    return pl.BlockSpec(memory_space=pltpu.VMEM)


def smem():
    return pl.BlockSpec(memory_space=pltpu.SMEM)


def pairings(count):
    found = []
    for first in (0, 1):
        pairs = [(i, i + 1) for i in range(first, count - 1, 2)]
        if pairs:
            found.append(pairs)
    return found


def swap(block, axis, pairs):
    return lax.ppermute(block, axis, pairs + [(b, a) for a, b in pairs])


def partner(place, count, first):
    low = lax.rem(place + first, 2) == 0
    step = jnp.where(low, 1, -1)
    other = place + step
    return jnp.where((other >= 0) & (other < count), step, 0)


def split(spans, pattern_hbm, kv_hbm, q_hbm, *refs):
    kv_refs, q_refs = refs[:spans], refs[spans : 2 * spans]
    pattern_ref, kv_sem, q_sem, pattern_sem = refs[2 * spans :]
    me = lax.axis_index("span")
    kv_width = kv_hbm.shape[1] // 2
    rows = q_hbm.shape[0]
    width = q_hbm.shape[1] // spans
    copies = [pltpu.make_async_copy(pattern_hbm, pattern_ref, pattern_sem)]
    for k in range(spans):
        head = me ^ k
        for part in range(2):
            start = pl.multiple_of(part * kv_width + head * HEAD_SIZE, HEAD_SIZE)
            copies.append(
                pltpu.make_async_copy(
                    kv_hbm.at[:, pl.ds(start, HEAD_SIZE)], kv_refs[k].at[part], kv_sem.at[k, part]
                )
            )
    for k in range(spans):
        start = pl.multiple_of((me ^ k) * width, HEAD_SIZE)
        copies.append(
            pltpu.make_async_copy(
                q_hbm.at[:, pl.ds(start, width)], q_refs[k].at[pl.ds(0, rows)], q_sem.at[k]
            )
        )
    for copy in copies:
        copy.start()
    copies[0].wait()
    row_ids = lax.broadcasted_iota(jnp.int32, (EXTRA, width), 0)
    extra = jnp.zeros((EXTRA, width), jnp.float32)
    for o in range(NEIGH):
        extra = jnp.where(row_ids == o, pattern_ref[o].astype(jnp.float32), extra)
    extra = extra.astype(jnp.bfloat16)
    for k in range(spans):
        q_refs[k][rows:] = extra
    for copy in copies[1:]:
        copy.wait()


class Place:
    def __init__(self, spans, sizes, ways, counts_ref, mask_ref):
        self.spans, self.sizes, self.ways = spans, sizes, ways
        self.counts_ref, self.mask_ref = counts_ref, mask_ref
        self.me = lax.axis_index("span")
        self.at = [lax.axis_index(axis) for axis in ("ty", "tx")]

    def count(self, span, step_row=0, step_col=0):
        row, col = self.at[0] + step_row, self.at[1] + step_col
        return self.counts_ref[(span * self.sizes[0] + row) * self.sizes[1] + col]

    def bias(self, q_ref, span):
        slots = q_ref.shape[1] - EXTRA
        lanes = lax.broadcasted_iota(jnp.int32, (1, slots), 1)
        extra = q_ref[self.me ^ span, slots:, :HEAD_SIZE].astype(jnp.float32)
        parts = []
        for other in range(span + 1):
            opened = self.mask_ref[span * self.spans + other]
            for way in self.ways:
                if way is None:
                    chosen, near = extra[0:1], self.count(other)
                else:
                    dim, first = way
                    step = partner(self.at[dim], self.sizes[dim], first)
                    base = 1 + 2 * dim
                    chosen = jnp.where(step > 0, extra[base + 1 : base + 2], extra[base : base + 1])
                    near = self.count(other, *((step, 0) if dim == 0 else (0, step)))
                    near = jnp.where(step == 0, 0, near)
                near = jnp.where(opened > 0, near, 0)
                parts.append(jnp.where((lanes < near) & (chosen > 0), 0.0, DEAD))
        return jnp.concatenate(parts, axis=1)


def scores_of(q_ref, k, tile_refs, others, score_ref):
    tok_rows = q_ref.shape[1] - EXTRA
    groups = q_ref.shape[2] // HEAD_SIZE
    query = jnp.concatenate(
        [q_ref[k, :tok_rows, g * HEAD_SIZE : (g + 1) * HEAD_SIZE] for g in range(groups)], axis=0
    )
    keys = jnp.concatenate([t[other, 0] for other in others for t in tile_refs], axis=0)
    score_ref[:, : keys.shape[0]] = lax.dot_general(
        query, keys, (((1,), (1,)), ((), ())), preferred_element_type=jnp.float32
    )


def weigh(rows, bias, score_ref, weight_ref, before):
    blocks = range(bias.shape[1] // HEAD_SIZE)
    factor = HEAD_SIZE ** (-0.5) * math.log2(math.e)

    def block(b):
        lanes = slice(b * HEAD_SIZE, (b + 1) * HEAD_SIZE)
        return score_ref[rows, lanes] + bias[:, lanes]

    top = before
    for b in blocks:
        top = jnp.maximum(top, block(b))
    top = jnp.broadcast_to(jnp.max(top, axis=1, keepdims=True), top.shape)
    total = jnp.zeros(top.shape, jnp.float32)
    for b in blocks:
        weights = jnp.exp2((block(b) - top) * factor)
        total = total + weights
        weight_ref[rows, b * HEAD_SIZE : (b + 1) * HEAD_SIZE] = weights.astype(jnp.bfloat16)
    return top, total


def weighted(tile_refs, others, weight_ref):
    values = jnp.concatenate([t[other, 1] for other in others for t in tile_refs], axis=0)
    return jnp.dot(
        weight_ref[:, : values.shape[0]], values, preferred_element_type=jnp.float32
    )


def chunks(total):
    return [slice(start, start + CHUNK) for start in range(0, total, CHUNK)]


def attend_near(spans, sizes, ways, *refs):
    counts_ref, mask_ref, q_ref = refs[:3]
    tile_refs = refs[3 : 3 + len(ways)]
    top_ref, sum_ref, acc_ref, score_ref, weight_ref = refs[3 + len(ways) :]
    place = Place(spans, sizes, ways, counts_ref, mask_ref)
    for span in range(spans):
        others = [place.me ^ other for other in range(span + 1)]
        scores_of(q_ref, place.me ^ span, tile_refs, others, score_ref.at[span])
        bias = place.bias(q_ref, span)
        for rows in chunks(score_ref.shape[1]):
            before = jnp.full((CHUNK, HEAD_SIZE), DEAD, jnp.float32)
            top, total = weigh(rows, bias, score_ref.at[span], weight_ref.at[span], before)
            top_ref[span, rows] = top
            sum_ref[span, rows] = total
        acc_ref[span] = weighted(tile_refs, others, weight_ref.at[span])


def attend_far(spans, sizes, ways, k, *refs):
    counts_ref, mask_ref, q_ref = refs[:3]
    tile_refs = refs[3 : 3 + len(ways)]
    top_in, sum_in, acc_in, out_ref, score_ref, weight_ref, fade_ref, sum_ref = refs[3 + len(ways) :]
    place = Place(spans, sizes, ways, counts_ref, mask_ref)
    tok_rows = out_ref.shape[0]
    factor = HEAD_SIZE ** (-0.5) * math.log2(math.e)

    def finish(span, product):
        valid = place.count(span)
        for rows in chunks(acc_in.shape[1]):
            result = (acc_in[span, rows] * fade_ref[rows] + product[rows]) * sum_ref[rows]
            group, first = rows.start // tok_rows, rows.start % tok_rows
            ids = first + lax.broadcasted_iota(jnp.int32, (CHUNK, HEAD_SIZE), 0)
            out_ref[first : first + CHUNK, group * HEAD_SIZE : (group + 1) * HEAD_SIZE] = jnp.where(
                ids < valid, result, 0.0
            ).astype(jnp.bfloat16)

    for span in range(spans):

        @pl.when(place.me ^ k == span)
        def _(span=span):
            others = [place.me ^ other for other in range(span + 1)]
            scores_of(q_ref, k, tile_refs, others, score_ref)
            bias = place.bias(q_ref, span)
            for rows in chunks(score_ref.shape[0]):
                before = top_in[span, rows]
                top, total = weigh(rows, bias, score_ref, weight_ref, before)
                fade = jnp.exp2((before - top) * factor)
                total = jnp.sum(total + sum_in[span, rows] * fade, axis=1, keepdims=True)
                fade_ref[rows] = fade
                sum_ref[rows] = jnp.where(top > 0.5 * DEAD, 1.0 / total, jnp.nan)
            finish(span, weighted(tile_refs, others, weight_ref))


def join(spans, *refs):
    me = lax.axis_index("span")
    out_ref = refs[spans]
    width = refs[0].shape[1]
    for k in range(spans):
        start = pl.multiple_of((me ^ k) * width, HEAD_SIZE)
        out_ref[:, pl.ds(start, width)] = refs[k][...]


def shards(queries, key_value, pattern, counts, span_mask):
    spans, ty_count, tx_count = (lax.axis_size(a) for a in ("span", "ty", "tx"))
    tok_rows = queries.shape[3]
    kv_heads = key_value.shape[4] // (2 * HEAD_SIZE)
    assert kv_heads == spans and spans & (spans - 1) == 0
    width = queries.shape[4] // spans
    groups = width // HEAD_SIZE
    bf16 = jnp.bfloat16
    params = pltpu.CompilerParams(vmem_limit_bytes=VMEM_LIMIT)

    def exchange(block, k):
        return lax.ppermute(block, "span", [(i, i ^ k) for i in range(spans)])

    order = sorted(range(1, spans), key=lambda k: -bin(k).count("1"))

    pieces = pl.pallas_call(
        functools.partial(split, spans),
        out_shape=[jax.ShapeDtypeStruct((2, tok_rows, HEAD_SIZE), bf16)] * spans
        + [jax.ShapeDtypeStruct((tok_rows + EXTRA, width), bf16)] * spans,
        in_specs=[pl.BlockSpec(memory_space=pltpu.HBM)] * 3,
        out_specs=[vmem()] * (2 * spans),
        scratch_shapes=[
            pltpu.SMEM((NEIGH,), jnp.int32),
            pltpu.SemaphoreType.DMA((spans, 2)),
            pltpu.SemaphoreType.DMA((spans,)),
            pltpu.SemaphoreType.DMA,
        ],
        compiler_params=params,
        name="split",
    )(
        *(
            pltpu.with_memory_space_constraint(x, pltpu.HBM)
            for x in (
                pattern.reshape(NEIGH),
                key_value.reshape(tok_rows, -1),
                queries.reshape(tok_rows, -1),
            )
        )
    )
    kv_pieces, q_pieces = pieces[:spans], pieces[spans:]

    column = [kv_pieces[0]] + [None] * (spans - 1)
    for k in order:
        column[k] = exchange(kv_pieces[k], k)
    own = jnp.stack(column)
    q_here = [q_pieces[0]] + [None] * (spans - 1)
    for k in order:
        q_here[k] = exchange(q_pieces[k], k)

    near_ways, near, far_ways, far = [None], [own], [], []
    for first, pairs in enumerate(pairings(tx_count)):
        far_ways.append((1, first))
        far.append(swap(own, "tx", pairs))
    for first, pairs in enumerate(pairings(ty_count)):
        (near_ways if first == 0 else far_ways).append((0, first))
        (near if first == 0 else far).append(swap(own, "ty", pairs))

    sizes = (ty_count, tx_count)
    rows = groups * tok_rows
    q_all = jnp.stack(q_here)
    scalars = (counts.reshape(-1), span_mask.reshape(-1))
    states = pl.pallas_call(
        functools.partial(attend_near, spans, sizes, tuple(near_ways)),
        out_shape=[jax.ShapeDtypeStruct((spans, rows, HEAD_SIZE), jnp.float32)] * 3,
        in_specs=[smem(), smem()] + [vmem()] * (1 + len(near)),
        out_specs=[vmem()] * 3,
        scratch_shapes=[
            pltpu.VMEM((spans, rows, spans * len(near) * tok_rows), jnp.float32),
            pltpu.VMEM((spans, rows, spans * len(near) * tok_rows), bf16),
        ],
        compiler_params=params,
        cost_estimate=pl.CostEstimate(flops=NEAR_FLOPS, bytes_accessed=4_000_000, transcendentals=0),
        name="attend_near",
    )(*scalars, q_all, *near)
    outs = [None] * spans
    for k in order + [0]:
        outs[k] = pl.pallas_call(
            functools.partial(attend_far, spans, sizes, tuple(far_ways), k),
            out_shape=jax.ShapeDtypeStruct((tok_rows, width), bf16),
            in_specs=[smem(), smem()] + [vmem()] * (4 + len(far)),
            out_specs=vmem(),
            scratch_shapes=[
                pltpu.VMEM((rows, spans * len(far) * tok_rows), jnp.float32),
                pltpu.VMEM((rows, spans * len(far) * tok_rows), bf16),
                pltpu.VMEM((rows, HEAD_SIZE), jnp.float32),
                pltpu.VMEM((rows, HEAD_SIZE), jnp.float32),
            ],
            compiler_params=params,
            name=f"attend_far_{k}",
        )(*scalars, q_all, *far, *states)

    home = [outs[0]] + [None] * (spans - 1)
    for k in order:
        home[k] = exchange(outs[k], k)
    attended = pl.pallas_call(
        functools.partial(join, spans),
        out_shape=jax.ShapeDtypeStruct((tok_rows, spans * width), bf16),
        in_specs=[vmem()] * spans,
        out_specs=vmem(),
        compiler_params=params,
        name="join",
    )(*home)
    return attended.reshape(1, 1, 1, tok_rows, -1)


def solution(mesh):
    return jax.shard_map(
        shards,
        mesh=mesh,
        in_specs=(
            P("span", "ty", "tx", None, None),
            P("span", "ty", "tx", None, None),
            P("span", "ty", "tx", None),
            P(),
            P(),
        ),
        out_specs=P("span", "ty", "tx", None, None),
        check_vma=False,
    )
```

time: 41.8 us -> 34.7 us (0.83)
  the two profiles are of different devices: /device:TPU:0 before, /device:TPU:16 now
where the time goes in v2:
time: 34.7 us; the launch traced here: 34.6 us
  starting transfers between devices  14.7 us (42%)
  Pallas kernels  10.4 us (30%)
  waiting for transfers between devices  9.04 us (26%)
    ppermute x9, starting transfers between devices, exchange(): return lax.ppermute(block, 'span', [(i, i ^ k) for i in range(spans)])  11.2 us
    ppermute x9, waiting for transfers between devices, exchange(): return lax.ppermute(block, 'span', [(i, i ^ k) for i in range(spans)])  5.88 us
    pallas_call x4, Pallas kernels, shards(): pl.pallas_call(functools.partial(attend_far, spans, sizes, tuple(far_ways...  5.26 us
    ppermute x3, starting transfers between devices, swap(): return lax.ppermute(block, axis, pairs + [(b, a) for a, b in pairs])  3.56 us
    ppermute x3, waiting for transfers between devices, swap(): return lax.ppermute(block, axis, pairs + [(b, a) for a, b in pairs])  3.16 us
    pallas_call x1, Pallas kernels, shards(): pl.pallas_call(functools.partial(attend_near, spans, sizes, tuple(near_wa...  3.03 us
    pallas_call x1, Pallas kernels, shards(): pl.pallas_call(functools.partial(split, spans), out_shape=[jax.ShapeDtype...  1.29 us
    pallas_call x1, Pallas kernels, shards(): pl.pallas_call(functools.partial(join, spans), out_shape=jax.ShapeDtypeSt...  0.8 us
  transfers between devices with their start and end apart: 12, of which 5 were waited for; matrix products, arithmetic and copies ran while one was open for 1% of the time, Pallas kernels for 19%

profile of v2, /device:TPU:16, one launch (start us, length us, event | category | flops | bytes accessed | tf_op | source)
XLA Modules:
  0.0 34.6 jit_solution(6453486876081806912)
XLA Ops:
  0.0 1.3 %split.1 = (bf16[2,128,128]{2,1,0:T(8,128)(2,1)S(1)}, bf16[2,128,128]{2,1,0:T(8,128)(2,1)S(1)}, bf16[2,128,128]{2,1,0:T(8,128)(2,1)S(1)}, bf16[2,128,128]{2,1,0:...) custom-call(s32[5]{0:T(128)} %bitcast.22, ...), custom_call_target="tpu_custom_call" | custom-call | tf_op jit(solution)/shard_map/split/pallas_call | solution.py:238
  1.3 2.5 %collective-permute-start.5 = (bf16[2,128,128]{2,1,0:T(8,128)(2,1)S(1)}, bf16[2,128,128]{2,1,0:T(8,128)(2,1)S(1)}, u32[]{:S(2)}, u32[]{:S(2)}) collective-permute-start(bf16[2,128,128]{2,1,0:T(8,128)(2,1)S(1)} %get-tuple-element.23), channel_id=1, source_target_pairs={{0,24},{8,16},{16,8},{24,0},{1,25},{9,17},{17,9},{25,1},{2,26},{10... | collective-permute-start | bytes 196616 | tf_op jit(solution)/shard_map/ppermute | solution.py:234
  3.8 0.5 %collective-permute-start.3 = (bf16[2,128,128]{2,1,0:T(8,128)(2,1)S(1)}, bf16[2,128,128]{2,1,0:T(8,128)(2,1)S(1)}, u32[]{:S(2)}, u32[]{:S(2)}) collective-permute-start(bf16[2,128,128]{2,1,0:T(8,128)(2,1)S(1)} %get-tuple-element.21), channel_id=1, source_target_pairs={{0,8},{8,0},{16,24},{24,16},{1,9},{9,1},{17,25},{25,17},{2,10},{10... | collective-permute-start | bytes 196616 | tf_op jit(solution)/shard_map/ppermute | solution.py:234
  4.4 0.5 %collective-permute-start.4 = (bf16[2,128,128]{2,1,0:T(8,128)(2,1)S(1)}, bf16[2,128,128]{2,1,0:T(8,128)(2,1)S(1)}, u32[]{:S(2)}, u32[]{:S(2)}) collective-permute-start(bf16[2,128,128]{2,1,0:T(8,128)(2,1)S(1)} %get-tuple-element.22), channel_id=1, source_target_pairs={{0,16},{8,24},{16,0},{24,8},{1,17},{9,25},{17,1},{25,9},{2,18},{10... | collective-permute-start | bytes 196616 | tf_op jit(solution)/shard_map/ppermute | solution.py:234
  4.9 1.5 %collective-permute-start = (bf16[144,384]{1,0:T(8,128)(2,1)S(1)}, bf16[144,384]{1,0:T(8,128)(2,1)S(1)}, u32[]{:S(2)}, u32[]{:S(2)}) collective-permute-start(bf16[144,384]{1,0:T(8,128)(2,1)S(1)} %get-tuple-element.17), channel_id=1, source_target_pairs={{0,8},{8,0},{16,24},{24,16},{1,9},{9,1},{17,25},{25,17},{2,10},{10... | collective-permute-start | bytes 331784 | tf_op jit(solution)/shard_map/ppermute | solution.py:234
  6.3 0.8 %collective-permute-done.5 = bf16[2,128,128]{2,1,0:T(8,128)(2,1)S(1)} collective-permute-done((bf16[2,128,128]{2,1,0:T(8,128)(2,1)S(1)}, bf16[2,128,128]{2,1,0:T(8,128)(2,1)S(1)}, u32[]{:S(2)}, u32[]{:S(2)}) %collective-permute-start.5) | collective-permute-done | bytes 65568 | tf_op jit(solution)/shard_map/ppermute | solution.py:234
  7.2 1.7 %collective-permute-done.3 = bf16[2,128,128]{2,1,0:T(8,128)(2,1)S(1)} collective-permute-done((bf16[2,128,128]{2,1,0:T(8,128)(2,1)S(1)}, bf16[2,128,128]{2,1,0:T(8,128)(2,1)S(1)}, u32[]{:S(2)}, u32[]{:S(2)}) %collective-permute-start.3) | collective-permute-done | bytes 65568 | tf_op jit(solution)/shard_map/ppermute | solution.py:234
  9.0 0.5 %collective-permute-start.1 = (bf16[144,384]{1,0:T(8,128)(2,1)S(1)}, bf16[144,384]{1,0:T(8,128)(2,1)S(1)}, u32[]{:S(2)}, u32[]{:S(2)}) collective-permute-start(bf16[144,384]{1,0:T(8,128)(2,1)S(1)} %get-tuple-element.18), channel_id=1, source_target_pairs={{0,16},{8,24},{16,0},{24,8},{1,17},{9,25},{17,1},{25,9},{2,18},{10... | collective-permute-start | bytes 331784 | tf_op jit(solution)/shard_map/ppermute | solution.py:234
  9.4 2.4 %collective-permute-start.2 = (bf16[144,384]{1,0:T(8,128)(2,1)S(1)}, bf16[144,384]{1,0:T(8,128)(2,1)S(1)}, u32[]{:S(2)}, u32[]{:S(2)}) collective-permute-start(bf16[144,384]{1,0:T(8,128)(2,1)S(1)} %get-tuple-element.19), channel_id=1, source_target_pairs={{0,24},{8,16},{16,8},{24,0},{1,25},{9,17},{17,9},{25,1},{2,26},{10... | collective-permute-start | bytes 331784 | tf_op jit(solution)/shard_map/ppermute | solution.py:234
  11.8 1.6 %collective-permute-start.6 = (bf16[4,2,128,128]{3,2,1,0:T(8,128)(2,1)S(1)}, bf16[4,2,128,128]{3,2,1,0:T(8,128)(2,1)S(1)}, u32[]{:S(2)}, u32[]{:S(2)}) collective-permute-start(bf16[4,2,128,128]{3,2,1,0:T(8,128)(2,1)S(1)} %pad_maximum_fusion.1.refs_3_), channel_id=1, source_target_pairs={{0,1},{2,3},{1,0},{3,2},{4,5},{6,7},{5,4},{7,6},{8,9},{10,11},{9,8... | collective-permute-start | bytes 786440 | tf_op jit(solution)/shard_map/ppermute | solution.py:38
  13.4 1.9 %collective-permute-start.7 = (bf16[4,2,128,128]{3,2,1,0:T(8,128)(2,1)S(1)}, bf16[4,2,128,128]{3,2,1,0:T(8,128)(2,1)S(1)}, u32[]{:S(2)}, u32[]{:S(2)}) collective-permute-start(bf16[4,2,128,128]{3,2,1,0:T(8,128)(2,1)S(1)} %pad_maximum_fusion.1.refs_3_), channel_id=1, source_target_pairs={{1,2},{2,1},{5,6},{6,5},{9,10},{10,9},{13,14},{14,13},{17,18},{18,... | collective-permute-start | bytes 786440 | tf_op jit(solution)/shard_map/ppermute | solution.py:38
  15.3 0.1 reshape.18.refs_0_
  15.5 1.3 %collective-permute-done.1 = bf16[144,384]{1,0:T(8,128)(2,1)S(1)} collective-permute-done((bf16[144,384]{1,0:T(8,128)(2,1)S(1)}, bf16[144,384]{1,0:T(8,128)(2,1)S(1)}, u32[]{:S(2)}, u32[]{:S(2)}) %collective-permute-start.1) | collective-permute-done | bytes 110624 | tf_op jit(solution)/shard_map/ppermute | solution.py:234
  16.9 3.0 %attend_near.1 = (f32[4,384,128]{2,1,0:T(8,128)S(1)}, f32[4,384,128]{2,1,0:T(8,128)S(1)}, f32[4,384,128]{2,1,0:T(8,128)S(1)}) custom-call(s32[32]{0:T(128)S(1)} %reshape.18.refs_0_, s32[16]{0:T(128)S(1)} %reshape.19.refs_1_, bf16[4,144,384]{2,1,0:T(8,128)(2,1)S(1)} %pad_maximum_fusion.refs_2_, bf16[4,2,128,128]{3,2,1,0:T(8,128)(2,1)S(1)} %pad_maximum_fusion.1.refs_3_, ...), custom_call_target="tpu_custom_call" | custom-call | flops 1000000000 | bytes 4000000 | tf_op jit(solution)/shard_map/attend_near/pallas_call | solution.py:284
  19.9 3.2 %collective-permute-done.7.refs_4_ = bf16[4,2,128,128]{3,2,1,0:T(8,128)(2,1)S(1)} collective-permute-done((bf16[4,2,128,128]{3,2,1,0:T(8,128)(2,1)S(1)}, bf16[4,2,128,128]{3,2,1,0:T(8,128)(2,1)S(1)}, u32[]{:S(2)}, u32[]{:S(2)}) %collective-permute-start.7) | collective-permute-done | bytes 262176 | tf_op jit(solution)/shard_map/ppermute | solution.py:38
  23.1 1.6 %attend_far_3.1 = bf16[128,384]{1,0:T(8,128)(2,1)S(1)} custom-call(s32[32]{0:T(128)S(1)} %reshape.18.refs_0_, s32[16]{0:T(128)S(1)} %reshape.19.refs_1_, bf16[4,144,384]{2,1,0:T(8,128)(2,1)S(1)} %pad_maximum_fusion.refs_2_, bf16[4,2,128,128]{3,2,1,0:T(8,128)(2,1)S(1)} %collective-permute-done.6.refs_3_, ...), custom_call_target="tpu_custom_call" | custom-call | tf_op jit(solution)/shard_map/attend_far_3/pallas_call | solution.py:299
  24.7 0.1 collective-permute-start.11
  24.8 1.5 %attend_far_2.1 = bf16[128,384]{1,0:T(8,128)(2,1)S(1)} custom-call(s32[32]{0:T(128)S(1)} %reshape.18.refs_0_, s32[16]{0:T(128)S(1)} %reshape.19.refs_1_, bf16[4,144,384]{2,1,0:T(8,128)(2,1)S(1)} %pad_maximum_fusion.refs_2_, bf16[4,2,128,128]{3,2,1,0:T(8,128)(2,1)S(1)} %collective-permute-done.6.refs_3_, ...), custom_call_target="tpu_custom_call" | custom-call | tf_op jit(solution)/shard_map/attend_far_2/pallas_call | solution.py:299
  26.3 1.7 %collective-permute-start.10 = (bf16[128,384]{1,0:T(8,128)(2,1)S(1)}, bf16[128,384]{1,0:T(8,128)(2,1)S(1)}, u32[]{:S(2)}, u32[]{:S(2)}) collective-permute-start(bf16[128,384]{1,0:T(8,128)(2,1)S(1)} %attend_far_2.1), channel_id=1, source_target_pairs={{0,16},{8,24},{16,0},{24,8},{1,17},{9,25},{17,1},{25,9},{2,18},{10... | collective-permute-start | bytes 294920 | tf_op jit(solution)/shard_map/ppermute | solution.py:234
  27.9 1.2 %attend_far_1.1 = bf16[128,384]{1,0:T(8,128)(2,1)S(1)} custom-call(s32[32]{0:T(128)S(1)} %reshape.18.refs_0_, s32[16]{0:T(128)S(1)} %reshape.19.refs_1_, bf16[4,144,384]{2,1,0:T(8,128)(2,1)S(1)} %pad_maximum_fusion.refs_2_, bf16[4,2,128,128]{3,2,1,0:T(8,128)(2,1)S(1)} %collective-permute-done.6.refs_3_, ...), custom_call_target="tpu_custom_call" | custom-call | tf_op jit(solution)/shard_map/attend_far_1/pallas_call | solution.py:299
  29.1 1.5 %collective-permute-start.9 = (bf16[128,384]{1,0:T(8,128)(2,1)S(1)}, bf16[128,384]{1,0:T(8,128)(2,1)S(1)}, u32[]{:S(2)}, u32[]{:S(2)}) collective-permute-start(bf16[128,384]{1,0:T(8,128)(2,1)S(1)} %attend_far_1.1), channel_id=1, source_target_pairs={{0,8},{8,0},{16,24},{24,16},{1,9},{9,1},{17,25},{25,17},{2,10},{10... | collective-permute-start | bytes 294920 | tf_op jit(solution)/shard_map/ppermute | solution.py:234
  30.6 1.1 %attend_far_0.1.refs_0_ = bf16[128,384]{1,0:T(8,128)(2,1)S(1)} custom-call(s32[32]{0:T(128)S(1)} %reshape.18.refs_0_, s32[16]{0:T(128)S(1)} %reshape.19.refs_1_, bf16[4,144,384]{2,1,0:T(8,128)(2,1)S(1)} %pad_maximum_fusion.refs_2_, bf16[4,2,128,128]{3,2,1,0:T(8,128)(2,1)S(1)} %collective-permute-done.6.refs_3_, ...), custom_call_target="tpu_custom_call" | custom-call | tf_op jit(solution)/shard_map/attend_far_0/pallas_call | solution.py:299
  31.7 2.1 %collective-permute-done.9.refs_1_ = bf16[128,384]{1,0:T(8,128)(2,1)S(1)} collective-permute-done((bf16[128,384]{1,0:T(8,128)(2,1)S(1)}, bf16[128,384]{1,0:T(8,128)(2,1)S(1)}, u32[]{:S(2)}, u32[]{:S(2)}) %collective-permute-start.9) | collective-permute-done | bytes 98336 | tf_op jit(solution)/shard_map/ppermute | solution.py:234
  33.8 0.8 %join.1 = bf16[128,1536]{1,0:T(8,128)(2,1)} custom-call(bf16[128,384]{1,0:T(8,128)(2,1)S(1)} %attend_far_0.1.refs_0_, bf16[128,384]{1,0:T(8,128)(2,1)S(1)} %collective-permute-done.9.refs_1_, bf16[128,384]{1,0:T(8,128)(2,1)S(1)} %collective-permute-done.10.refs_2_, bf16[128,384]{1,0:T(8,128)(2,1)S(1)} %collective-permute-done.11.refs_3_), custom_call_target="tpu_custom_call" | custom-call | tf_op jit(solution)/shard_map/join/pallas_call | solution.py:317
  (15 shorter events, 0.3 us)
Async XLA Ops:
  1.3 5.9 %collective-permute-start.5 = (bf16[2,128,128]{2,1,0:T(8,128)(2,1)S(1)}, bf16[2,128,128]{2,1,0:T(8,128)(2,1)S(1)}, u32[]{:S(2)}, u32[]{:S(2)}) collective-permute-start(bf16[2,128,128]{2,1,0:T(8,128)(2,1)S(1)} %get-tuple-element.23), channel_id=1, source_target_pairs={{0,24},{8,16},{16,8},{24,0},{1,25},{9,17},{17,9},{25,1},{2,26},{10... | collective-permute-start | bytes 196616 | tf_op jit(solution)/shard_map/ppermute | solution.py:234
  3.8 5.0 %collective-permute-start.3 = (bf16[2,128,128]{2,1,0:T(8,128)(2,1)S(1)}, bf16[2,128,128]{2,1,0:T(8,128)(2,1)S(1)}, u32[]{:S(2)}, u32[]{:S(2)}) collective-permute-start(bf16[2,128,128]{2,1,0:T(8,128)(2,1)S(1)} %get-tuple-element.21), channel_id=1, source_target_pairs={{0,8},{8,0},{16,24},{24,16},{1,9},{9,1},{17,25},{25,17},{2,10},{10... | collective-permute-start | bytes 196616 | tf_op jit(solution)/shard_map/ppermute | solution.py:234
  4.4 4.5 %collective-permute-start.4 = (bf16[2,128,128]{2,1,0:T(8,128)(2,1)S(1)}, bf16[2,128,128]{2,1,0:T(8,128)(2,1)S(1)}, u32[]{:S(2)}, u32[]{:S(2)}) collective-permute-start(bf16[2,128,128]{2,1,0:T(8,128)(2,1)S(1)} %get-tuple-element.22), channel_id=1, source_target_pairs={{0,16},{8,24},{16,0},{24,8},{1,17},{9,25},{17,1},{25,9},{2,18},{10... | collective-permute-start | bytes 196616 | tf_op jit(solution)/shard_map/ppermute | solution.py:234
  4.9 8.5 %collective-permute-start = (bf16[144,384]{1,0:T(8,128)(2,1)S(1)}, bf16[144,384]{1,0:T(8,128)(2,1)S(1)}, u32[]{:S(2)}, u32[]{:S(2)}) collective-permute-start(bf16[144,384]{1,0:T(8,128)(2,1)S(1)} %get-tuple-element.17), channel_id=1, source_target_pairs={{0,8},{8,0},{16,24},{24,16},{1,9},{9,1},{17,25},{25,17},{2,10},{10... | collective-permute-start | bytes 331784 | tf_op jit(solution)/shard_map/ppermute | solution.py:234
  8.8 6.5 %copy-start = (s32[4,2,4]{2,1,0:T(2,128)S(1)}, s32[4,2,4]{2,1,0:T(2,128)}, u32[]{:S(2)}) copy-start(s32[4,2,4]{2,1,0:T(2,128)} %param.8) | copy-start | bytes 388
  8.9 8.0 %collective-permute-start.8 = (bf16[4,2,128,128]{3,2,1,0:T(8,128)(2,1)S(1)}, bf16[4,2,128,128]{3,2,1,0:T(8,128)(2,1)S(1)}, u32[]{:S(2)}, u32[]{:S(2)}) collective-permute-start(bf16[4,2,128,128]{3,2,1,0:T(8,128)(2,1)S(1)} %pad_maximum_fusion.1.refs_3_), channel_id=1, source_target_pairs={{0,4},{4,0},{1,5},{5,1},{2,6},{6,2},{3,7},{7,3},{8,12},{12,8},{9,1... | collective-permute-start | bytes 786440 | tf_op jit(solution)/shard_map/ppermute | solution.py:38
  9.0 7.8 %collective-permute-start.1 = (bf16[144,384]{1,0:T(8,128)(2,1)S(1)}, bf16[144,384]{1,0:T(8,128)(2,1)S(1)}, u32[]{:S(2)}, u32[]{:S(2)}) collective-permute-start(bf16[144,384]{1,0:T(8,128)(2,1)S(1)} %get-tuple-element.18), channel_id=1, source_target_pairs={{0,16},{8,24},{16,0},{24,8},{1,17},{9,25},{17,1},{25,9},{2,18},{10... | collective-permute-start | bytes 331784 | tf_op jit(solution)/shard_map/ppermute | solution.py:234
  9.4 6.0 %copy-start.1 = (s32[4,4]{1,0:T(4,128)S(1)}, s32[4,4]{1,0:T(4,128)}, u32[]{:S(2)}) copy-start(s32[4,4]{1,0:T(4,128)} %param.9) | copy-start | bytes 196
  9.4 7.4 %collective-permute-start.2 = (bf16[144,384]{1,0:T(8,128)(2,1)S(1)}, bf16[144,384]{1,0:T(8,128)(2,1)S(1)}, u32[]{:S(2)}, u32[]{:S(2)}) collective-permute-start(bf16[144,384]{1,0:T(8,128)(2,1)S(1)} %get-tuple-element.19), channel_id=1, source_target_pairs={{0,24},{8,16},{16,8},{24,0},{1,25},{9,17},{17,9},{25,1},{2,26},{10... | collective-permute-start | bytes 331784 | tf_op jit(solution)/shard_map/ppermute | solution.py:234
  11.8 8.1 %collective-permute-start.6 = (bf16[4,2,128,128]{3,2,1,0:T(8,128)(2,1)S(1)}, bf16[4,2,128,128]{3,2,1,0:T(8,128)(2,1)S(1)}, u32[]{:S(2)}, u32[]{:S(2)}) collective-permute-start(bf16[4,2,128,128]{3,2,1,0:T(8,128)(2,1)S(1)} %pad_maximum_fusion.1.refs_3_), channel_id=1, source_target_pairs={{0,1},{2,3},{1,0},{3,2},{4,5},{6,7},{5,4},{7,6},{8,9},{10,11},{9,8... | collective-permute-start | bytes 786440 | tf_op jit(solution)/shard_map/ppermute | solution.py:38
  13.4 9.7 %collective-permute-start.7 = (bf16[4,2,128,128]{3,2,1,0:T(8,128)(2,1)S(1)}, bf16[4,2,128,128]{3,2,1,0:T(8,128)(2,1)S(1)}, u32[]{:S(2)}, u32[]{:S(2)}) collective-permute-start(bf16[4,2,128,128]{3,2,1,0:T(8,128)(2,1)S(1)} %pad_maximum_fusion.1.refs_3_), channel_id=1, source_target_pairs={{1,2},{2,1},{5,6},{6,5},{9,10},{10,9},{13,14},{14,13},{17,18},{18,... | collective-permute-start | bytes 786440 | tf_op jit(solution)/shard_map/ppermute | solution.py:38
  24.7 7.0 %collective-permute-start.11 = (bf16[128,384]{1,0:T(8,128)(2,1)S(1)}, bf16[128,384]{1,0:T(8,128)(2,1)S(1)}, u32[]{:S(2)}, u32[]{:S(2)}) collective-permute-start(bf16[128,384]{1,0:T(8,128)(2,1)S(1)} %attend_far_3.1), channel_id=1, source_target_pairs={{0,24},{8,16},{16,8},{24,0},{1,25},{9,17},{17,9},{25,1},{2,26},{10... | collective-permute-start | bytes 294920 | tf_op jit(solution)/shard_map/ppermute | solution.py:234
  26.3 5.4 %collective-permute-start.10 = (bf16[128,384]{1,0:T(8,128)(2,1)S(1)}, bf16[128,384]{1,0:T(8,128)(2,1)S(1)}, u32[]{:S(2)}, u32[]{:S(2)}) collective-permute-start(bf16[128,384]{1,0:T(8,128)(2,1)S(1)} %attend_far_2.1), channel_id=1, source_target_pairs={{0,16},{8,24},{16,0},{24,8},{1,17},{9,25},{17,1},{25,9},{2,18},{10... | collective-permute-start | bytes 294920 | tf_op jit(solution)/shard_map/ppermute | solution.py:234
  29.1 4.7 %collective-permute-start.9 = (bf16[128,384]{1,0:T(8,128)(2,1)S(1)}, bf16[128,384]{1,0:T(8,128)(2,1)S(1)}, u32[]{:S(2)}, u32[]{:S(2)}) collective-permute-start(bf16[128,384]{1,0:T(8,128)(2,1)S(1)} %attend_far_1.1), channel_id=1, source_target_pairs={{0,8},{8,0},{16,24},{24,16},{1,9},{9,1},{17,25},{25,17},{2,10},{10... | collective-permute-start | bytes 294920 | tf_op jit(solution)/shard_map/ppermute | solution.py:234

commit v3 on v2

v3 whole, which is shorter than its diff:
```python
import functools
import math

import jax
import jax.numpy as jnp
from jax import lax
from jax.experimental import pallas as pl
from jax.experimental.pallas import tpu as pltpu
from jax.sharding import PartitionSpec as P

HEAD_SIZE = 128
NEIGH = 5
EXTRA = 16
OWN_FLOPS = 10_000_000_000
LATER_FLOPS = 1_000_000
DEAD = -1e30
VMEM_LIMIT = 40 * 1024 * 1024


def vmem():
    return pl.BlockSpec(memory_space=pltpu.VMEM)


def smem():
    return pl.BlockSpec(memory_space=pltpu.SMEM)


def pairings(count):
    found = []
    for first in (0, 1):
        pairs = [(i, i + 1) for i in range(first, count - 1, 2)]
        if pairs:
            found.append(pairs)
    return found


def swap(block, sizes, dim, pairs):
    rows, cols = sizes
    paired = {i: j for a, b in pairs for i, j in ((a, b), (b, a))}
    moves = []
    for row in range(rows):
        for col in range(cols):
            place = [row, col]
            if place[dim] in paired:
                place[dim] = paired[place[dim]]
            elif dim == 1 and rows % 2 == 0:
                place[0] = row ^ 1
            else:
                continue
            moves.append((row * cols + col, place[0] * cols + place[1]))
    return lax.ppermute(block, ("ty", "tx"), moves)


def partner(place, count, first):
    low = lax.rem(place + first, 2) == 0
    step = jnp.where(low, 1, -1)
    other = place + step
    return jnp.where((other >= 0) & (other < count), step, 0)


def split(spans, pattern_hbm, kv_hbm, q_hbm, *refs):
    kv_refs, q_refs = refs[:spans], refs[spans : 2 * spans]
    pattern_ref, kv_sem, q_sem, pattern_sem = refs[2 * spans :]
    me = lax.axis_index("span")
    kv_width = kv_hbm.shape[1] // 2
    rows = q_hbm.shape[0]
    width = q_hbm.shape[1] // spans
    copies = [pltpu.make_async_copy(pattern_hbm, pattern_ref, pattern_sem)]
    for k in range(spans):
        head = me ^ k
        for part in range(2):
            start = pl.multiple_of(part * kv_width + head * HEAD_SIZE, HEAD_SIZE)
            copies.append(
                pltpu.make_async_copy(
                    kv_hbm.at[:, pl.ds(start, HEAD_SIZE)], kv_refs[k].at[part], kv_sem.at[k, part]
                )
            )
    for k in range(spans):
        start = pl.multiple_of((me ^ k) * width, HEAD_SIZE)
        copies.append(
            pltpu.make_async_copy(
                q_hbm.at[:, pl.ds(start, width)], q_refs[k].at[pl.ds(0, rows)], q_sem.at[k]
            )
        )
    for copy in copies:
        copy.start()
    copies[0].wait()
    row_ids = lax.broadcasted_iota(jnp.int32, (EXTRA, width), 0)
    extra = jnp.zeros((EXTRA, width), jnp.float32)
    for o in range(NEIGH):
        extra = jnp.where(row_ids == o, pattern_ref[o].astype(jnp.float32), extra)
    extra = extra.astype(jnp.bfloat16)
    for k in range(spans):
        q_refs[k][rows:] = extra
    for copy in copies[1:]:
        copy.wait()


def window_masks(spans, sizes, ways, counts_ref, mask_ref, q_ref, bias_ref, keep_ref):
    me = lax.axis_index("span")
    at = [lax.axis_index(axis) for axis in ("ty", "tx")]
    slots = q_ref.shape[1] - EXTRA
    lanes = lax.broadcasted_iota(jnp.int32, (1, slots), 1)
    row_ids = lax.broadcasted_iota(jnp.int32, (slots, HEAD_SIZE), 0)

    def count(span, step_row, step_col):
        return counts_ref[(span * sizes[0] + at[0] + step_row) * sizes[1] + at[1] + step_col]

    for span in range(spans):
        extra = q_ref[me ^ span, slots:, :HEAD_SIZE].astype(jnp.float32)
        keep_ref[span] = jnp.where(row_ids < count(span, 0, 0), 1.0, 0.0)
        for t, way in enumerate(ways):
            if way is None:
                chosen, move, here = extra[0:1], (0, 0), True
            else:
                dim, first = way
                step = partner(at[dim], sizes[dim], first)
                base = 1 + 2 * dim
                chosen = jnp.where(step > 0, extra[base + 1 : base + 2], extra[base : base + 1])
                move, here = ((step, 0) if dim == 0 else (0, step)), step != 0
            for other in range(span + 1):
                seen = (mask_ref[span * spans + other] > 0) & here
                near = jnp.where(seen, count(other, *move), 0)
                bias_ref[span, t : t + 1, other * slots : (other + 1) * slots] = jnp.where(
                    (lanes < near) & (chosen > 0), 0.0, DEAD
                )


def attend(spans, sizes, ways, number, *refs):
    first, last = number == 0, number == len(ways) - 1
    if first:
        (counts_ref, mask_ref, q_ref, tile_ref), refs = refs[:4], refs[4:]
    else:
        (q_ref, tile_ref, bias_ref, keep_ref, top_in, sum_in, acc_in), refs = refs[:7], refs[7:]
    if last:
        (out_ref,), refs = refs[:1], refs[1:]
    else:
        (top_ref, sum_ref, acc_ref), refs = refs[:3], refs[3:]
    if first:
        (bias_ref, keep_ref), refs = refs[:2], refs[2:]
        window_masks(spans, sizes, ways, counts_ref, mask_ref, q_ref, bias_ref, keep_ref)
    (score_ref,) = refs
    me = lax.axis_index("span")
    tok_rows = q_ref.shape[1] - EXTRA
    groups = q_ref.shape[2] // HEAD_SIZE
    factor = HEAD_SIZE ** (-0.5) * math.log2(math.e)

    def gathered(span, part):
        return jnp.concatenate([tile_ref[me ^ other, part] for other in range(span + 1)], axis=0)

    def score(span):
        query = jnp.concatenate(
            [q_ref[me ^ span, :tok_rows, g * HEAD_SIZE : (g + 1) * HEAD_SIZE] for g in range(groups)],
            axis=0,
        )
        keys = gathered(span, 0)
        score_ref[span, :, : keys.shape[0]] = lax.dot_general(
            query, keys, (((1,), (1,)), ((), ())), preferred_element_type=jnp.float32
        )

    def weigh(span):
        values = gathered(span, 1)
        bias = bias_ref[span, number : number + 1, : values.shape[0]]
        blocks = [slice(b, b + HEAD_SIZE) for b in range(0, values.shape[0], HEAD_SIZE)]
        for g in range(groups):
            rows = slice(g * tok_rows, (g + 1) * tok_rows)
            shape = (tok_rows, HEAD_SIZE)
            before = jnp.full(shape, DEAD, jnp.float32) if first else top_in[span, rows]
            top = before
            for lanes in blocks:
                top = jnp.maximum(top, score_ref[span, rows, lanes] + bias[:, lanes])
            top = jnp.broadcast_to(jnp.max(top, axis=1, keepdims=True), shape)
            total, weights = jnp.zeros(shape, jnp.float32), []
            for lanes in blocks:
                weight = jnp.exp2((score_ref[span, rows, lanes] + bias[:, lanes] - top) * factor)
                total = total + weight
                weights.append(weight.astype(jnp.bfloat16))
            result = jnp.dot(
                jnp.concatenate(weights, axis=1), values, preferred_element_type=jnp.float32
            )
            if not first:
                fade = jnp.exp2((before - top) * factor)
                total = total + sum_in[span, rows] * fade
                result = result + acc_in[span, rows] * fade
            if not last:
                top_ref[span, rows], sum_ref[span, rows], acc_ref[span, rows] = top, total, result
                continue
            share = 1.0 / jnp.sum(total, axis=1, keepdims=True)
            result = result * jnp.where(top > 0.5 * DEAD, share, jnp.nan)
            out_ref[me ^ span, :, g * HEAD_SIZE : (g + 1) * HEAD_SIZE] = jnp.where(
                keep_ref[span] > 0, result, 0.0
            ).astype(jnp.bfloat16)

    score(0)
    for span in range(spans):
        if span + 1 < spans:
            score(span + 1)
        weigh(span)


def join(spans, *refs):
    me = lax.axis_index("span")
    out_ref = refs[spans]
    width = refs[0].shape[1]
    for k in range(spans):
        start = pl.multiple_of((me ^ k) * width, HEAD_SIZE)
        out_ref[:, pl.ds(start, width)] = refs[k][...]


def shards(queries, key_value, pattern, counts, span_mask):
    spans, ty_count, tx_count = (lax.axis_size(a) for a in ("span", "ty", "tx"))
    tok_rows = queries.shape[3]
    kv_heads = key_value.shape[4] // (2 * HEAD_SIZE)
    assert kv_heads == spans and spans & (spans - 1) == 0
    width = queries.shape[4] // spans
    groups = width // HEAD_SIZE
    bf16 = jnp.bfloat16
    params = pltpu.CompilerParams(vmem_limit_bytes=VMEM_LIMIT)

    def exchange(block, k):
        return lax.ppermute(block, "span", [(i, i ^ k) for i in range(spans)])

    sizes = (ty_count, tx_count)
    order = sorted(range(1, spans), key=lambda k: -bin(k).count("1"))

    pieces = pl.pallas_call(
        functools.partial(split, spans),
        out_shape=[jax.ShapeDtypeStruct((2, tok_rows, HEAD_SIZE), bf16)] * spans
        + [jax.ShapeDtypeStruct((tok_rows + EXTRA, width), bf16)] * spans,
        in_specs=[pl.BlockSpec(memory_space=pltpu.HBM)] * 3,
        out_specs=[vmem()] * (2 * spans),
        scratch_shapes=[
            pltpu.SMEM((NEIGH,), jnp.int32),
            pltpu.SemaphoreType.DMA((spans, 2)),
            pltpu.SemaphoreType.DMA((spans,)),
            pltpu.SemaphoreType.DMA,
        ],
        compiler_params=params,
        name="split",
    )(
        *(
            pltpu.with_memory_space_constraint(x, pltpu.HBM)
            for x in (
                pattern.reshape(NEIGH),
                key_value.reshape(tok_rows, -1),
                queries.reshape(tok_rows, -1),
            )
        )
    )
    kv_pieces, q_pieces = pieces[:spans], pieces[spans:]

    column = [kv_pieces[0]] + [None] * (spans - 1)
    for k in order:
        column[k] = exchange(kv_pieces[k], k)
    own = jnp.stack(column)
    q_here = [q_pieces[0]] + [None] * (spans - 1)
    for k in order:
        q_here[k] = exchange(q_pieces[k], k)

    sizes = (ty_count, tx_count)
    rows = groups * tok_rows
    q_all = jnp.stack(q_here)
    scalars = (counts.reshape(-1), span_mask.reshape(-1))

    ways, tiles = [None], [own]
    for dim, backwards in ((0, False), (1, True)):
        found = list(enumerate(pairings(sizes[dim])))
        for first, pairs in reversed(found) if backwards else found:
            ways.append((dim, first))
            tiles.append(swap(own, sizes, dim, pairs))

    kept = jax.ShapeDtypeStruct((spans, rows, HEAD_SIZE), jnp.float32)
    bias = jax.ShapeDtypeStruct((spans, 8, spans * tok_rows), jnp.float32)
    keep = jax.ShapeDtypeStruct((spans, tok_rows, HEAD_SIZE), jnp.float32)
    result = jax.ShapeDtypeStruct((spans, tok_rows, width), bf16)
    masks = state = ()
    for number, tile in enumerate(tiles):
        first, last = number == 0, number == len(tiles) - 1
        outs = ([result] if last else [kept] * 3) + ([bias, keep] if first else [])
        given = (*scalars, q_all, tile) if first else (q_all, tile, *masks, *state)
        state = pl.pallas_call(
            functools.partial(attend, spans, sizes, tuple(ways), number),
            out_shape=outs,
            in_specs=([smem()] * 2 + [vmem()] * 2) if first else [vmem()] * len(given),
            out_specs=[vmem()] * len(outs),
            scratch_shapes=[pltpu.VMEM((spans, rows, spans * tok_rows), jnp.float32)],
            compiler_params=params,
            cost_estimate=pl.CostEstimate(
                flops=OWN_FLOPS if first else LATER_FLOPS, bytes_accessed=4_000_000, transcendentals=0
            ),
            name=f"attend_{number}",
        )(*given)
        if first and not last:
            state, masks = state[:3], state[3:]
    outs = state[0]

    home = [outs[0]] + [None] * (spans - 1)
    for k in order:
        home[k] = exchange(outs[k], k)
    attended = pl.pallas_call(
        functools.partial(join, spans),
        out_shape=jax.ShapeDtypeStruct((tok_rows, spans * width), bf16),
        in_specs=[vmem()] * spans,
        out_specs=vmem(),
        compiler_params=params,
        name="join",
    )(*home)
    return attended.reshape(1, 1, 1, tok_rows, -1)


def solution(mesh):
    return jax.shard_map(
        shards,
        mesh=mesh,
        in_specs=(
            P("span", "ty", "tx", None, None),
            P("span", "ty", "tx", None, None),
            P("span", "ty", "tx", None),
            P(),
            P(),
        ),
        out_specs=P("span", "ty", "tx", None, None),
        check_vma=False,
    )
```

time: 34.7 us -> 31.5 us (0.908)
  the two profiles are of different devices: /device:TPU:16 before, /device:TPU:0 now
where the time goes in v3:
time: 31.5 us; the launch traced here: 31.4 us
  starting transfers between devices  15.6 us (50%)
  waiting for transfers between devices  8.16 us (26%)
  Pallas kernels  7.25 us (23%)
    ppermute x9, starting transfers between devices, exchange(): return lax.ppermute(block, 'span', [(i, i ^ k) for i in range(spans)])  13.2 us
    ppermute x9, waiting for transfers between devices, exchange(): return lax.ppermute(block, 'span', [(i, i ^ k) for i in range(spans)])  6.14 us
    pallas_call x4, Pallas kernels, shards(): pl.pallas_call(functools.partial(attend, spans, sizes, tuple(ways), numbe...  5.15 us
    ppermute x3, starting transfers between devices, swap(): return lax.ppermute(block, ('ty', 'tx'), moves)  2.37 us
    ppermute x3, waiting for transfers between devices, swap(): return lax.ppermute(block, ('ty', 'tx'), moves)  2.02 us
    pallas_call x1, Pallas kernels, shards(): pl.pallas_call(functools.partial(split, spans), out_shape=[jax.ShapeDtype...  1.29 us
    pallas_call x1, Pallas kernels, shards(): pl.pallas_call(functools.partial(join, spans), out_shape=jax.ShapeDtypeSt...  0.8 us
  transfers between devices with their start and end apart: 12, of which 6 were waited for; matrix products, arithmetic and copies ran while one was open for 1% of the time, Pallas kernels for 12%

profile of v3, /device:TPU:0, one launch (start us, length us, event | category | flops | bytes accessed | tf_op | source)
XLA Modules:
  0.0 31.4 jit_solution(15619595937542174852)
XLA Ops:
  0.0 1.3 %split.1 = (bf16[2,128,128]{2,1,0:T(8,128)(2,1)S(1)}, bf16[2,128,128]{2,1,0:T(8,128)(2,1)S(1)}, bf16[2,128,128]{2,1,0:T(8,128)(2,1)S(1)}, bf16[2,128,128]{2,1,0:...) custom-call(s32[5]{0:T(128)} %bitcast.30, ...), custom_call_target="tpu_custom_call" | custom-call | tf_op jit(solution)/shard_map/split/pallas_call | solution.py:226
  1.3 4.0 %collective-permute-start.5 = (bf16[2,128,128]{2,1,0:T(8,128)(2,1)S(1)}, bf16[2,128,128]{2,1,0:T(8,128)(2,1)S(1)}, u32[]{:S(2)}, u32[]{:S(2)}) collective-permute-start(bf16[2,128,128]{2,1,0:T(8,128)(2,1)S(1)} %get-tuple-element.31), channel_id=1, source_target_pairs={{0,24},{8,16},{16,8},{24,0},{1,25},{9,17},{17,9},{25,1},{2,26},{10... | collective-permute-start | bytes 196616 | tf_op jit(solution)/shard_map/ppermute | solution.py:221
  5.3 0.5 %collective-permute-start.3 = (bf16[2,128,128]{2,1,0:T(8,128)(2,1)S(1)}, bf16[2,128,128]{2,1,0:T(8,128)(2,1)S(1)}, u32[]{:S(2)}, u32[]{:S(2)}) collective-permute-start(bf16[2,128,128]{2,1,0:T(8,128)(2,1)S(1)} %get-tuple-element.29), channel_id=1, source_target_pairs={{0,8},{8,0},{16,24},{24,16},{1,9},{9,1},{17,25},{25,17},{2,10},{10... | collective-permute-start | bytes 196616 | tf_op jit(solution)/shard_map/ppermute | solution.py:221
  5.8 0.1 collective-permute-start.4
  5.9 1.9 %collective-permute-start = (bf16[144,384]{1,0:T(8,128)(2,1)S(1)}, bf16[144,384]{1,0:T(8,128)(2,1)S(1)}, u32[]{:S(2)}, u32[]{:S(2)}) collective-permute-start(bf16[144,384]{1,0:T(8,128)(2,1)S(1)} %get-tuple-element.25), channel_id=1, source_target_pairs={{0,8},{8,0},{16,24},{24,16},{1,9},{9,1},{17,25},{25,17},{2,10},{10... | collective-permute-start | bytes 331784 | tf_op jit(solution)/shard_map/ppermute | solution.py:221
  7.8 1.5 %collective-permute-start.1 = (bf16[144,384]{1,0:T(8,128)(2,1)S(1)}, bf16[144,384]{1,0:T(8,128)(2,1)S(1)}, u32[]{:S(2)}, u32[]{:S(2)}) collective-permute-start(bf16[144,384]{1,0:T(8,128)(2,1)S(1)} %get-tuple-element.26), channel_id=1, source_target_pairs={{0,16},{8,24},{16,0},{24,8},{1,17},{9,25},{17,1},{25,9},{2,18},{10... | collective-permute-start | bytes 331784 | tf_op jit(solution)/shard_map/ppermute | solution.py:221
  9.3 0.1 reshape.21.refs_0_
  9.5 1.6 %collective-permute-start.2 = (bf16[144,384]{1,0:T(8,128)(2,1)S(1)}, bf16[144,384]{1,0:T(8,128)(2,1)S(1)}, u32[]{:S(2)}, u32[]{:S(2)}) collective-permute-start(bf16[144,384]{1,0:T(8,128)(2,1)S(1)} %get-tuple-element.27), channel_id=1, source_target_pairs={{0,24},{8,16},{16,8},{24,0},{1,25},{9,17},{17,9},{25,1},{2,26},{10... | collective-permute-start | bytes 331784 | tf_op jit(solution)/shard_map/ppermute | solution.py:221
  11.2 0.5 %collective-permute-start.7 = (bf16[4,2,128,128]{3,2,1,0:T(8,128)(2,1)S(1)}, bf16[4,2,128,128]{3,2,1,0:T(8,128)(2,1)S(1)}, u32[]{:S(2)}, u32[]{:S(2)}) collective-permute-start(bf16[4,2,128,128]{3,2,1,0:T(8,128)(2,1)S(1)} %pad_maximum_fusion.1.refs_3_), channel_id=1, source_target_pairs={{0,4},{1,2},{2,1},{3,7},{4,0},{5,6},{6,5},{7,3},{8,12},{9,10},{10,... | collective-permute-start | bytes 786440 | tf_op jit(solution)/shard_map/ppermute | solution.py:51
  11.7 0.9 %collective-permute-done = bf16[144,384]{1,0:T(8,128)(2,1)S(1)} collective-permute-done((bf16[144,384]{1,0:T(8,128)(2,1)S(1)}, bf16[144,384]{1,0:T(8,128)(2,1)S(1)}, u32[]{:S(2)}, u32[]{:S(2)}) %collective-permute-start) | collective-permute-done | bytes 110624 | tf_op jit(solution)/shard_map/ppermute | solution.py:221
  12.7 1.8 %collective-permute-start.6 = (bf16[4,2,128,128]{3,2,1,0:T(8,128)(2,1)S(1)}, bf16[4,2,128,128]{3,2,1,0:T(8,128)(2,1)S(1)}, u32[]{:S(2)}, u32[]{:S(2)}) collective-permute-start(bf16[4,2,128,128]{3,2,1,0:T(8,128)(2,1)S(1)} %pad_maximum_fusion.1.refs_3_), channel_id=1, source_target_pairs={{0,1},{1,0},{2,3},{3,2},{4,5},{5,4},{6,7},{7,6},{8,9},{9,8},{10,11... | collective-permute-start | bytes 786440 | tf_op jit(solution)/shard_map/ppermute | solution.py:51
  14.5 0.7 %collective-permute-done.2 = bf16[144,384]{1,0:T(8,128)(2,1)S(1)} collective-permute-done((bf16[144,384]{1,0:T(8,128)(2,1)S(1)}, bf16[144,384]{1,0:T(8,128)(2,1)S(1)}, u32[]{:S(2)}, u32[]{:S(2)}) %collective-permute-start.2) | collective-permute-done | bytes 110624 | tf_op jit(solution)/shard_map/ppermute | solution.py:221
  15.2 1.6 %attend_0.1 = (f32[4,384,128]{2,1,0:T(8,128)S(1)}, f32[4,384,128]{2,1,0:T(8,128)S(1)}, f32[4,384,128]{2,1,0:T(8,128)S(1)}, f32[4,8,512]{2,1,0:T(8,128)S(1)}, f32[4,128,128]{2,1,0:T(8,128)S(1)}) custom-call(s32[32]{0:T(128)S(1)} %reshape.21.refs_0_, s32[16]{0:T(128)S(1)} %reshape.22.refs_1_, bf16[4,144,384]{2,1,0:T(8,128)(2,1)S(1)} %pad_maximum_fusion.refs_2_.refs_0_, ...), custom_call_target="tpu_custom_call" | custom-call | flops 10000000000 | bytes 4000000 | tf_op jit(solution)/shard_map/attend_0/pallas_call | solution.py:281
  16.8 1.2 %attend_1.1 = (f32[4,384,128]{2,1,0:T(8,128)S(1)}, f32[4,384,128]{2,1,0:T(8,128)S(1)}, f32[4,384,128]{2,1,0:T(8,128)S(1)}) custom-call(bf16[4,144,384]{2,1,0:T(8,128)(2,1)S(1)} %pad_maximum_fusion.refs_2_.refs_0_, bf16[4,2,128,128]{3,2,1,0:T(8,128)(2,1)S(1)} %collective-permute-done.8.refs_1_, f32[4,8,512]{2,1,0:T(8,128)S(1)} %get-tuple-element.32.refs_2_, ...), custom_call_target="tpu_custom_call" | custom-call | flops 1000000 | bytes 4000000 | tf_op jit(solution)/shard_map/attend_1/pallas_call | solution.py:281
  18.0 1.1 %attend_2.1 = (f32[4,384,128]{2,1,0:T(8,128)S(1)}, f32[4,384,128]{2,1,0:T(8,128)S(1)}, f32[4,384,128]{2,1,0:T(8,128)S(1)}) custom-call(bf16[4,144,384]{2,1,0:T(8,128)(2,1)S(1)} %pad_maximum_fusion.refs_2_.refs_0_, bf16[4,2,128,128]{3,2,1,0:T(8,128)(2,1)S(1)} %collective-permute-done.7.refs_1_, f32[4,8,512]{2,1,0:T(8,128)S(1)} %get-tuple-element.32.refs_2_, ...), custom_call_target="tpu_custom_call" | custom-call | flops 1000000 | bytes 4000000 | tf_op jit(solution)/shard_map/attend_2/pallas_call | solution.py:281
  19.1 2.0 %collective-permute-done.6.refs_1_ = bf16[4,2,128,128]{3,2,1,0:T(8,128)(2,1)S(1)} collective-permute-done((bf16[4,2,128,128]{3,2,1,0:T(8,128)(2,1)S(1)}, bf16[4,2,128,128]{3,2,1,0:T(8,128)(2,1)S(1)}, u32[]{:S(2)}, u32[]{:S(2)}) %collective-permute-start.6) | collective-permute-done | bytes 262176 | tf_op jit(solution)/shard_map/ppermute | solution.py:51
  21.1 1.3 %attend_3.1 = bf16[4,128,384]{2,1,0:T(8,128)(2,1)S(1)} custom-call(bf16[4,144,384]{2,1,0:T(8,128)(2,1)S(1)} %pad_maximum_fusion.refs_2_.refs_0_, bf16[4,2,128,128]{3,2,1,0:T(8,128)(2,1)S(1)} %collective-permute-done.6.refs_1_, f32[4,8,512]{2,1,0:T(8,128)S(1)} %get-tuple-element.32.refs_2_, f32[4,128,128]{2,1,0:T(8,128)S(1)} %get-tuple-element.33.refs_3_, ...), custom_call_target="tpu_custom_call" | custom-call | flops 1000000 | bytes 4000000 | tf_op jit(solution)/shard_map/attend_3/pallas_call | solution.py:281
  22.5 0.5 %collective-permute-start.10 = (bf16[128,384]{1,0:T(8,128)(2,1)S(1)}, bf16[128,384]{1,0:T(8,128)(2,1)S(1)}, u32[]{:S(2)}, u32[]{:S(2)}) collective-permute-start(bf16[128,384]{1,0:T(8,128)(2,1)S(1)} %get-tuple-element.44), channel_id=1, source_target_pairs={{0,16},{8,24},{16,0},{24,8},{1,17},{9,25},{17,1},{25,9},{2,18},{10... | collective-permute-start | bytes 294920 | tf_op jit(solution)/shard_map/ppermute | solution.py:221
  23.0 2.8 %collective-permute-start.11 = (bf16[128,384]{1,0:T(8,128)(2,1)S(1)}, bf16[128,384]{1,0:T(8,128)(2,1)S(1)}, u32[]{:S(2)}, u32[]{:S(2)}) collective-permute-start(bf16[128,384]{1,0:T(8,128)(2,1)S(1)} %get-tuple-element.43), channel_id=1, source_target_pairs={{0,24},{8,16},{16,8},{24,0},{1,25},{9,17},{17,9},{25,1},{2,26},{10... | collective-permute-start | bytes 294920 | tf_op jit(solution)/shard_map/ppermute | solution.py:221
  25.7 0.3 %collective-permute-start.9 = (bf16[128,384]{1,0:T(8,128)(2,1)S(1)}, bf16[128,384]{1,0:T(8,128)(2,1)S(1)}, u32[]{:S(2)}, u32[]{:S(2)}) collective-permute-start(bf16[128,384]{1,0:T(8,128)(2,1)S(1)} %get-tuple-element.45), channel_id=1, source_target_pairs={{0,8},{8,0},{16,24},{24,16},{1,9},{9,1},{17,25},{25,17},{2,10},{10... | collective-permute-start | bytes 294920 | tf_op jit(solution)/shard_map/ppermute | solution.py:221
  26.1 2.6 %collective-permute-done.10.refs_2_ = bf16[128,384]{1,0:T(8,128)(2,1)S(1)} collective-permute-done((bf16[128,384]{1,0:T(8,128)(2,1)S(1)}, bf16[128,384]{1,0:T(8,128)(2,1)S(1)}, u32[]{:S(2)}, u32[]{:S(2)}) %collective-permute-start.10) | collective-permute-done | bytes 98336 | tf_op jit(solution)/shard_map/ppermute | solution.py:221
  28.7 0.6 %collective-permute-done.11.refs_3_ = bf16[128,384]{1,0:T(8,128)(2,1)S(1)} collective-permute-done((bf16[128,384]{1,0:T(8,128)(2,1)S(1)}, bf16[128,384]{1,0:T(8,128)(2,1)S(1)}, u32[]{:S(2)}, u32[]{:S(2)}) %collective-permute-start.11) | collective-permute-done | bytes 98336 | tf_op jit(solution)/shard_map/ppermute | solution.py:221
  29.3 1.3 %collective-permute-done.9.refs_1_ = bf16[128,384]{1,0:T(8,128)(2,1)S(1)} collective-permute-done((bf16[128,384]{1,0:T(8,128)(2,1)S(1)}, bf16[128,384]{1,0:T(8,128)(2,1)S(1)}, u32[]{:S(2)}, u32[]{:S(2)}) %collective-permute-start.9) | collective-permute-done | bytes 98336 | tf_op jit(solution)/shard_map/ppermute | solution.py:221
  30.6 0.8 %join.1 = bf16[128,1536]{1,0:T(8,128)(2,1)} custom-call(bf16[128,384]{1,0:T(8,128)(2,1)S(1)} %get-tuple-element.46.refs_0_, bf16[128,384]{1,0:T(8,128)(2,1)S(1)} %collective-permute-done.9.refs_1_, bf16[128,384]{1,0:T(8,128)(2,1)S(1)} %collective-permute-done.10.refs_2_, bf16[128,384]{1,0:T(8,128)(2,1)S(1)} %collective-permute-done.11.refs_3_), custom_call_target="tpu_custom_call" | custom-call | tf_op jit(solution)/shard_map/join/pallas_call | solution.py:300
  (15 shorter events, 0.3 us)
Async XLA Ops:
  1.3 8.0 %copy-start = (s32[4,2,4]{2,1,0:T(2,128)S(1)}, s32[4,2,4]{2,1,0:T(2,128)}, u32[]{:S(2)}) copy-start(s32[4,2,4]{2,1,0:T(2,128)} %param.8) | copy-start | bytes 388
  1.3 8.2 %collective-permute-start.5 = (bf16[2,128,128]{2,1,0:T(8,128)(2,1)S(1)}, bf16[2,128,128]{2,1,0:T(8,128)(2,1)S(1)}, u32[]{:S(2)}, u32[]{:S(2)}) collective-permute-start(bf16[2,128,128]{2,1,0:T(8,128)(2,1)S(1)} %get-tuple-element.31), channel_id=1, source_target_pairs={{0,24},{8,16},{16,8},{24,0},{1,25},{9,17},{17,9},{25,1},{2,26},{10... | collective-permute-start | bytes 196616 | tf_op jit(solution)/shard_map/ppermute | solution.py:221
  5.3 5.8 %collective-permute-start.3 = (bf16[2,128,128]{2,1,0:T(8,128)(2,1)S(1)}, bf16[2,128,128]{2,1,0:T(8,128)(2,1)S(1)}, u32[]{:S(2)}, u32[]{:S(2)}) collective-permute-start(bf16[2,128,128]{2,1,0:T(8,128)(2,1)S(1)} %get-tuple-element.29), channel_id=1, source_target_pairs={{0,8},{8,0},{16,24},{24,16},{1,9},{9,1},{17,25},{25,17},{2,10},{10... | collective-permute-start | bytes 196616 | tf_op jit(solution)/shard_map/ppermute | solution.py:221
  5.8 5.3 %collective-permute-start.4 = (bf16[2,128,128]{2,1,0:T(8,128)(2,1)S(1)}, bf16[2,128,128]{2,1,0:T(8,128)(2,1)S(1)}, u32[]{:S(2)}, u32[]{:S(2)}) collective-permute-start(bf16[2,128,128]{2,1,0:T(8,128)(2,1)S(1)} %get-tuple-element.30), channel_id=1, source_target_pairs={{0,16},{8,24},{16,0},{24,8},{1,17},{9,25},{17,1},{25,9},{2,18},{10... | collective-permute-start | bytes 196616 | tf_op jit(solution)/shard_map/ppermute | solution.py:221
  5.9 6.7 %collective-permute-start = (bf16[144,384]{1,0:T(8,128)(2,1)S(1)}, bf16[144,384]{1,0:T(8,128)(2,1)S(1)}, u32[]{:S(2)}, u32[]{:S(2)}) collective-permute-start(bf16[144,384]{1,0:T(8,128)(2,1)S(1)} %get-tuple-element.25), channel_id=1, source_target_pairs={{0,8},{8,0},{16,24},{24,16},{1,9},{9,1},{17,25},{25,17},{2,10},{10... | collective-permute-start | bytes 331784 | tf_op jit(solution)/shard_map/ppermute | solution.py:221
  7.8 1.6 %copy-start.1 = (s32[4,4]{1,0:T(4,128)S(1)}, s32[4,4]{1,0:T(4,128)}, u32[]{:S(2)}) copy-start(s32[4,4]{1,0:T(4,128)} %param.9) | copy-start | bytes 196
  7.8 6.7 %collective-permute-start.1 = (bf16[144,384]{1,0:T(8,128)(2,1)S(1)}, bf16[144,384]{1,0:T(8,128)(2,1)S(1)}, u32[]{:S(2)}, u32[]{:S(2)}) collective-permute-start(bf16[144,384]{1,0:T(8,128)(2,1)S(1)} %get-tuple-element.26), channel_id=1, source_target_pairs={{0,16},{8,24},{16,0},{24,8},{1,17},{9,25},{17,1},{25,9},{2,18},{10... | collective-permute-start | bytes 331784 | tf_op jit(solution)/shard_map/ppermute | solution.py:221
  9.5 5.7 %collective-permute-start.2 = (bf16[144,384]{1,0:T(8,128)(2,1)S(1)}, bf16[144,384]{1,0:T(8,128)(2,1)S(1)}, u32[]{:S(2)}, u32[]{:S(2)}) collective-permute-start(bf16[144,384]{1,0:T(8,128)(2,1)S(1)} %get-tuple-element.27), channel_id=1, source_target_pairs={{0,24},{8,16},{16,8},{24,0},{1,25},{9,17},{17,9},{25,1},{2,26},{10... | collective-permute-start | bytes 331784 | tf_op jit(solution)/shard_map/ppermute | solution.py:221
  11.2 5.6 %collective-permute-start.8 = (bf16[4,2,128,128]{3,2,1,0:T(8,128)(2,1)S(1)}, bf16[4,2,128,128]{3,2,1,0:T(8,128)(2,1)S(1)}, u32[]{:S(2)}, u32[]{:S(2)}) collective-permute-start(bf16[4,2,128,128]{3,2,1,0:T(8,128)(2,1)S(1)} %pad_maximum_fusion.1.refs_3_), channel_id=1, source_target_pairs={{0,4},{1,5},{2,6},{3,7},{4,0},{5,1},{6,2},{7,3},{8,12},{9,13},{10,... | collective-permute-start | bytes 786440 | tf_op jit(solution)/shard_map/ppermute | solution.py:51
  11.2 6.7 %collective-permute-start.7 = (bf16[4,2,128,128]{3,2,1,0:T(8,128)(2,1)S(1)}, bf16[4,2,128,128]{3,2,1,0:T(8,128)(2,1)S(1)}, u32[]{:S(2)}, u32[]{:S(2)}) collective-permute-start(bf16[4,2,128,128]{3,2,1,0:T(8,128)(2,1)S(1)} %pad_maximum_fusion.1.refs_3_), channel_id=1, source_target_pairs={{0,4},{1,2},{2,1},{3,7},{4,0},{5,6},{6,5},{7,3},{8,12},{9,10},{10,... | collective-permute-start | bytes 786440 | tf_op jit(solution)/shard_map/ppermute | solution.py:51
  12.7 8.4 %collective-permute-start.6 = (bf16[4,2,128,128]{3,2,1,0:T(8,128)(2,1)S(1)}, bf16[4,2,128,128]{3,2,1,0:T(8,128)(2,1)S(1)}, u32[]{:S(2)}, u32[]{:S(2)}) collective-permute-start(bf16[4,2,128,128]{3,2,1,0:T(8,128)(2,1)S(1)} %pad_maximum_fusion.1.refs_3_), channel_id=1, source_target_pairs={{0,1},{1,0},{2,3},{3,2},{4,5},{5,4},{6,7},{7,6},{8,9},{9,8},{10,11... | collective-permute-start | bytes 786440 | tf_op jit(solution)/shard_map/ppermute | solution.py:51
  22.5 6.2 %collective-permute-start.10 = (bf16[128,384]{1,0:T(8,128)(2,1)S(1)}, bf16[128,384]{1,0:T(8,128)(2,1)S(1)}, u32[]{:S(2)}, u32[]{:S(2)}) collective-permute-start(bf16[128,384]{1,0:T(8,128)(2,1)S(1)} %get-tuple-element.44), channel_id=1, source_target_pairs={{0,16},{8,24},{16,0},{24,8},{1,17},{9,25},{17,1},{25,9},{2,18},{10... | collective-permute-start | bytes 294920 | tf_op jit(solution)/shard_map/ppermute | solution.py:221
  23.0 6.4 %collective-permute-start.11 = (bf16[128,384]{1,0:T(8,128)(2,1)S(1)}, bf16[128,384]{1,0:T(8,128)(2,1)S(1)}, u32[]{:S(2)}, u32[]{:S(2)}) collective-permute-start(bf16[128,384]{1,0:T(8,128)(2,1)S(1)} %get-tuple-element.43), channel_id=1, source_target_pairs={{0,24},{8,16},{16,8},{24,0},{1,25},{9,17},{17,9},{25,1},{2,26},{10... | collective-permute-start | bytes 294920 | tf_op jit(solution)/shard_map/ppermute | solution.py:221
  25.7 4.9 %collective-permute-start.9 = (bf16[128,384]{1,0:T(8,128)(2,1)S(1)}, bf16[128,384]{1,0:T(8,128)(2,1)S(1)}, u32[]{:S(2)}, u32[]{:S(2)}) collective-permute-start(bf16[128,384]{1,0:T(8,128)(2,1)S(1)} %get-tuple-element.45), channel_id=1, source_target_pairs={{0,8},{8,0},{16,24},{24,16},{1,9},{9,1},{17,25},{25,17},{2,10},{10... | collective-permute-start | bytes 294920 | tf_op jit(solution)/shard_map/ppermute | solution.py:221

commit v4 on v3

--- a/solution.py
+++ b/solution.py
@@ -198,6 +198,13 @@
         weigh(span)
 
 
+def collect(spans, own_ref, *refs):
+    q_refs, (q_all_ref, copy_ref) = refs[:spans], refs[spans:]
+    for k in range(spans):
+        q_all_ref[k] = q_refs[k][...]
+    copy_ref[...] = own_ref[...]
+
+
 def join(spans, *refs):
     me = lax.axis_index("span")
     out_ref = refs[spans]
@@ -259,15 +266,25 @@
 
     sizes = (ty_count, tx_count)
     rows = groups * tok_rows
-    q_all = jnp.stack(q_here)
+    q_all, own_copy = pl.pallas_call(
+        functools.partial(collect, spans),
+        out_shape=[
+            jax.ShapeDtypeStruct((spans, *q_here[0].shape), bf16),
+            jax.ShapeDtypeStruct(own.shape, bf16),
+        ],
+        in_specs=[vmem()] * (1 + spans),
+        out_specs=[vmem()] * 2,
+        compiler_params=params,
+        name="collect",
+    )(own, *q_here)
     scalars = (counts.reshape(-1), span_mask.reshape(-1))
 
     ways, tiles = [None], [own]
-    for dim, backwards in ((0, False), (1, True)):
+    for dim, backwards in ((0, False), (1, False)):
         found = list(enumerate(pairings(sizes[dim])))
         for first, pairs in reversed(found) if backwards else found:
             ways.append((dim, first))
-            tiles.append(swap(own, sizes, dim, pairs))
+            tiles.append(swap(own if dim else own_copy, sizes, dim, pairs))
 
     kept = jax.ShapeDtypeStruct((spans, rows, HEAD_SIZE), jnp.float32)
     bias = jax.ShapeDtypeStruct((spans, 8, spans * tok_rows), jnp.float32)

time: 31.5 us -> 30.1 us (0.956)
  starting transfers between devices: 15.6 us -> 13.8 us
    ppermute x9, waiting for transfers between devices: 6.14 us -> 8.43 us  [exchange(): return lax.ppermute(block, 'span', [(i, i ^ k) for i in range(spans)])]
    ppermute x3, waiting for transfers between devices: 2.02 us -> 0.01 us  [swap(): return lax.ppermute(block, ('ty', 'tx'), moves)]
    ppermute x9, starting transfers between devices: 13.2 us -> 12.1 us  [exchange(): return lax.ppermute(block, 'span', [(i, i ^ k) for i in range(spans)])]
    ppermute x3, starting transfers between devices: 2.37 us -> 1.72 us  [swap(): return lax.ppermute(block, ('ty', 'tx'), moves)]
  transfers between devices with their start and end apart: 12 -> 12, of which waited for: 6 -> 6; matrix products, arithmetic and copies ran while one was open for 1% -> 1% of each run, Pallas kernels for 12% -> 13%
where the time goes in v4:
time: 30.1 us; the launch traced here: 30 us
  starting transfers between devices  13.8 us (46%)
  waiting for transfers between devices  8.44 us (28%)
  Pallas kernels  7.33 us (24%)
    ppermute x9, starting transfers between devices, exchange(): return lax.ppermute(block, 'span', [(i, i ^ k) for i in range(spans)])  12.1 us
    ppermute x9, waiting for transfers between devices, exchange(): return lax.ppermute(block, 'span', [(i, i ^ k) for i in range(spans)])  8.43 us
    pallas_call x4, Pallas kernels, shards(): pl.pallas_call(functools.partial(attend, spans, sizes, tuple(ways), numbe...  5.18 us
    ppermute x3, starting transfers between devices, swap(): return lax.ppermute(block, ('ty', 'tx'), moves)  1.72 us
    pallas_call x1, Pallas kernels, shards(): pl.pallas_call(functools.partial(split, spans), out_shape=[jax.ShapeDtype...  1.29 us
    pallas_call x1, Pallas kernels, shards(): pl.pallas_call(functools.partial(join, spans), out_shape=jax.ShapeDtypeSt...  0.8 us
  transfers between devices with their start and end apart: 12, of which 6 were waited for; matrix products, arithmetic and copies ran while one was open for 1% of the time, Pallas kernels for 13%

profile of v4, /device:TPU:0, one launch (start us, length us, event | category | flops | bytes accessed | tf_op | source)
XLA Modules:
  0.0 30.0 jit_solution(6349294211752780317)
XLA Ops:
  0.0 1.3 %split.1 = (bf16[2,128,128]{2,1,0:T(8,128)(2,1)S(1)}, bf16[2,128,128]{2,1,0:T(8,128)(2,1)S(1)}, bf16[2,128,128]{2,1,0:T(8,128)(2,1)S(1)}, bf16[2,128,128]{2,1,0:...) custom-call(s32[5]{0:T(128)} %bitcast.22, ...), custom_call_target="tpu_custom_call" | custom-call | tf_op jit(solution)/shard_map/split/pallas_call | solution.py:233
  1.3 3.0 %collective-permute-start = (bf16[2,128,128]{2,1,0:T(8,128)(2,1)S(1)}, bf16[2,128,128]{2,1,0:T(8,128)(2,1)S(1)}, u32[]{:S(2)}, u32[]{:S(2)}) collective-permute-start(bf16[2,128,128]{2,1,0:T(8,128)(2,1)S(1)} %get-tuple-element.27), channel_id=1, source_target_pairs={{0,8},{8,0},{16,24},{24,16},{1,9},{9,1},{17,25},{25,17},{2,10},{10... | collective-permute-start | bytes 196616 | tf_op jit(solution)/shard_map/ppermute | solution.py:228
  4.3 1.5 %collective-permute-start.1 = (bf16[2,128,128]{2,1,0:T(8,128)(2,1)S(1)}, bf16[2,128,128]{2,1,0:T(8,128)(2,1)S(1)}, u32[]{:S(2)}, u32[]{:S(2)}) collective-permute-start(bf16[2,128,128]{2,1,0:T(8,128)(2,1)S(1)} %get-tuple-element.28), channel_id=1, source_target_pairs={{0,16},{8,24},{16,0},{24,8},{1,17},{9,25},{17,1},{25,9},{2,18},{10... | collective-permute-start | bytes 196616 | tf_op jit(solution)/shard_map/ppermute | solution.py:228
  5.9 1.9 %collective-permute-start.3 = (bf16[144,384]{1,0:T(8,128)(2,1)S(1)}, bf16[144,384]{1,0:T(8,128)(2,1)S(1)}, u32[]{:S(2)}, u32[]{:S(2)}) collective-permute-start(bf16[144,384]{1,0:T(8,128)(2,1)S(1)} %get-tuple-element.31), channel_id=1, source_target_pairs={{0,8},{8,0},{16,24},{24,16},{1,9},{9,1},{17,25},{25,17},{2,10},{10... | collective-permute-start | bytes 331784 | tf_op jit(solution)/shard_map/ppermute | solution.py:228
  7.8 1.5 %collective-permute-start.4 = (bf16[144,384]{1,0:T(8,128)(2,1)S(1)}, bf16[144,384]{1,0:T(8,128)(2,1)S(1)}, u32[]{:S(2)}, u32[]{:S(2)}) collective-permute-start(bf16[144,384]{1,0:T(8,128)(2,1)S(1)} %get-tuple-element.32), channel_id=1, source_target_pairs={{0,16},{8,24},{16,0},{24,8},{1,17},{9,25},{17,1},{25,9},{2,18},{10... | collective-permute-start | bytes 331784 | tf_op jit(solution)/shard_map/ppermute | solution.py:228
  9.3 0.1 reshape.21.refs_0_
  9.4 0.1 reshape.22.refs_1_
  9.5 0.6 %collective-permute-start.5 = (bf16[144,384]{1,0:T(8,128)(2,1)S(1)}, bf16[144,384]{1,0:T(8,128)(2,1)S(1)}, u32[]{:S(2)}, u32[]{:S(2)}) collective-permute-start(bf16[144,384]{1,0:T(8,128)(2,1)S(1)} %get-tuple-element.33), channel_id=1, source_target_pairs={{0,24},{8,16},{16,8},{24,0},{1,25},{9,17},{17,9},{25,1},{2,26},{10... | collective-permute-start | bytes 331784 | tf_op jit(solution)/shard_map/ppermute | solution.py:228
  10.1 1.1 %collective-permute-done.2 = bf16[2,128,128]{2,1,0:T(8,128)(2,1)S(1)} collective-permute-done((bf16[2,128,128]{2,1,0:T(8,128)(2,1)S(1)}, bf16[2,128,128]{2,1,0:T(8,128)(2,1)S(1)}, u32[]{:S(2)}, u32[]{:S(2)}) %collective-permute-start.2) | collective-permute-done | bytes 65568 | tf_op jit(solution)/shard_map/ppermute | solution.py:228
  11.2 1.6 %collective-permute-start.7 = (bf16[4,2,128,128]{3,2,1,0:T(8,128)(2,1)S(1)}, bf16[4,2,128,128]{3,2,1,0:T(8,128)(2,1)S(1)}, u32[]{:S(2)}, u32[]{:S(2)}) collective-permute-start(bf16[4,2,128,128]{3,2,1,0:T(8,128)(2,1)S(1)} %pad_maximum_fusion.own_ref.refs_3_), channel_id=1, source_target_pairs={{0,1},{1,0},{2,3},{3,2},{4,5},{5,4},{6,7},{7,6},{8,9},{9,8},{10,11... | collective-permute-start | bytes 786440 | tf_op jit(solution)/shard_map/ppermute | solution.py:51
  12.9 0.9 %collective-permute-done.4.refs_2_ = bf16[144,384]{1,0:T(8,128)(2,1)S(1)} collective-permute-done((bf16[144,384]{1,0:T(8,128)(2,1)S(1)}, bf16[144,384]{1,0:T(8,128)(2,1)S(1)}, u32[]{:S(2)}, u32[]{:S(2)}) %collective-permute-start.4) | collective-permute-done | bytes 110624 | tf_op jit(solution)/shard_map/ppermute | solution.py:228
  13.7 1.4 %collective-permute-done.5.refs_3_ = bf16[144,384]{1,0:T(8,128)(2,1)S(1)} collective-permute-done((bf16[144,384]{1,0:T(8,128)(2,1)S(1)}, bf16[144,384]{1,0:T(8,128)(2,1)S(1)}, u32[]{:S(2)}, u32[]{:S(2)}) %collective-permute-start.5) | collective-permute-done | bytes 110624 | tf_op jit(solution)/shard_map/ppermute | solution.py:228
  15.2 0.1 collective-permute-start.8
  15.3 1.6 %attend_0.1 = (f32[4,384,128]{2,1,0:T(8,128)S(1)}, f32[4,384,128]{2,1,0:T(8,128)S(1)}, f32[4,384,128]{2,1,0:T(8,128)S(1)}, f32[4,8,512]{2,1,0:T(8,128)S(1)}, f32[4,128,128]{2,1,0:T(8,128)S(1)}) custom-call(s32[32]{0:T(128)S(1)} %reshape.21.refs_0_, s32[16]{0:T(128)S(1)} %reshape.22.refs_1_, bf16[4,144,384]{2,1,0:T(8,128)(2,1)S(1)} %get-tuple-element.34.refs_2_.refs_0_, ...), custom_call_target="tpu_custom_call" | custom-call | flops 10000000000 | bytes 4000000 | tf_op jit(solution)/shard_map/attend_0/pallas_call | solution.py:298
  16.9 1.2 %attend_1.1 = (f32[4,384,128]{2,1,0:T(8,128)S(1)}, f32[4,384,128]{2,1,0:T(8,128)S(1)}, f32[4,384,128]{2,1,0:T(8,128)S(1)}) custom-call(bf16[4,144,384]{2,1,0:T(8,128)(2,1)S(1)} %get-tuple-element.34.refs_2_.refs_0_, bf16[4,2,128,128]{3,2,1,0:T(8,128)(2,1)S(1)} %collective-permute-done.8.refs_1_, f32[4,8,512]{2,1,0:T(8,128)S(1)} %get-tuple-element.35.refs_2_, ...), custom_call_target="tpu_custom_call" | custom-call | flops 1000000 | bytes 4000000 | tf_op jit(solution)/shard_map/attend_1/pallas_call | solution.py:298
  18.1 1.1 %attend_2.1 = (f32[4,384,128]{2,1,0:T(8,128)S(1)}, f32[4,384,128]{2,1,0:T(8,128)S(1)}, f32[4,384,128]{2,1,0:T(8,128)S(1)}) custom-call(bf16[4,144,384]{2,1,0:T(8,128)(2,1)S(1)} %get-tuple-element.34.refs_2_.refs_0_, bf16[4,2,128,128]{3,2,1,0:T(8,128)(2,1)S(1)} %collective-permute-done.7.refs_1_, f32[4,8,512]{2,1,0:T(8,128)S(1)} %get-tuple-element.35.refs_2_, ...), custom_call_target="tpu_custom_call" | custom-call | flops 1000000 | bytes 4000000 | tf_op jit(solution)/shard_map/attend_2/pallas_call | solution.py:298
  19.2 1.3 %attend_3.1 = bf16[4,128,384]{2,1,0:T(8,128)(2,1)S(1)} custom-call(bf16[4,144,384]{2,1,0:T(8,128)(2,1)S(1)} %get-tuple-element.34.refs_2_.refs_0_, bf16[4,2,128,128]{3,2,1,0:T(8,128)(2,1)S(1)} %collective-permute-done.6.refs_1_, f32[4,8,512]{2,1,0:T(8,128)S(1)} %get-tuple-element.35.refs_2_, f32[4,128,128]{2,1,0:T(8,128)S(1)} %get-tuple-element.36.refs_3_, ...), custom_call_target="tpu_custom_call" | custom-call | flops 1000000 | bytes 4000000 | tf_op jit(solution)/shard_map/attend_3/pallas_call | solution.py:298
  20.6 1.1 %collective-permute-start.10 = (bf16[128,384]{1,0:T(8,128)(2,1)S(1)}, bf16[128,384]{1,0:T(8,128)(2,1)S(1)}, u32[]{:S(2)}, u32[]{:S(2)}) collective-permute-start(bf16[128,384]{1,0:T(8,128)(2,1)S(1)} %get-tuple-element.48), channel_id=1, source_target_pairs={{0,16},{8,24},{16,0},{24,8},{1,17},{9,25},{17,1},{25,9},{2,18},{10... | collective-permute-start | bytes 294920 | tf_op jit(solution)/shard_map/ppermute | solution.py:228
  21.7 1.1 %collective-permute-start.11 = (bf16[128,384]{1,0:T(8,128)(2,1)S(1)}, bf16[128,384]{1,0:T(8,128)(2,1)S(1)}, u32[]{:S(2)}, u32[]{:S(2)}) collective-permute-start(bf16[128,384]{1,0:T(8,128)(2,1)S(1)} %get-tuple-element.47), channel_id=1, source_target_pairs={{0,24},{8,16},{16,8},{24,0},{1,25},{9,17},{17,9},{25,1},{2,26},{10... | collective-permute-start | bytes 294920 | tf_op jit(solution)/shard_map/ppermute | solution.py:228
  22.7 1.4 %collective-permute-start.9 = (bf16[128,384]{1,0:T(8,128)(2,1)S(1)}, bf16[128,384]{1,0:T(8,128)(2,1)S(1)}, u32[]{:S(2)}, u32[]{:S(2)}) collective-permute-start(bf16[128,384]{1,0:T(8,128)(2,1)S(1)} %get-tuple-element.49), channel_id=1, source_target_pairs={{0,8},{8,0},{16,24},{24,16},{1,9},{9,1},{17,25},{25,17},{2,10},{10... | collective-permute-start | bytes 294920 | tf_op jit(solution)/shard_map/ppermute | solution.py:228
  24.1 3.5 %collective-permute-done.10.refs_2_ = bf16[128,384]{1,0:T(8,128)(2,1)S(1)} collective-permute-done((bf16[128,384]{1,0:T(8,128)(2,1)S(1)}, bf16[128,384]{1,0:T(8,128)(2,1)S(1)}, u32[]{:S(2)}, u32[]{:S(2)}) %collective-permute-start.10) | collective-permute-done | bytes 98336 | tf_op jit(solution)/shard_map/ppermute | solution.py:228
  27.6 0.6 %collective-permute-done.11.refs_3_ = bf16[128,384]{1,0:T(8,128)(2,1)S(1)} collective-permute-done((bf16[128,384]{1,0:T(8,128)(2,1)S(1)}, bf16[128,384]{1,0:T(8,128)(2,1)S(1)}, u32[]{:S(2)}, u32[]{:S(2)}) %collective-permute-start.11) | collective-permute-done | bytes 98336 | tf_op jit(solution)/shard_map/ppermute | solution.py:228
  28.2 0.9 %collective-permute-done.9.refs_1_ = bf16[128,384]{1,0:T(8,128)(2,1)S(1)} collective-permute-done((bf16[128,384]{1,0:T(8,128)(2,1)S(1)}, bf16[128,384]{1,0:T(8,128)(2,1)S(1)}, u32[]{:S(2)}, u32[]{:S(2)}) %collective-permute-start.9) | collective-permute-done | bytes 98336 | tf_op jit(solution)/shard_map/ppermute | solution.py:228
  29.2 0.8 %join.1 = bf16[128,1536]{1,0:T(8,128)(2,1)} custom-call(bf16[128,384]{1,0:T(8,128)(2,1)S(1)} %get-tuple-element.50.refs_0_, bf16[128,384]{1,0:T(8,128)(2,1)S(1)} %collective-permute-done.9.refs_1_, bf16[128,384]{1,0:T(8,128)(2,1)S(1)} %collective-permute-done.10.refs_2_, bf16[128,384]{1,0:T(8,128)(2,1)S(1)} %collective-permute-done.11.refs_3_), custom_call_target="tpu_custom_call" | custom-call | tf_op jit(solution)/shard_map/join/pallas_call | solution.py:317
  (15 shorter events, 0.2 us)
Async XLA Ops:
  1.3 8.0 %copy-start = (s32[4,2,4]{2,1,0:T(2,128)S(1)}, s32[4,2,4]{2,1,0:T(2,128)}, u32[]{:S(2)}) copy-start(s32[4,2,4]{2,1,0:T(2,128)} %param.8) | copy-start | bytes 388
  1.3 8.2 %collective-permute-start = (bf16[2,128,128]{2,1,0:T(8,128)(2,1)S(1)}, bf16[2,128,128]{2,1,0:T(8,128)(2,1)S(1)}, u32[]{:S(2)}, u32[]{:S(2)}) collective-permute-start(bf16[2,128,128]{2,1,0:T(8,128)(2,1)S(1)} %get-tuple-element.27), channel_id=1, source_target_pairs={{0,8},{8,0},{16,24},{24,16},{1,9},{9,1},{17,25},{25,17},{2,10},{10... | collective-permute-start | bytes 196616 | tf_op jit(solution)/shard_map/ppermute | solution.py:228
  4.3 5.8 %collective-permute-start.1 = (bf16[2,128,128]{2,1,0:T(8,128)(2,1)S(1)}, bf16[2,128,128]{2,1,0:T(8,128)(2,1)S(1)}, u32[]{:S(2)}, u32[]{:S(2)}) collective-permute-start(bf16[2,128,128]{2,1,0:T(8,128)(2,1)S(1)} %get-tuple-element.28), channel_id=1, source_target_pairs={{0,16},{8,24},{16,0},{24,8},{1,17},{9,25},{17,1},{25,9},{2,18},{10... | collective-permute-start | bytes 196616 | tf_op jit(solution)/shard_map/ppermute | solution.py:228
  5.8 5.4 %collective-permute-start.2 = (bf16[2,128,128]{2,1,0:T(8,128)(2,1)S(1)}, bf16[2,128,128]{2,1,0:T(8,128)(2,1)S(1)}, u32[]{:S(2)}, u32[]{:S(2)}) collective-permute-start(bf16[2,128,128]{2,1,0:T(8,128)(2,1)S(1)} %get-tuple-element.29), channel_id=1, source_target_pairs={{0,24},{8,16},{16,8},{24,0},{1,25},{9,17},{17,9},{25,1},{2,26},{10... | collective-permute-start | bytes 196616 | tf_op jit(solution)/shard_map/ppermute | solution.py:228
  5.9 7.0 %collective-permute-start.3 = (bf16[144,384]{1,0:T(8,128)(2,1)S(1)}, bf16[144,384]{1,0:T(8,128)(2,1)S(1)}, u32[]{:S(2)}, u32[]{:S(2)}) collective-permute-start(bf16[144,384]{1,0:T(8,128)(2,1)S(1)} %get-tuple-element.31), channel_id=1, source_target_pairs={{0,8},{8,0},{16,24},{24,16},{1,9},{9,1},{17,25},{25,17},{2,10},{10... | collective-permute-start | bytes 331784 | tf_op jit(solution)/shard_map/ppermute | solution.py:228
  7.8 1.6 %copy-start.1 = (s32[4,4]{1,0:T(4,128)S(1)}, s32[4,4]{1,0:T(4,128)}, u32[]{:S(2)}) copy-start(s32[4,4]{1,0:T(4,128)} %param.9) | copy-start | bytes 196
  7.8 5.9 %collective-permute-start.4 = (bf16[144,384]{1,0:T(8,128)(2,1)S(1)}, bf16[144,384]{1,0:T(8,128)(2,1)S(1)}, u32[]{:S(2)}, u32[]{:S(2)}) collective-permute-start(bf16[144,384]{1,0:T(8,128)(2,1)S(1)} %get-tuple-element.32), channel_id=1, source_target_pairs={{0,16},{8,24},{16,0},{24,8},{1,17},{9,25},{17,1},{25,9},{2,18},{10... | collective-permute-start | bytes 331784 | tf_op jit(solution)/shard_map/ppermute | solution.py:228
  9.5 5.7 %collective-permute-start.5 = (bf16[144,384]{1,0:T(8,128)(2,1)S(1)}, bf16[144,384]{1,0:T(8,128)(2,1)S(1)}, u32[]{:S(2)}, u32[]{:S(2)}) collective-permute-start(bf16[144,384]{1,0:T(8,128)(2,1)S(1)} %get-tuple-element.33), channel_id=1, source_target_pairs={{0,24},{8,16},{16,8},{24,0},{1,25},{9,17},{17,9},{25,1},{2,26},{10... | collective-permute-start | bytes 331784 | tf_op jit(solution)/shard_map/ppermute | solution.py:228
  11.2 6.8 %collective-permute-start.7 = (bf16[4,2,128,128]{3,2,1,0:T(8,128)(2,1)S(1)}, bf16[4,2,128,128]{3,2,1,0:T(8,128)(2,1)S(1)}, u32[]{:S(2)}, u32[]{:S(2)}) collective-permute-start(bf16[4,2,128,128]{3,2,1,0:T(8,128)(2,1)S(1)} %pad_maximum_fusion.own_ref.refs_3_), channel_id=1, source_target_pairs={{0,1},{1,0},{2,3},{3,2},{4,5},{5,4},{6,7},{7,6},{8,9},{9,8},{10,11... | collective-permute-start | bytes 786440 | tf_op jit(solution)/shard_map/ppermute | solution.py:51
  12.9 6.3 %collective-permute-start.6 = (bf16[4,2,128,128]{3,2,1,0:T(8,128)(2,1)S(1)}, bf16[4,2,128,128]{3,2,1,0:T(8,128)(2,1)S(1)}, u32[]{:S(2)}, u32[]{:S(2)}) collective-permute-start(bf16[4,2,128,128]{3,2,1,0:T(8,128)(2,1)S(1)} %pad_maximum_fusion.own_ref.refs_3_), channel_id=1, source_target_pairs={{0,4},{1,2},{2,1},{3,7},{4,0},{5,6},{6,5},{7,3},{8,12},{9,10},{10,... | collective-permute-start | bytes 786440 | tf_op jit(solution)/shard_map/ppermute | solution.py:51
  15.2 1.7 %collective-permute-start.8 = (bf16[4,2,128,128]{3,2,1,0:T(8,128)(2,1)S(1)}, bf16[4,2,128,128]{3,2,1,0:T(8,128)(2,1)S(1)}, u32[]{:S(2)}, u32[]{:S(2)}) collective-permute-start(bf16[4,2,128,128]{3,2,1,0:T(8,128)(2,1)S(1)} %get-tuple-element.37), channel_id=1, source_target_pairs={{0,4},{1,5},{2,6},{3,7},{4,0},{5,1},{6,2},{7,3},{8,12},{9,13},{10,... | collective-permute-start | bytes 786440 | tf_op jit(solution)/shard_map/ppermute | solution.py:51
  20.6 7.0 %collective-permute-start.10 = (bf16[128,384]{1,0:T(8,128)(2,1)S(1)}, bf16[128,384]{1,0:T(8,128)(2,1)S(1)}, u32[]{:S(2)}, u32[]{:S(2)}) collective-permute-start(bf16[128,384]{1,0:T(8,128)(2,1)S(1)} %get-tuple-element.48), channel_id=1, source_target_pairs={{0,16},{8,24},{16,0},{24,8},{1,17},{9,25},{17,1},{25,9},{2,18},{10... | collective-permute-start | bytes 294920 | tf_op jit(solution)/shard_map/ppermute | solution.py:228
  21.7 6.6 %collective-permute-start.11 = (bf16[128,384]{1,0:T(8,128)(2,1)S(1)}, bf16[128,384]{1,0:T(8,128)(2,1)S(1)}, u32[]{:S(2)}, u32[]{:S(2)}) collective-permute-start(bf16[128,384]{1,0:T(8,128)(2,1)S(1)} %get-tuple-element.47), channel_id=1, source_target_pairs={{0,24},{8,16},{16,8},{24,0},{1,25},{9,17},{17,9},{25,1},{2,26},{10... | collective-permute-start | bytes 294920 | tf_op jit(solution)/shard_map/ppermute | solution.py:228
  22.7 6.4 %collective-permute-start.9 = (bf16[128,384]{1,0:T(8,128)(2,1)S(1)}, bf16[128,384]{1,0:T(8,128)(2,1)S(1)}, u32[]{:S(2)}, u32[]{:S(2)}) collective-permute-start(bf16[128,384]{1,0:T(8,128)(2,1)S(1)} %get-tuple-element.49), channel_id=1, source_target_pairs={{0,8},{8,0},{16,24},{24,16},{1,9},{9,1},{17,25},{25,17},{2,10},{10... | collective-permute-start | bytes 294920 | tf_op jit(solution)/shard_map/ppermute | solution.py:228

commit v5 on v4

v5 whole, which is shorter than its diff:
```python
import functools
import math

import jax
import jax.numpy as jnp
from jax import lax
from jax.experimental import pallas as pl
from jax.experimental.pallas import tpu as pltpu
from jax.sharding import PartitionSpec as P

HEAD_SIZE = 128
NEIGH = 5
EXTRA = 16
OWN_FLOPS = 10_000_000_000
LATER_FLOPS = 1_000_000
CUTS = (1, 2)
SMALL = pl.CostEstimate(flops=1000, bytes_accessed=1000, transcendentals=0)
DEAD = -1e30
VMEM_LIMIT = 40 * 1024 * 1024


def vmem():
    return pl.BlockSpec(memory_space=pltpu.VMEM)


def smem():
    return pl.BlockSpec(memory_space=pltpu.SMEM)


def pairings(count):
    found = []
    for first in (0, 1):
        pairs = [(i, i + 1) for i in range(first, count - 1, 2)]
        if pairs:
            found.append(pairs)
    return found


def swap(block, sizes, dim, pairs):
    rows, cols = sizes
    paired = {i: j for a, b in pairs for i, j in ((a, b), (b, a))}
    moves = []
    for row in range(rows):
        for col in range(cols):
            place = [row, col]
            if place[dim] in paired:
                place[dim] = paired[place[dim]]
            elif dim == 1 and rows % 2 == 0:
                place[0] = row ^ 1
            else:
                continue
            moves.append((row * cols + col, place[0] * cols + place[1]))
    return lax.ppermute(block, ("ty", "tx"), moves)


def partner(place, count, first):
    low = lax.rem(place + first, 2) == 0
    step = jnp.where(low, 1, -1)
    other = place + step
    return jnp.where((other >= 0) & (other < count), step, 0)


def split(spans, sizes, ways, *refs):
    (pattern_hbm, counts_hbm, mask_hbm, kv_hbm, q_hbm), refs = refs[:5], refs[5:]
    kv_refs, q_refs, refs = refs[:spans], refs[spans : 2 * spans], refs[2 * spans :]
    bias_ref, keep_ref, pattern_ref, counts_ref, mask_ref, kv_ref, q_ref, sems = refs
    me = lax.axis_index("span")
    at = [lax.axis_index(axis) for axis in ("ty", "tx")]
    kv_width = kv_hbm.shape[1] // 2
    rows = q_hbm.shape[0]
    width = q_hbm.shape[1] // spans
    copies = [
        pltpu.make_async_copy(source, target, sems.at[i])
        for i, (source, target) in enumerate(
            (
                (pattern_hbm, pattern_ref),
                (counts_hbm, counts_ref),
                (mask_hbm, mask_ref),
                (kv_hbm, kv_ref),
                (q_hbm, q_ref),
            )
        )
    ]
    for copy in copies:
        copy.start()
    for copy in copies[:3]:
        copy.wait()
    row_ids = lax.broadcasted_iota(jnp.int32, (EXTRA, width), 0)
    extra = jnp.zeros((EXTRA, width), jnp.float32)
    for o in range(NEIGH):
        extra = jnp.where(row_ids == o, pattern_ref[o].astype(jnp.float32), extra)
    extra = extra.astype(jnp.bfloat16)
    for k in range(spans):
        q_refs[k][rows:] = extra

    lanes = lax.broadcasted_iota(jnp.int32, (1, rows), 1)
    row_ids = lax.broadcasted_iota(jnp.int32, (rows, HEAD_SIZE), 0)

    def count(span, step_row, step_col):
        return counts_ref[span, at[0] + step_row, at[1] + step_col]

    for other in range(spans):
        keep_ref[other] = jnp.where(row_ids < count(other, 0, 0), 1.0, 0.0)
        for t, way in enumerate(ways):
            if way is None:
                near = count(other, 0, 0)
            else:
                step = partner(at[way[0]], sizes[way[0]], way[1])
                near = count(other, *((step, 0) if way[0] == 0 else (0, step)))
                near = jnp.where(step == 0, 0, near)
            for span in range(other, spans):
                seen = jnp.where(mask_ref[span, other] > 0, near, 0)
                bias_ref[span, t : t + 1, other * rows : (other + 1) * rows] = jnp.where(
                    lanes < seen, 0.0, DEAD
                )

    copies[3].wait()
    for k in range(spans):
        for part in range(2):
            start = pl.multiple_of(part * kv_width + (me ^ k) * HEAD_SIZE, HEAD_SIZE)
            kv_refs[k][part] = kv_ref[:, pl.ds(start, HEAD_SIZE)]
    copies[4].wait()
    for k in range(spans):
        q_refs[k][:rows] = q_ref[:, pl.ds(pl.multiple_of((me ^ k) * width, HEAD_SIZE), width)]


def attend(spans, sizes, ways, numbers, *refs):
    first, last = numbers[0] == 0, numbers[-1] == len(ways) - 1
    q_ref, refs = refs[0], refs[1:]
    tile_refs, refs = refs[: len(numbers)], refs[len(numbers) :]
    (bias_ref, keep_ref), refs = refs[:2], refs[2:]
    if not first:
        (top_in, sum_in, acc_in), refs = refs[:3], refs[3:]
    if last:
        (out_ref,), refs = refs[:1], refs[1:]
    else:
        (top_ref, sum_ref, acc_ref), refs = refs[:3], refs[3:]
    (score_ref,) = refs
    me = lax.axis_index("span")
    tok_rows = q_ref.shape[1] - EXTRA
    groups = q_ref.shape[2] // HEAD_SIZE
    factor = HEAD_SIZE ** (-0.5) * math.log2(math.e)

    def pattern_rows(n):
        if ways[n] is None:
            return 0, 0
        base = 1 + 2 * ways[n][0]
        return base, base + 1

    steps = [
        None
        if ways[n] is None
        else partner(lax.axis_index(("ty", "tx")[ways[n][0]]), sizes[ways[n][0]], ways[n][1])
        for n in numbers
    ]

    def bias_of(span):
        extra = q_ref[me ^ span, tok_rows:, :HEAD_SIZE].astype(jnp.float32)
        parts = []
        for n, step in zip(numbers, steps, strict=True):
            low, high = pattern_rows(n)
            chosen = extra[low : low + 1]
            if step is not None:
                chosen = jnp.where(step > 0, extra[high : high + 1], chosen)
            closed = jnp.where(chosen > 0, 0.0, DEAD)
            for other in range(span + 1):
                lanes = slice(other * tok_rows, (other + 1) * tok_rows)
                parts.append(bias_ref[span, n : n + 1, lanes] + closed)
        return jnp.concatenate(parts, axis=1)

    def gathered(span, part):
        return jnp.concatenate([t[me ^ o, part] for t in tile_refs for o in range(span + 1)], axis=0)

    def score(span):
        query = jnp.concatenate(
            [q_ref[me ^ span, :tok_rows, g * HEAD_SIZE : (g + 1) * HEAD_SIZE] for g in range(groups)],
            axis=0,
        )
        keys = gathered(span, 0)
        score_ref[span, :, : keys.shape[0]] = lax.dot_general(
            query, keys, (((1,), (1,)), ((), ())), preferred_element_type=jnp.float32
        )

    def weigh(span):
        values = gathered(span, 1)
        bias = bias_of(span)
        blocks = [slice(b, b + HEAD_SIZE) for b in range(0, values.shape[0], HEAD_SIZE)]
        for g in range(groups):
            rows = slice(g * tok_rows, (g + 1) * tok_rows)
            shape = (tok_rows, HEAD_SIZE)
            before = jnp.full(shape, DEAD, jnp.float32) if first else top_in[span, rows]
            top = before
            for lanes in blocks:
                top = jnp.maximum(top, score_ref[span, rows, lanes] + bias[:, lanes])
            top = jnp.broadcast_to(jnp.max(top, axis=1, keepdims=True), shape)
            total, weights = jnp.zeros(shape, jnp.float32), []
            for lanes in blocks:
                weight = jnp.exp2((score_ref[span, rows, lanes] + bias[:, lanes] - top) * factor)
                total = total + weight
                weights.append(weight.astype(jnp.bfloat16))
            result = jnp.dot(
                jnp.concatenate(weights, axis=1), values, preferred_element_type=jnp.float32
            )
            if not first:
                fade = jnp.exp2((before - top) * factor)
                total = total + sum_in[span, rows] * fade
                result = result + acc_in[span, rows] * fade
            if not last:
                top_ref[span, rows], sum_ref[span, rows], acc_ref[span, rows] = top, total, result
                continue
            share = 1.0 / jnp.sum(total, axis=1, keepdims=True)
            result = result * jnp.where(top > 0.5 * DEAD, share, jnp.nan)
            out_ref[me ^ span, :, g * HEAD_SIZE : (g + 1) * HEAD_SIZE] = jnp.where(
                keep_ref[span] > 0, result, 0.0
            ).astype(jnp.bfloat16)

    score(0)
    for span in range(spans):
        if span + 1 < spans:
            score(span + 1)
        weigh(span)


def collect(spans, own_ref, *refs):
    q_refs, (q_all_ref, copy_ref) = refs[:spans], refs[spans:]
    for k in range(spans):
        q_all_ref[k] = q_refs[k][...]
    copy_ref[...] = own_ref[...]


def join(places, *refs):
    me = lax.axis_index("span")
    out_ref = refs[-1]
    for k, ref in zip(places, refs, strict=False):
        width = ref.shape[1]
        start = pl.multiple_of((me ^ k) * width, HEAD_SIZE)
        out_ref[:, pl.ds(start, width)] = ref[...]


def shards(queries, key_value, pattern, counts, span_mask):
    spans, ty_count, tx_count = (lax.axis_size(a) for a in ("span", "ty", "tx"))
    tok_rows = queries.shape[3]
    kv_heads = key_value.shape[4] // (2 * HEAD_SIZE)
    assert kv_heads == spans and spans & (spans - 1) == 0
    width = queries.shape[4] // spans
    groups = width // HEAD_SIZE
    bf16 = jnp.bfloat16
    params = pltpu.CompilerParams(vmem_limit_bytes=VMEM_LIMIT)

    def exchange(block, k):
        return lax.ppermute(block, "span", [(i, i ^ k) for i in range(spans)])

    sizes = (ty_count, tx_count)
    order = sorted(range(1, spans), key=lambda k: -bin(k).count("1"))

    swaps = [
        (dim, first, pairs) for dim in (0, 1) for first, pairs in enumerate(pairings(sizes[dim]))
    ]
    ways = (None, *((dim, first) for dim, first, _ in swaps))
    piece = jax.ShapeDtypeStruct((2, tok_rows, HEAD_SIZE), bf16)
    pieces = pl.pallas_call(
        functools.partial(split, spans, sizes, ways),
        out_shape=[piece] * spans
        + [jax.ShapeDtypeStruct((tok_rows + EXTRA, width), bf16)] * spans
        + [
            jax.ShapeDtypeStruct((spans, 8, spans * tok_rows), jnp.float32),
            jax.ShapeDtypeStruct((spans, tok_rows, HEAD_SIZE), jnp.float32),
        ],
        in_specs=[pl.BlockSpec(memory_space=pltpu.HBM)] * 5,
        out_specs=[vmem()] * (2 * spans + 2),
        scratch_shapes=[
            pltpu.SMEM((NEIGH,), jnp.int32),
            pltpu.SMEM(counts.shape, jnp.int32),
            pltpu.SMEM(span_mask.shape, jnp.int32),
            pltpu.VMEM((tok_rows, 2 * kv_heads * HEAD_SIZE), bf16),
            pltpu.VMEM((tok_rows, spans * width), bf16),
            pltpu.SemaphoreType.DMA((5,)),
        ],
        compiler_params=params,
        name="split",
    )(
        *(
            pltpu.with_memory_space_constraint(x, pltpu.HBM)
            for x in (
                pattern.reshape(NEIGH),
                counts,
                span_mask,
                key_value.reshape(tok_rows, -1),
                queries.reshape(tok_rows, -1),
            )
        )
    )
    kv_pieces, q_pieces, masks = pieces[:spans], pieces[spans : 2 * spans], pieces[2 * spans :]

    column = [kv_pieces[0]] + [None] * (spans - 1)
    for k in order:
        column[k] = exchange(kv_pieces[k], k)
    own = jnp.stack(column)
    q_here = [q_pieces[0]] + [None] * (spans - 1)
    for k in order:
        q_here[k] = exchange(q_pieces[k], k)

    sizes = (ty_count, tx_count)
    rows = groups * tok_rows
    q_all, own_copy = pl.pallas_call(
        functools.partial(collect, spans),
        out_shape=[
            jax.ShapeDtypeStruct((spans, *q_here[0].shape), bf16),
            jax.ShapeDtypeStruct(own.shape, bf16),
        ],
        in_specs=[vmem()] * (1 + spans),
        out_specs=[vmem()] * 2,
        compiler_params=params,
        name="collect",
    )(own, *q_here)

    tiles = [own] + [swap(own if dim else own_copy, sizes, dim, pairs) for dim, _, pairs in swaps]
    kept = jax.ShapeDtypeStruct((spans, rows, HEAD_SIZE), jnp.float32)
    result = jax.ShapeDtypeStruct((spans, tok_rows, width), bf16)
    state = ()
    cut = [0] + [n for n in CUTS if n < len(tiles)] + [len(tiles)]
    for start, stop in zip(cut, cut[1:], strict=False):
        numbers = tuple(range(start, stop))
        first, last = start == 0, stop == len(tiles)
        outs = [result] if last else [kept] * 3
        given = (q_all, *tiles[start:stop], *masks, *state)
        state = pl.pallas_call(
            functools.partial(attend, spans, sizes, ways, numbers),
            out_shape=outs,
            in_specs=[vmem()] * len(given),
            out_specs=[vmem()] * len(outs),
            scratch_shapes=[pltpu.VMEM((spans, rows, spans * len(numbers) * tok_rows), jnp.float32)],
            compiler_params=params,
            cost_estimate=pl.CostEstimate(
                flops=OWN_FLOPS if first else LATER_FLOPS, bytes_accessed=4_000_000, transcendentals=0
            ),
            name=f"attend_{start}",
        )(*given)
    outs = state[0]

    home = [outs[0]] + [None] * (spans - 1)
    places = [0, *range(1, spans - 2), *range(spans - 2, spans)[::-1]] if spans > 2 else list(range(spans))
    for k in order:
        home[k] = exchange(outs[k], k)
    attended = pl.pallas_call(
        functools.partial(join, places),
        out_shape=jax.ShapeDtypeStruct((tok_rows, spans * width), bf16),
        in_specs=[vmem()] * spans,
        out_specs=vmem(),
        compiler_params=params,
        name="join",
    )(*(home[k] for k in places))
    return attended.reshape(1, 1, 1, tok_rows, -1)


def solution(mesh):
    return jax.shard_map(
        shards,
        mesh=mesh,
        in_specs=(
            P("span", "ty", "tx", None, None),
            P("span", "ty", "tx", None, None),
            P("span", "ty", "tx", None),
            P(),
            P(),
        ),
        out_specs=P("span", "ty", "tx", None, None),
        check_vma=False,
    )
```

time: 30.1 us -> 28.2 us (0.937)
  Pallas kernels: 7.33 us -> 5.99 us
  waiting for transfers between devices: 8.44 us -> 8.04 us
    pallas_call x6 -> x5, Pallas kernels: 7.28 us -> 5.94 us  [the longest x3 3.98 us: shards(): pl.pallas_call(functools.partial(attend, spans, sizes, ways, numbers), ou...]
    ppermute x9, waiting for transfers between devices: 8.43 us -> 7.53 us  [exchange(): return lax.ppermute(block, 'span', [(i, i ^ k) for i in range(spans)])]
    ppermute x3, waiting for transfers between devices: 0.01 us -> 0.52 us  [swap(): return lax.ppermute(block, ('ty', 'tx'), moves)]
  transfers between devices with their start and end apart: 12 -> 12, of which waited for: 6 -> 6; matrix products, arithmetic and copies ran while one was open for 1% -> 0% of each run, Pallas kernels for 13% -> 8%
where the time goes in v5:
time: 28.2 us; the launch traced here: 28.1 us
  starting transfers between devices  13.9 us (49%)
  waiting for transfers between devices  8.04 us (29%)
  Pallas kernels  5.99 us (21%)
    ppermute x9, starting transfers between devices, exchange(): return lax.ppermute(block, 'span', [(i, i ^ k) for i in range(spans)])  12.2 us
    ppermute x9, waiting for transfers between devices, exchange(): return lax.ppermute(block, 'span', [(i, i ^ k) for i in range(spans)])  7.53 us
    pallas_call x3, Pallas kernels, shards(): pl.pallas_call(functools.partial(attend, spans, sizes, ways, numbers), ou...  3.98 us
    ppermute x3, starting transfers between devices, swap(): return lax.ppermute(block, ('ty', 'tx'), moves)  1.72 us
    pallas_call x1, Pallas kernels, shards(): pl.pallas_call(functools.partial(split, spans, sizes, ways), out_shape=[p...  1.16 us
    pallas_call x1, Pallas kernels, shards(): pl.pallas_call(functools.partial(join, places), out_shape=jax.ShapeDtypeS...  0.8 us
  transfers between devices with their start and end apart: 12, of which 6 were waited for; matrix products, arithmetic and copies ran while one was open for 0% of the time, Pallas kernels for 8%

profile of v5, /device:TPU:0, one launch (start us, length us, event | category | flops | bytes accessed | tf_op | source)
XLA Modules:
  0.0 28.1 jit_solution(15777453393935757572)
XLA Ops:
  0.0 1.2 %split.1 = (bf16[2,128,128]{2,1,0:T(8,128)(2,1)S(1)}, bf16[2,128,128]{2,1,0:T(8,128)(2,1)S(1)}, bf16[2,128,128]{2,1,0:T(8,128)(2,1)S(1)}, bf16[2,128,128]{2,1,0:...) custom-call(s32[5]{0:T(128)} %bitcast.22, ...), custom_call_target="tpu_custom_call" | custom-call | tf_op jit(solution)/shard_map/split/pallas_call | solution.py:261
  1.2 3.0 %collective-permute-start = (bf16[2,128,128]{2,1,0:T(8,128)(2,1)S(1)}, bf16[2,128,128]{2,1,0:T(8,128)(2,1)S(1)}, u32[]{:S(2)}, u32[]{:S(2)}) collective-permute-start(bf16[2,128,128]{2,1,0:T(8,128)(2,1)S(1)} %get-tuple-element.24), channel_id=1, source_target_pairs={{0,8},{8,0},{16,24},{24,16},{1,9},{9,1},{17,25},{25,17},{2,10},{10... | collective-permute-start | bytes 196616 | tf_op jit(solution)/shard_map/ppermute | solution.py:251
  4.2 1.5 %collective-permute-start.1 = (bf16[2,128,128]{2,1,0:T(8,128)(2,1)S(1)}, bf16[2,128,128]{2,1,0:T(8,128)(2,1)S(1)}, u32[]{:S(2)}, u32[]{:S(2)}) collective-permute-start(bf16[2,128,128]{2,1,0:T(8,128)(2,1)S(1)} %get-tuple-element.25), channel_id=1, source_target_pairs={{0,16},{8,24},{16,0},{24,8},{1,17},{9,25},{17,1},{25,9},{2,18},{10... | collective-permute-start | bytes 196616 | tf_op jit(solution)/shard_map/ppermute | solution.py:251
  5.7 0.0 collective-permute-start.2
  5.7 1.9 %collective-permute-start.3 = (bf16[144,384]{1,0:T(8,128)(2,1)S(1)}, bf16[144,384]{1,0:T(8,128)(2,1)S(1)}, u32[]{:S(2)}, u32[]{:S(2)}) collective-permute-start(bf16[144,384]{1,0:T(8,128)(2,1)S(1)} %get-tuple-element.28), channel_id=1, source_target_pairs={{0,8},{8,0},{16,24},{24,16},{1,9},{9,1},{17,25},{25,17},{2,10},{10... | collective-permute-start | bytes 331784 | tf_op jit(solution)/shard_map/ppermute | solution.py:251
  7.7 1.5 %collective-permute-start.4 = (bf16[144,384]{1,0:T(8,128)(2,1)S(1)}, bf16[144,384]{1,0:T(8,128)(2,1)S(1)}, u32[]{:S(2)}, u32[]{:S(2)}) collective-permute-start(bf16[144,384]{1,0:T(8,128)(2,1)S(1)} %get-tuple-element.29), channel_id=1, source_target_pairs={{0,16},{8,24},{16,0},{24,8},{1,17},{9,25},{17,1},{25,9},{2,18},{10... | collective-permute-start | bytes 331784 | tf_op jit(solution)/shard_map/ppermute | solution.py:251
  9.2 0.6 %collective-permute-start.5 = (bf16[144,384]{1,0:T(8,128)(2,1)S(1)}, bf16[144,384]{1,0:T(8,128)(2,1)S(1)}, u32[]{:S(2)}, u32[]{:S(2)}) collective-permute-start(bf16[144,384]{1,0:T(8,128)(2,1)S(1)} %get-tuple-element.30), channel_id=1, source_target_pairs={{0,24},{8,16},{16,8},{24,0},{1,25},{9,17},{17,9},{25,1},{2,26},{10... | collective-permute-start | bytes 331784 | tf_op jit(solution)/shard_map/ppermute | solution.py:251
  9.8 0.0 collective-permute-done.1
  9.8 1.3 %collective-permute-done.2 = bf16[2,128,128]{2,1,0:T(8,128)(2,1)S(1)} collective-permute-done((bf16[2,128,128]{2,1,0:T(8,128)(2,1)S(1)}, bf16[2,128,128]{2,1,0:T(8,128)(2,1)S(1)}, u32[]{:S(2)}, u32[]{:S(2)}) %collective-permute-start.2) | collective-permute-done | bytes 65568 | tf_op jit(solution)/shard_map/ppermute | solution.py:251
  11.1 1.6 %collective-permute-start.6 = (bf16[4,2,128,128]{3,2,1,0:T(8,128)(2,1)S(1)}, bf16[4,2,128,128]{3,2,1,0:T(8,128)(2,1)S(1)}, u32[]{:S(2)}, u32[]{:S(2)}) collective-permute-start(bf16[4,2,128,128]{3,2,1,0:T(8,128)(2,1)S(1)} %pad_maximum_fusion.own_ref.refs_1_), channel_id=1, source_target_pairs={{0,1},{1,0},{2,3},{3,2},{4,5},{5,4},{6,7},{7,6},{8,9},{9,8},{10,11... | collective-permute-start | bytes 786440 | tf_op jit(solution)/shard_map/ppermute | solution.py:53
  12.7 0.8 %collective-permute-done.4.refs_2_ = bf16[144,384]{1,0:T(8,128)(2,1)S(1)} collective-permute-done((bf16[144,384]{1,0:T(8,128)(2,1)S(1)}, bf16[144,384]{1,0:T(8,128)(2,1)S(1)}, u32[]{:S(2)}, u32[]{:S(2)}) %collective-permute-start.4) | collective-permute-done | bytes 110624 | tf_op jit(solution)/shard_map/ppermute | solution.py:251
  13.5 1.3 %collective-permute-done.5.refs_3_ = bf16[144,384]{1,0:T(8,128)(2,1)S(1)} collective-permute-done((bf16[144,384]{1,0:T(8,128)(2,1)S(1)}, bf16[144,384]{1,0:T(8,128)(2,1)S(1)}, u32[]{:S(2)}, u32[]{:S(2)}) %collective-permute-start.5) | collective-permute-done | bytes 110624 | tf_op jit(solution)/shard_map/ppermute | solution.py:251
  14.8 0.1 collect.1
  14.9 0.1 collective-permute-start.8
  15.0 1.0 %attend_0.1 = (f32[4,384,128]{2,1,0:T(8,128)S(1)}, f32[4,384,128]{2,1,0:T(8,128)S(1)}, f32[4,384,128]{2,1,0:T(8,128)S(1)}) custom-call(bf16[4,144,384]{2,1,0:T(8,128)(2,1)S(1)} %get-tuple-element.31.refs_0_, bf16[4,2,128,128]{3,2,1,0:T(8,128)(2,1)S(1)} %pad_maximum_fusion.own_ref.refs_1_, f32[4,8,512]{2,1,0:T(8,128)S(1)} %get-tuple-element.32.refs_2_.refs_3_, ...), custom_call_target="tpu_custom_call" | custom-call | flops 10000000000 | bytes 4000000 | tf_op jit(solution)/shard_map/attend_0/pallas_call | solution.py:327
  16.0 0.5 %collective-permute-done.8.refs_1_ = bf16[4,2,128,128]{3,2,1,0:T(8,128)(2,1)S(1)} collective-permute-done((bf16[4,2,128,128]{3,2,1,0:T(8,128)(2,1)S(1)}, bf16[4,2,128,128]{3,2,1,0:T(8,128)(2,1)S(1)}, u32[]{:S(2)}, u32[]{:S(2)}) %collective-permute-start.8) | collective-permute-done | bytes 262176 | tf_op jit(solution)/shard_map/ppermute | solution.py:53
  16.5 1.1 %attend_1.1 = (f32[4,384,128]{2,1,0:T(8,128)S(1)}, f32[4,384,128]{2,1,0:T(8,128)S(1)}, f32[4,384,128]{2,1,0:T(8,128)S(1)}) custom-call(bf16[4,144,384]{2,1,0:T(8,128)(2,1)S(1)} %get-tuple-element.31.refs_0_, bf16[4,2,128,128]{3,2,1,0:T(8,128)(2,1)S(1)} %collective-permute-done.8.refs_1_, f32[4,8,512]{2,1,0:T(8,128)S(1)} %get-tuple-element.32.refs_2_.refs_3_, ...), custom_call_target="tpu_custom_call" | custom-call | flops 1000000 | bytes 4000000 | tf_op jit(solution)/shard_map/attend_1/pallas_call | solution.py:327
  17.6 1.9 %attend_2.1 = bf16[4,128,384]{2,1,0:T(8,128)(2,1)S(1)} custom-call(bf16[4,144,384]{2,1,0:T(8,128)(2,1)S(1)} %get-tuple-element.31.refs_0_, bf16[4,2,128,128]{3,2,1,0:T(8,128)(2,1)S(1)} %collective-permute-done.6.refs_1_, bf16[4,2,128,128]{3,2,1,0:T(8,128)(2,1)S(1)} %collective-permute-done.7.refs_2_, f32[4,8,512]{2,1,0:T(8,128)S(1)} %get-tuple-element.32.refs_2_.refs_3_, ...), custom_call_target="tpu_custom_call" | custom-call | flops 1000000 | bytes 4000000 | tf_op jit(solution)/shard_map/attend_2/pallas_call | solution.py:327
  19.6 1.1 %collective-permute-start.10 = (bf16[128,384]{1,0:T(8,128)(2,1)S(1)}, bf16[128,384]{1,0:T(8,128)(2,1)S(1)}, u32[]{:S(2)}, u32[]{:S(2)}) collective-permute-start(bf16[128,384]{1,0:T(8,128)(2,1)S(1)} %get-tuple-element.42), channel_id=1, source_target_pairs={{0,24},{8,16},{16,8},{24,0},{1,25},{9,17},{17,9},{25,1},{2,26},{10... | collective-permute-start | bytes 294920 | tf_op jit(solution)/shard_map/ppermute | solution.py:251
  20.6 1.3 %collective-permute-start.11 = (bf16[128,384]{1,0:T(8,128)(2,1)S(1)}, bf16[128,384]{1,0:T(8,128)(2,1)S(1)}, u32[]{:S(2)}, u32[]{:S(2)}) collective-permute-start(bf16[128,384]{1,0:T(8,128)(2,1)S(1)} %get-tuple-element.41), channel_id=1, source_target_pairs={{0,16},{8,24},{16,0},{24,8},{1,17},{9,25},{17,1},{25,9},{2,18},{10... | collective-permute-start | bytes 294920 | tf_op jit(solution)/shard_map/ppermute | solution.py:251
  22.0 1.1 %collective-permute-start.9 = (bf16[128,384]{1,0:T(8,128)(2,1)S(1)}, bf16[128,384]{1,0:T(8,128)(2,1)S(1)}, u32[]{:S(2)}, u32[]{:S(2)}) collective-permute-start(bf16[128,384]{1,0:T(8,128)(2,1)S(1)} %get-tuple-element.43), channel_id=1, source_target_pairs={{0,8},{8,0},{16,24},{24,16},{1,9},{9,1},{17,25},{25,17},{2,10},{10... | collective-permute-start | bytes 294920 | tf_op jit(solution)/shard_map/ppermute | solution.py:251
  23.1 3.1 %collective-permute-done.10.refs_2_ = bf16[128,384]{1,0:T(8,128)(2,1)S(1)} collective-permute-done((bf16[128,384]{1,0:T(8,128)(2,1)S(1)}, bf16[128,384]{1,0:T(8,128)(2,1)S(1)}, u32[]{:S(2)}, u32[]{:S(2)}) %collective-permute-start.10) | collective-permute-done | bytes 98336 | tf_op jit(solution)/shard_map/ppermute | solution.py:251
  26.2 1.1 %collective-permute-done.11.refs_3_ = bf16[128,384]{1,0:T(8,128)(2,1)S(1)} collective-permute-done((bf16[128,384]{1,0:T(8,128)(2,1)S(1)}, bf16[128,384]{1,0:T(8,128)(2,1)S(1)}, u32[]{:S(2)}, u32[]{:S(2)}) %collective-permute-start.11) | collective-permute-done | bytes 98336 | tf_op jit(solution)/shard_map/ppermute | solution.py:251
  27.3 0.8 %join.1 = bf16[128,1536]{1,0:T(8,128)(2,1)} custom-call(bf16[128,384]{1,0:T(8,128)(2,1)S(1)} %get-tuple-element.44.refs_0_, bf16[128,384]{1,0:T(8,128)(2,1)S(1)} %collective-permute-done.9.refs_1_, bf16[128,384]{1,0:T(8,128)(2,1)S(1)} %collective-permute-done.10.refs_2_, bf16[128,384]{1,0:T(8,128)(2,1)S(1)} %collective-permute-done.11.refs_3_), custom_call_target="tpu_custom_call" | custom-call | tf_op jit(solution)/shard_map/join/pallas_call | solution.py:345
  (8 shorter events, 0.1 us)
Async XLA Ops:
  1.2 8.0 %collective-permute-start = (bf16[2,128,128]{2,1,0:T(8,128)(2,1)S(1)}, bf16[2,128,128]{2,1,0:T(8,128)(2,1)S(1)}, u32[]{:S(2)}, u32[]{:S(2)}) collective-permute-start(bf16[2,128,128]{2,1,0:T(8,128)(2,1)S(1)} %get-tuple-element.24), channel_id=1, source_target_pairs={{0,8},{8,0},{16,24},{24,16},{1,9},{9,1},{17,25},{25,17},{2,10},{10... | collective-permute-start | bytes 196616 | tf_op jit(solution)/shard_map/ppermute | solution.py:251
  4.2 5.6 %collective-permute-start.1 = (bf16[2,128,128]{2,1,0:T(8,128)(2,1)S(1)}, bf16[2,128,128]{2,1,0:T(8,128)(2,1)S(1)}, u32[]{:S(2)}, u32[]{:S(2)}) collective-permute-start(bf16[2,128,128]{2,1,0:T(8,128)(2,1)S(1)} %get-tuple-element.25), channel_id=1, source_target_pairs={{0,16},{8,24},{16,0},{24,8},{1,17},{9,25},{17,1},{25,9},{2,18},{10... | collective-permute-start | bytes 196616 | tf_op jit(solution)/shard_map/ppermute | solution.py:251
  5.7 5.4 %collective-permute-start.2 = (bf16[2,128,128]{2,1,0:T(8,128)(2,1)S(1)}, bf16[2,128,128]{2,1,0:T(8,128)(2,1)S(1)}, u32[]{:S(2)}, u32[]{:S(2)}) collective-permute-start(bf16[2,128,128]{2,1,0:T(8,128)(2,1)S(1)} %get-tuple-element.26), channel_id=1, source_target_pairs={{0,24},{8,16},{16,8},{24,0},{1,25},{9,17},{17,9},{25,1},{2,26},{10... | collective-permute-start | bytes 196616 | tf_op jit(solution)/shard_map/ppermute | solution.py:251
  5.7 7.0 %collective-permute-start.3 = (bf16[144,384]{1,0:T(8,128)(2,1)S(1)}, bf16[144,384]{1,0:T(8,128)(2,1)S(1)}, u32[]{:S(2)}, u32[]{:S(2)}) collective-permute-start(bf16[144,384]{1,0:T(8,128)(2,1)S(1)} %get-tuple-element.28), channel_id=1, source_target_pairs={{0,8},{8,0},{16,24},{24,16},{1,9},{9,1},{17,25},{25,17},{2,10},{10... | collective-permute-start | bytes 331784 | tf_op jit(solution)/shard_map/ppermute | solution.py:251
  7.7 5.9 %collective-permute-start.4 = (bf16[144,384]{1,0:T(8,128)(2,1)S(1)}, bf16[144,384]{1,0:T(8,128)(2,1)S(1)}, u32[]{:S(2)}, u32[]{:S(2)}) collective-permute-start(bf16[144,384]{1,0:T(8,128)(2,1)S(1)} %get-tuple-element.29), channel_id=1, source_target_pairs={{0,16},{8,24},{16,0},{24,8},{1,17},{9,25},{17,1},{25,9},{2,18},{10... | collective-permute-start | bytes 331784 | tf_op jit(solution)/shard_map/ppermute | solution.py:251
  9.2 5.6 %collective-permute-start.5 = (bf16[144,384]{1,0:T(8,128)(2,1)S(1)}, bf16[144,384]{1,0:T(8,128)(2,1)S(1)}, u32[]{:S(2)}, u32[]{:S(2)}) collective-permute-start(bf16[144,384]{1,0:T(8,128)(2,1)S(1)} %get-tuple-element.30), channel_id=1, source_target_pairs={{0,24},{8,16},{16,8},{24,0},{1,25},{9,17},{17,9},{25,1},{2,26},{10... | collective-permute-start | bytes 331784 | tf_op jit(solution)/shard_map/ppermute | solution.py:251
  11.1 6.5 %collective-permute-start.6 = (bf16[4,2,128,128]{3,2,1,0:T(8,128)(2,1)S(1)}, bf16[4,2,128,128]{3,2,1,0:T(8,128)(2,1)S(1)}, u32[]{:S(2)}, u32[]{:S(2)}) collective-permute-start(bf16[4,2,128,128]{3,2,1,0:T(8,128)(2,1)S(1)} %pad_maximum_fusion.own_ref.refs_1_), channel_id=1, source_target_pairs={{0,1},{1,0},{2,3},{3,2},{4,5},{5,4},{6,7},{7,6},{8,9},{9,8},{10,11... | collective-permute-start | bytes 786440 | tf_op jit(solution)/shard_map/ppermute | solution.py:53
  12.7 4.9 %collective-permute-start.7 = (bf16[4,2,128,128]{3,2,1,0:T(8,128)(2,1)S(1)}, bf16[4,2,128,128]{3,2,1,0:T(8,128)(2,1)S(1)}, u32[]{:S(2)}, u32[]{:S(2)}) collective-permute-start(bf16[4,2,128,128]{3,2,1,0:T(8,128)(2,1)S(1)} %pad_maximum_fusion.own_ref.refs_1_), channel_id=1, source_target_pairs={{0,4},{1,2},{2,1},{3,7},{4,0},{5,6},{6,5},{7,3},{8,12},{9,10},{10,... | collective-permute-start | bytes 786440 | tf_op jit(solution)/shard_map/ppermute | solution.py:53
  14.9 1.6 %collective-permute-start.8 = (bf16[4,2,128,128]{3,2,1,0:T(8,128)(2,1)S(1)}, bf16[4,2,128,128]{3,2,1,0:T(8,128)(2,1)S(1)}, u32[]{:S(2)}, u32[]{:S(2)}) collective-permute-start(bf16[4,2,128,128]{3,2,1,0:T(8,128)(2,1)S(1)} %get-tuple-element.34), channel_id=1, source_target_pairs={{0,4},{1,5},{2,6},{3,7},{4,0},{5,1},{6,2},{7,3},{8,12},{9,13},{10,... | collective-permute-start | bytes 786440 | tf_op jit(solution)/shard_map/ppermute | solution.py:53
  19.6 6.6 %collective-permute-start.10 = (bf16[128,384]{1,0:T(8,128)(2,1)S(1)}, bf16[128,384]{1,0:T(8,128)(2,1)S(1)}, u32[]{:S(2)}, u32[]{:S(2)}) collective-permute-start(bf16[128,384]{1,0:T(8,128)(2,1)S(1)} %get-tuple-element.42), channel_id=1, source_target_pairs={{0,24},{8,16},{16,8},{24,0},{1,25},{9,17},{17,9},{25,1},{2,26},{10... | collective-permute-start | bytes 294920 | tf_op jit(solution)/shard_map/ppermute | solution.py:251
  20.6 6.7 %collective-permute-start.11 = (bf16[128,384]{1,0:T(8,128)(2,1)S(1)}, bf16[128,384]{1,0:T(8,128)(2,1)S(1)}, u32[]{:S(2)}, u32[]{:S(2)}) collective-permute-start(bf16[128,384]{1,0:T(8,128)(2,1)S(1)} %get-tuple-element.41), channel_id=1, source_target_pairs={{0,16},{8,24},{16,0},{24,8},{1,17},{9,25},{17,1},{25,9},{2,18},{10... | collective-permute-start | bytes 294920 | tf_op jit(solution)/shard_map/ppermute | solution.py:251
  22.0 5.3 %collective-permute-start.9 = (bf16[128,384]{1,0:T(8,128)(2,1)S(1)}, bf16[128,384]{1,0:T(8,128)(2,1)S(1)}, u32[]{:S(2)}, u32[]{:S(2)}) collective-permute-start(bf16[128,384]{1,0:T(8,128)(2,1)S(1)} %get-tuple-element.43), channel_id=1, source_target_pairs={{0,8},{8,0},{16,24},{24,16},{1,9},{9,1},{17,25},{25,17},{2,10},{10... | collective-permute-start | bytes 294920 | tf_op jit(solution)/shard_map/ppermute | solution.py:251

commit v6 on v5

--- a/solution.py
+++ b/solution.py
@@ -1,4 +1,5 @@
 import functools
+import itertools
 import math
 
 import jax
@@ -58,6 +59,11 @@
     step = jnp.where(low, 1, -1)
     other = place + step
     return jnp.where((other >= 0) & (other < count), step, 0)
+
+
+def has_partner(place, sizes, way):
+    other = place + 1 if (place + way[1]) % 2 == 0 else place - 1
+    return 0 <= other < sizes[way[0]]
 
 
 def split(spans, sizes, ways, *refs):
@@ -124,10 +130,10 @@
         q_refs[k][:rows] = q_ref[:, pl.ds(pl.multiple_of((me ^ k) * width, HEAD_SIZE), width)]
 
 
-def attend(spans, sizes, ways, numbers, *refs):
+def attend(spans, sizes, ways, numbers, chosen, *refs):
     first, last = numbers[0] == 0, numbers[-1] == len(ways) - 1
     q_ref, refs = refs[0], refs[1:]
-    tile_refs, refs = refs[: len(numbers)], refs[len(numbers) :]
+    tile_refs, refs = dict(zip(numbers, refs, strict=False)), refs[len(numbers) :]
     (bias_ref, keep_ref), refs = refs[:2], refs[2:]
     if not first:
         (top_in, sum_in, acc_in), refs = refs[:3], refs[3:]
@@ -147,17 +153,18 @@
         base = 1 + 2 * ways[n][0]
         return base, base + 1
 
-    steps = [
-        None
+    steps = {
+        n: None
         if ways[n] is None
         else partner(lax.axis_index(("ty", "tx")[ways[n][0]]), sizes[ways[n][0]], ways[n][1])
         for n in numbers
-    ]
-
-    def bias_of(span):
+    }
+
+    def bias_of(span, used):
         extra = q_ref[me ^ span, tok_rows:, :HEAD_SIZE].astype(jnp.float32)
         parts = []
-        for n, step in zip(numbers, steps, strict=True):
+        for n in used:
+            step = steps[n]
             low, high = pattern_rows(n)
             chosen = extra[low : low + 1]
             if step is not None:
@@ -168,22 +175,22 @@
                 parts.append(bias_ref[span, n : n + 1, lanes] + closed)
         return jnp.concatenate(parts, axis=1)
 
-    def gathered(span, part):
-        return jnp.concatenate([t[me ^ o, part] for t in tile_refs for o in range(span + 1)], axis=0)
-
-    def score(span):
+    def gathered(span, part, used):
+        return jnp.concatenate([t[me ^ o, part] for t in map(tile_refs.get, used) for o in range(span + 1)], axis=0)
+
+    def score(span, used):
         query = jnp.concatenate(
             [q_ref[me ^ span, :tok_rows, g * HEAD_SIZE : (g + 1) * HEAD_SIZE] for g in range(groups)],
             axis=0,
         )
-        keys = gathered(span, 0)
+        keys = gathered(span, 0, used)
         score_ref[span, :, : keys.shape[0]] = lax.dot_general(
             query, keys, (((1,), (1,)), ((), ())), preferred_element_type=jnp.float32
         )
 
-    def weigh(span):
-        values = gathered(span, 1)
-        bias = bias_of(span)
+    def weigh(span, used):
+        values = gathered(span, 1, used)
+        bias = bias_of(span, used)
         blocks = [slice(b, b + HEAD_SIZE) for b in range(0, values.shape[0], HEAD_SIZE)]
         for g in range(groups):
             rows = slice(g * tok_rows, (g + 1) * tok_rows)
@@ -214,11 +221,31 @@
                 keep_ref[span] > 0, result, 0.0
             ).astype(jnp.bfloat16)
 
-    score(0)
-    for span in range(spans):
-        if span + 1 < spans:
-            score(span + 1)
-        weigh(span)
+    def run(some, used):
+        score(some[0], used)
+        for i, span in enumerate(some):
+            if i + 1 < len(some):
+                score(some[i + 1], used)
+            weigh(span, used)
+
+    members = {}
+    for place in range(spans):
+        members.setdefault(tuple(sorted(place ^ k for k in chosen)), []).append(place)
+    borders = {
+        tuple(n for n in numbers if ways[n] is None or has_partner(spot[ways[n][0]], sizes, ways[n]))
+        for spot in itertools.product(*map(range, sizes))
+    }
+    for some, places in sorted(members.items()):
+        for inside in sorted(borders):
+            tests = [] if len(places) == spans else [[me == place for place in places]]
+            if len(borders) > 1:
+                tests += [[(steps[n] != 0) == (n in inside)] for n in numbers if steps[n] is not None]
+            case = functools.partial(run, some, inside or numbers[:1])
+            if tests:
+                tests = [functools.reduce(jnp.logical_or, test) for test in tests]
+                pl.when(functools.reduce(jnp.logical_and, tests))(case)
+            else:
+                case()
 
 
 def collect(spans, own_ref, *refs):
@@ -317,26 +344,33 @@
     tiles = [own] + [swap(own if dim else own_copy, sizes, dim, pairs) for dim, _, pairs in swaps]
     kept = jax.ShapeDtypeStruct((spans, rows, HEAD_SIZE), jnp.float32)
     result = jax.ShapeDtypeStruct((spans, tok_rows, width), bf16)
+
+    def stage(start, stop, chosen, state, flops, name):
+        numbers = tuple(range(start, stop))
+        last = stop == len(tiles)
+        given = (q_all, *tiles[start:stop], *masks, *state)
+        return pl.pallas_call(
+            functools.partial(attend, spans, sizes, ways, numbers, chosen),
+            out_shape=[result] if last else [kept] * 3,
+            in_specs=[vmem()] * len(given),
+            out_specs=[vmem()] * (1 if last else 3),
+            scratch_shapes=[pltpu.VMEM((spans, rows, spans * len(numbers) * tok_rows), jnp.float32)],
+            compiler_params=params,
+            cost_estimate=pl.CostEstimate(flops=flops, bytes_accessed=4_000_000, transcendentals=0),
+            name=name,
+        )(*given)
+
     state = ()
     cut = [0] + [n for n in CUTS if n < len(tiles)] + [len(tiles)]
-    for start, stop in zip(cut, cut[1:], strict=False):
-        numbers = tuple(range(start, stop))
-        first, last = start == 0, stop == len(tiles)
-        outs = [result] if last else [kept] * 3
-        given = (q_all, *tiles[start:stop], *masks, *state)
-        state = pl.pallas_call(
-            functools.partial(attend, spans, sizes, ways, numbers),
-            out_shape=outs,
-            in_specs=[vmem()] * len(given),
-            out_specs=[vmem()] * len(outs),
-            scratch_shapes=[pltpu.VMEM((spans, rows, spans * len(numbers) * tok_rows), jnp.float32)],
-            compiler_params=params,
-            cost_estimate=pl.CostEstimate(
-                flops=OWN_FLOPS if first else LATER_FLOPS, bytes_accessed=4_000_000, transcendentals=0
-            ),
-            name=f"attend_{start}",
-        )(*given)
-    outs = state[0]
+    for start, stop in zip(cut[:-2], cut[1:-1], strict=True):
+        flops = OWN_FLOPS if start == 0 else LATER_FLOPS
+        state = stage(start, stop, range(spans), state, flops, f"attend_{start}")
+    outs = [None] * spans
+    parts = [tuple(range(spans))]
+    for i, part in enumerate(parts):
+        done = stage(cut[-2], cut[-1], part, state, LATER_FLOPS, f"attend_last_{i}")[0]
+        for k in part:
+            outs[k] = done[k]
 
     home = [outs[0]] + [None] * (spans - 1)
     places = [0, *range(1, spans - 2), *range(spans - 2, spans)[::-1]] if spans > 2 else list(range(spans))

time: 28.2 us -> 27.7 us (0.982)
  Pallas kernels: 5.99 us -> 5.39 us
    pallas_call x3, Pallas kernels: 3.98 us -> 3.38 us  [stage(): pl.pallas_call(functools.partial(attend, spans, sizes, ways, numbers, cho...]
where the time goes in v6:
time: 27.7 us; the launch traced here: 27.5 us
  starting transfers between devices  13.9 us (50%)
  waiting for transfers between devices  8.06 us (29%)
  Pallas kernels  5.39 us (19%)
    ppermute x9, starting transfers between devices, exchange(): return lax.ppermute(block, 'span', [(i, i ^ k) for i in range(spans)])  12.2 us
    ppermute x9, waiting for transfers between devices, exchange(): return lax.ppermute(block, 'span', [(i, i ^ k) for i in range(spans)])  7.54 us
    pallas_call x3, Pallas kernels, stage(): pl.pallas_call(functools.partial(attend, spans, sizes, ways, numbers, cho...  3.38 us
    ppermute x3, starting transfers between devices, swap(): return lax.ppermute(block, ('ty', 'tx'), moves)  1.72 us
    pallas_call x1, Pallas kernels, shards(): pl.pallas_call(functools.partial(split, spans, sizes, ways), out_shape=[p...  1.16 us
    pallas_call x1, Pallas kernels, shards(): pl.pallas_call(functools.partial(join, places), out_shape=jax.ShapeDtypeS...  0.8 us
  transfers between devices with their start and end apart: 12, of which 6 were waited for; matrix products, arithmetic and copies ran while one was open for 0% of the time, Pallas kernels for 8%

profile of v6, /device:TPU:0, one launch (start us, length us, event | category | flops | bytes accessed | tf_op | source)
XLA Modules:
  0.0 27.5 jit_solution(17133497692652806573)
XLA Ops:
  0.0 1.2 %split.1 = (bf16[2,128,128]{2,1,0:T(8,128)(2,1)S(1)}, bf16[2,128,128]{2,1,0:T(8,128)(2,1)S(1)}, bf16[2,128,128]{2,1,0:T(8,128)(2,1)S(1)}, bf16[2,128,128]{2,1,0:...) custom-call(s32[5]{0:T(128)} %bitcast.22, ...), custom_call_target="tpu_custom_call" | custom-call | tf_op jit(solution)/shard_map/split/pallas_call | solution.py:288
  1.2 3.0 %collective-permute-start = (bf16[2,128,128]{2,1,0:T(8,128)(2,1)S(1)}, bf16[2,128,128]{2,1,0:T(8,128)(2,1)S(1)}, u32[]{:S(2)}, u32[]{:S(2)}) collective-permute-start(bf16[2,128,128]{2,1,0:T(8,128)(2,1)S(1)} %get-tuple-element.24), channel_id=1, source_target_pairs={{0,8},{8,0},{16,24},{24,16},{1,9},{9,1},{17,25},{25,17},{2,10},{10... | collective-permute-start | bytes 196616 | tf_op jit(solution)/shard_map/ppermute | solution.py:278
  4.2 1.5 %collective-permute-start.1 = (bf16[2,128,128]{2,1,0:T(8,128)(2,1)S(1)}, bf16[2,128,128]{2,1,0:T(8,128)(2,1)S(1)}, u32[]{:S(2)}, u32[]{:S(2)}) collective-permute-start(bf16[2,128,128]{2,1,0:T(8,128)(2,1)S(1)} %get-tuple-element.25), channel_id=1, source_target_pairs={{0,16},{8,24},{16,0},{24,8},{1,17},{9,25},{17,1},{25,9},{2,18},{10... | collective-permute-start | bytes 196616 | tf_op jit(solution)/shard_map/ppermute | solution.py:278
  5.7 0.0 collective-permute-start.2
  5.7 1.9 %collective-permute-start.3 = (bf16[144,384]{1,0:T(8,128)(2,1)S(1)}, bf16[144,384]{1,0:T(8,128)(2,1)S(1)}, u32[]{:S(2)}, u32[]{:S(2)}) collective-permute-start(bf16[144,384]{1,0:T(8,128)(2,1)S(1)} %get-tuple-element.28), channel_id=1, source_target_pairs={{0,8},{8,0},{16,24},{24,16},{1,9},{9,1},{17,25},{25,17},{2,10},{10... | collective-permute-start | bytes 331784 | tf_op jit(solution)/shard_map/ppermute | solution.py:278
  7.7 1.5 %collective-permute-start.4 = (bf16[144,384]{1,0:T(8,128)(2,1)S(1)}, bf16[144,384]{1,0:T(8,128)(2,1)S(1)}, u32[]{:S(2)}, u32[]{:S(2)}) collective-permute-start(bf16[144,384]{1,0:T(8,128)(2,1)S(1)} %get-tuple-element.29), channel_id=1, source_target_pairs={{0,16},{8,24},{16,0},{24,8},{1,17},{9,25},{17,1},{25,9},{2,18},{10... | collective-permute-start | bytes 331784 | tf_op jit(solution)/shard_map/ppermute | solution.py:278
  9.2 0.0 collective-permute-done
  9.2 0.6 %collective-permute-start.5 = (bf16[144,384]{1,0:T(8,128)(2,1)S(1)}, bf16[144,384]{1,0:T(8,128)(2,1)S(1)}, u32[]{:S(2)}, u32[]{:S(2)}) collective-permute-start(bf16[144,384]{1,0:T(8,128)(2,1)S(1)} %get-tuple-element.30), channel_id=1, source_target_pairs={{0,24},{8,16},{16,8},{24,0},{1,25},{9,17},{17,9},{25,1},{2,26},{10... | collective-permute-start | bytes 331784 | tf_op jit(solution)/shard_map/ppermute | solution.py:278
  9.8 1.3 %collective-permute-done.2 = bf16[2,128,128]{2,1,0:T(8,128)(2,1)S(1)} collective-permute-done((bf16[2,128,128]{2,1,0:T(8,128)(2,1)S(1)}, bf16[2,128,128]{2,1,0:T(8,128)(2,1)S(1)}, u32[]{:S(2)}, u32[]{:S(2)}) %collective-permute-start.2) | collective-permute-done | bytes 65568 | tf_op jit(solution)/shard_map/ppermute | solution.py:278
  11.1 1.6 %collective-permute-start.6 = (bf16[4,2,128,128]{3,2,1,0:T(8,128)(2,1)S(1)}, bf16[4,2,128,128]{3,2,1,0:T(8,128)(2,1)S(1)}, u32[]{:S(2)}, u32[]{:S(2)}) collective-permute-start(bf16[4,2,128,128]{3,2,1,0:T(8,128)(2,1)S(1)} %pad_maximum_fusion.own_ref.refs_1_), channel_id=1, source_target_pairs={{0,1},{1,0},{2,3},{3,2},{4,5},{5,4},{6,7},{7,6},{8,9},{9,8},{10,11... | collective-permute-start | bytes 786440 | tf_op jit(solution)/shard_map/ppermute | solution.py:54
  12.7 0.8 %collective-permute-done.4.refs_2_ = bf16[144,384]{1,0:T(8,128)(2,1)S(1)} collective-permute-done((bf16[144,384]{1,0:T(8,128)(2,1)S(1)}, bf16[144,384]{1,0:T(8,128)(2,1)S(1)}, u32[]{:S(2)}, u32[]{:S(2)}) %collective-permute-start.4) | collective-permute-done | bytes 110624 | tf_op jit(solution)/shard_map/ppermute | solution.py:278
  13.5 1.3 %collective-permute-done.5.refs_3_ = bf16[144,384]{1,0:T(8,128)(2,1)S(1)} collective-permute-done((bf16[144,384]{1,0:T(8,128)(2,1)S(1)}, bf16[144,384]{1,0:T(8,128)(2,1)S(1)}, u32[]{:S(2)}, u32[]{:S(2)}) %collective-permute-start.5) | collective-permute-done | bytes 110624 | tf_op jit(solution)/shard_map/ppermute | solution.py:278
  14.8 0.1 collect.1
  14.9 0.1 collective-permute-start.8
  15.0 1.0 %attend_0.1 = (f32[4,384,128]{2,1,0:T(8,128)S(1)}, f32[4,384,128]{2,1,0:T(8,128)S(1)}, f32[4,384,128]{2,1,0:T(8,128)S(1)}) custom-call(bf16[4,144,384]{2,1,0:T(8,128)(2,1)S(1)} %get-tuple-element.31.refs_0_, bf16[4,2,128,128]{3,2,1,0:T(8,128)(2,1)S(1)} %pad_maximum_fusion.own_ref.refs_1_, f32[4,8,512]{2,1,0:T(8,128)S(1)} %get-tuple-element.32.refs_2_.refs_3_, ...), custom_call_target="tpu_custom_call" | custom-call | flops 10000000000 | bytes 4000000 | tf_op jit(solution)/shard_map/attend_0/pallas_call | solution.py:352
  16.0 0.5 %collective-permute-done.8.refs_1_ = bf16[4,2,128,128]{3,2,1,0:T(8,128)(2,1)S(1)} collective-permute-done((bf16[4,2,128,128]{3,2,1,0:T(8,128)(2,1)S(1)}, bf16[4,2,128,128]{3,2,1,0:T(8,128)(2,1)S(1)}, u32[]{:S(2)}, u32[]{:S(2)}) %collective-permute-start.8) | collective-permute-done | bytes 262176 | tf_op jit(solution)/shard_map/ppermute | solution.py:54
  16.5 1.1 %attend_1.1 = (f32[4,384,128]{2,1,0:T(8,128)S(1)}, f32[4,384,128]{2,1,0:T(8,128)S(1)}, f32[4,384,128]{2,1,0:T(8,128)S(1)}) custom-call(bf16[4,144,384]{2,1,0:T(8,128)(2,1)S(1)} %get-tuple-element.31.refs_0_, bf16[4,2,128,128]{3,2,1,0:T(8,128)(2,1)S(1)} %collective-permute-done.8.refs_1_, f32[4,8,512]{2,1,0:T(8,128)S(1)} %get-tuple-element.32.refs_2_.refs_3_, ...), custom_call_target="tpu_custom_call" | custom-call | flops 1000000 | bytes 4000000 | tf_op jit(solution)/shard_map/attend_1/pallas_call | solution.py:352
  17.6 1.3 %attend_last_0.1 = bf16[4,128,384]{2,1,0:T(8,128)(2,1)S(1)} custom-call(bf16[4,144,384]{2,1,0:T(8,128)(2,1)S(1)} %get-tuple-element.31.refs_0_, bf16[4,2,128,128]{3,2,1,0:T(8,128)(2,1)S(1)} %collective-permute-done.6.refs_1_, bf16[4,2,128,128]{3,2,1,0:T(8,128)(2,1)S(1)} %collective-permute-done.7.refs_2_, ...), custom_call_target="tpu_custom_call" | custom-call | flops 1000000 | bytes 4000000 | tf_op jit(solution)/shard_map/attend_last_0/pallas_call | solution.py:352
  19.0 1.1 %collective-permute-start.10 = (bf16[128,384]{1,0:T(8,128)(2,1)S(1)}, bf16[128,384]{1,0:T(8,128)(2,1)S(1)}, u32[]{:S(2)}, u32[]{:S(2)}) collective-permute-start(bf16[128,384]{1,0:T(8,128)(2,1)S(1)} %get-tuple-element.42), channel_id=1, source_target_pairs={{0,24},{8,16},{16,8},{24,0},{1,25},{9,17},{17,9},{25,1},{2,26},{10... | collective-permute-start | bytes 294920 | tf_op jit(solution)/shard_map/ppermute | solution.py:278
  20.0 1.3 %collective-permute-start.11 = (bf16[128,384]{1,0:T(8,128)(2,1)S(1)}, bf16[128,384]{1,0:T(8,128)(2,1)S(1)}, u32[]{:S(2)}, u32[]{:S(2)}) collective-permute-start(bf16[128,384]{1,0:T(8,128)(2,1)S(1)} %get-tuple-element.41), channel_id=1, source_target_pairs={{0,16},{8,24},{16,0},{24,8},{1,17},{9,25},{17,1},{25,9},{2,18},{10... | collective-permute-start | bytes 294920 | tf_op jit(solution)/shard_map/ppermute | solution.py:278
  21.4 1.2 %collective-permute-start.9 = (bf16[128,384]{1,0:T(8,128)(2,1)S(1)}, bf16[128,384]{1,0:T(8,128)(2,1)S(1)}, u32[]{:S(2)}, u32[]{:S(2)}) collective-permute-start(bf16[128,384]{1,0:T(8,128)(2,1)S(1)} %get-tuple-element.43), channel_id=1, source_target_pairs={{0,8},{8,0},{16,24},{24,16},{1,9},{9,1},{17,25},{25,17},{2,10},{10... | collective-permute-start | bytes 294920 | tf_op jit(solution)/shard_map/ppermute | solution.py:278
  22.5 3.1 %collective-permute-done.10.refs_2_ = bf16[128,384]{1,0:T(8,128)(2,1)S(1)} collective-permute-done((bf16[128,384]{1,0:T(8,128)(2,1)S(1)}, bf16[128,384]{1,0:T(8,128)(2,1)S(1)}, u32[]{:S(2)}, u32[]{:S(2)}) %collective-permute-start.10) | collective-permute-done | bytes 98336 | tf_op jit(solution)/shard_map/ppermute | solution.py:278
  25.6 1.1 %collective-permute-done.11.refs_3_ = bf16[128,384]{1,0:T(8,128)(2,1)S(1)} collective-permute-done((bf16[128,384]{1,0:T(8,128)(2,1)S(1)}, bf16[128,384]{1,0:T(8,128)(2,1)S(1)}, u32[]{:S(2)}, u32[]{:S(2)}) %collective-permute-start.11) | collective-permute-done | bytes 98336 | tf_op jit(solution)/shard_map/ppermute | solution.py:278
  26.7 0.8 %join.1 = bf16[128,1536]{1,0:T(8,128)(2,1)} custom-call(bf16[128,384]{1,0:T(8,128)(2,1)S(1)} %get-tuple-element.44.refs_0_, bf16[128,384]{1,0:T(8,128)(2,1)S(1)} %collective-permute-done.9.refs_1_, bf16[128,384]{1,0:T(8,128)(2,1)S(1)} %collective-permute-done.10.refs_2_, bf16[128,384]{1,0:T(8,128)(2,1)S(1)} %collective-permute-done.11.refs_3_), custom_call_target="tpu_custom_call" | custom-call | tf_op jit(solution)/shard_map/join/pallas_call | solution.py:379
  (8 shorter events, 0.1 us)
Async XLA Ops:
  1.2 8.0 %collective-permute-start = (bf16[2,128,128]{2,1,0:T(8,128)(2,1)S(1)}, bf16[2,128,128]{2,1,0:T(8,128)(2,1)S(1)}, u32[]{:S(2)}, u32[]{:S(2)}) collective-permute-start(bf16[2,128,128]{2,1,0:T(8,128)(2,1)S(1)} %get-tuple-element.24), channel_id=1, source_target_pairs={{0,8},{8,0},{16,24},{24,16},{1,9},{9,1},{17,25},{25,17},{2,10},{10... | collective-permute-start | bytes 196616 | tf_op jit(solution)/shard_map/ppermute | solution.py:278
  4.2 5.6 %collective-permute-start.1 = (bf16[2,128,128]{2,1,0:T(8,128)(2,1)S(1)}, bf16[2,128,128]{2,1,0:T(8,128)(2,1)S(1)}, u32[]{:S(2)}, u32[]{:S(2)}) collective-permute-start(bf16[2,128,128]{2,1,0:T(8,128)(2,1)S(1)} %get-tuple-element.25), channel_id=1, source_target_pairs={{0,16},{8,24},{16,0},{24,8},{1,17},{9,25},{17,1},{25,9},{2,18},{10... | collective-permute-start | bytes 196616 | tf_op jit(solution)/shard_map/ppermute | solution.py:278
  5.7 5.4 %collective-permute-start.2 = (bf16[2,128,128]{2,1,0:T(8,128)(2,1)S(1)}, bf16[2,128,128]{2,1,0:T(8,128)(2,1)S(1)}, u32[]{:S(2)}, u32[]{:S(2)}) collective-permute-start(bf16[2,128,128]{2,1,0:T(8,128)(2,1)S(1)} %get-tuple-element.26), channel_id=1, source_target_pairs={{0,24},{8,16},{16,8},{24,0},{1,25},{9,17},{17,9},{25,1},{2,26},{10... | collective-permute-start | bytes 196616 | tf_op jit(solution)/shard_map/ppermute | solution.py:278
  5.7 7.0 %collective-permute-start.3 = (bf16[144,384]{1,0:T(8,128)(2,1)S(1)}, bf16[144,384]{1,0:T(8,128)(2,1)S(1)}, u32[]{:S(2)}, u32[]{:S(2)}) collective-permute-start(bf16[144,384]{1,0:T(8,128)(2,1)S(1)} %get-tuple-element.28), channel_id=1, source_target_pairs={{0,8},{8,0},{16,24},{24,16},{1,9},{9,1},{17,25},{25,17},{2,10},{10... | collective-permute-start | bytes 331784 | tf_op jit(solution)/shard_map/ppermute | solution.py:278
  7.7 5.9 %collective-permute-start.4 = (bf16[144,384]{1,0:T(8,128)(2,1)S(1)}, bf16[144,384]{1,0:T(8,128)(2,1)S(1)}, u32[]{:S(2)}, u32[]{:S(2)}) collective-permute-start(bf16[144,384]{1,0:T(8,128)(2,1)S(1)} %get-tuple-element.29), channel_id=1, source_target_pairs={{0,16},{8,24},{16,0},{24,8},{1,17},{9,25},{17,1},{25,9},{2,18},{10... | collective-permute-start | bytes 331784 | tf_op jit(solution)/shard_map/ppermute | solution.py:278
  9.2 5.6 %collective-permute-start.5 = (bf16[144,384]{1,0:T(8,128)(2,1)S(1)}, bf16[144,384]{1,0:T(8,128)(2,1)S(1)}, u32[]{:S(2)}, u32[]{:S(2)}) collective-permute-start(bf16[144,384]{1,0:T(8,128)(2,1)S(1)} %get-tuple-element.30), channel_id=1, source_target_pairs={{0,24},{8,16},{16,8},{24,0},{1,25},{9,17},{17,9},{25,1},{2,26},{10... | collective-permute-start | bytes 331784 | tf_op jit(solution)/shard_map/ppermute | solution.py:278
  11.1 6.5 %collective-permute-start.6 = (bf16[4,2,128,128]{3,2,1,0:T(8,128)(2,1)S(1)}, bf16[4,2,128,128]{3,2,1,0:T(8,128)(2,1)S(1)}, u32[]{:S(2)}, u32[]{:S(2)}) collective-permute-start(bf16[4,2,128,128]{3,2,1,0:T(8,128)(2,1)S(1)} %pad_maximum_fusion.own_ref.refs_1_), channel_id=1, source_target_pairs={{0,1},{1,0},{2,3},{3,2},{4,5},{5,4},{6,7},{7,6},{8,9},{9,8},{10,11... | collective-permute-start | bytes 786440 | tf_op jit(solution)/shard_map/ppermute | solution.py:54
  12.7 4.9 %collective-permute-start.7 = (bf16[4,2,128,128]{3,2,1,0:T(8,128)(2,1)S(1)}, bf16[4,2,128,128]{3,2,1,0:T(8,128)(2,1)S(1)}, u32[]{:S(2)}, u32[]{:S(2)}) collective-permute-start(bf16[4,2,128,128]{3,2,1,0:T(8,128)(2,1)S(1)} %pad_maximum_fusion.own_ref.refs_1_), channel_id=1, source_target_pairs={{0,4},{1,2},{2,1},{3,7},{4,0},{5,6},{6,5},{7,3},{8,12},{9,10},{10,... | collective-permute-start | bytes 786440 | tf_op jit(solution)/shard_map/ppermute | solution.py:54
  14.9 1.6 %collective-permute-start.8 = (bf16[4,2,128,128]{3,2,1,0:T(8,128)(2,1)S(1)}, bf16[4,2,128,128]{3,2,1,0:T(8,128)(2,1)S(1)}, u32[]{:S(2)}, u32[]{:S(2)}) collective-permute-start(bf16[4,2,128,128]{3,2,1,0:T(8,128)(2,1)S(1)} %get-tuple-element.34), channel_id=1, source_target_pairs={{0,4},{1,5},{2,6},{3,7},{4,0},{5,1},{6,2},{7,3},{8,12},{9,13},{10,... | collective-permute-start | bytes 786440 | tf_op jit(solution)/shard_map/ppermute | solution.py:54
  19.0 6.6 %collective-permute-start.10 = (bf16[128,384]{1,0:T(8,128)(2,1)S(1)}, bf16[128,384]{1,0:T(8,128)(2,1)S(1)}, u32[]{:S(2)}, u32[]{:S(2)}) collective-permute-start(bf16[128,384]{1,0:T(8,128)(2,1)S(1)} %get-tuple-element.42), channel_id=1, source_target_pairs={{0,24},{8,16},{16,8},{24,0},{1,25},{9,17},{17,9},{25,1},{2,26},{10... | collective-permute-start | bytes 294920 | tf_op jit(solution)/shard_map/ppermute | solution.py:278
  20.0 6.7 %collective-permute-start.11 = (bf16[128,384]{1,0:T(8,128)(2,1)S(1)}, bf16[128,384]{1,0:T(8,128)(2,1)S(1)}, u32[]{:S(2)}, u32[]{:S(2)}) collective-permute-start(bf16[128,384]{1,0:T(8,128)(2,1)S(1)} %get-tuple-element.41), channel_id=1, source_target_pairs={{0,16},{8,24},{16,0},{24,8},{1,17},{9,25},{17,1},{25,9},{2,18},{10... | collective-permute-start | bytes 294920 | tf_op jit(solution)/shard_map/ppermute | solution.py:278
  21.4 5.3 %collective-permute-start.9 = (bf16[128,384]{1,0:T(8,128)(2,1)S(1)}, bf16[128,384]{1,0:T(8,128)(2,1)S(1)}, u32[]{:S(2)}, u32[]{:S(2)}) collective-permute-start(bf16[128,384]{1,0:T(8,128)(2,1)S(1)} %get-tuple-element.43), channel_id=1, source_target_pairs={{0,8},{8,0},{16,24},{24,16},{1,9},{9,1},{17,25},{25,17},{2,10},{10... | collective-permute-start | bytes 294920 | tf_op jit(solution)/shard_map/ppermute | solution.py:278

commit v7 on v6

--- a/solution.py
+++ b/solution.py
@@ -14,7 +14,7 @@
 EXTRA = 16
 OWN_FLOPS = 10_000_000_000
 LATER_FLOPS = 1_000_000
-CUTS = (1, 2)
+CUTS = (1, 2, 3)
 SMALL = pl.CostEstimate(flops=1000, bytes_accessed=1000, transcendentals=0)
 DEAD = -1e30
 VMEM_LIMIT = 40 * 1024 * 1024
@@ -189,29 +189,33 @@
         )
 
     def weigh(span, used):
-        values = gathered(span, 1, used)
-        bias = bias_of(span, used)
-        blocks = [slice(b, b + HEAD_SIZE) for b in range(0, values.shape[0], HEAD_SIZE)]
+        if used:
+            values = gathered(span, 1, used)
+            bias = bias_of(span, used)
+            blocks = [slice(b, b + HEAD_SIZE) for b in range(0, values.shape[0], HEAD_SIZE)]
         for g in range(groups):
             rows = slice(g * tok_rows, (g + 1) * tok_rows)
             shape = (tok_rows, HEAD_SIZE)
-            before = jnp.full(shape, DEAD, jnp.float32) if first else top_in[span, rows]
-            top = before
-            for lanes in blocks:
-                top = jnp.maximum(top, score_ref[span, rows, lanes] + bias[:, lanes])
-            top = jnp.broadcast_to(jnp.max(top, axis=1, keepdims=True), shape)
-            total, weights = jnp.zeros(shape, jnp.float32), []
-            for lanes in blocks:
-                weight = jnp.exp2((score_ref[span, rows, lanes] + bias[:, lanes] - top) * factor)
-                total = total + weight
-                weights.append(weight.astype(jnp.bfloat16))
-            result = jnp.dot(
-                jnp.concatenate(weights, axis=1), values, preferred_element_type=jnp.float32
-            )
-            if not first:
-                fade = jnp.exp2((before - top) * factor)
-                total = total + sum_in[span, rows] * fade
-                result = result + acc_in[span, rows] * fade
+            if used:
+                before = jnp.full(shape, DEAD, jnp.float32) if first else top_in[span, rows]
+                top = before
+                for lanes in blocks:
+                    top = jnp.maximum(top, score_ref[span, rows, lanes] + bias[:, lanes])
+                top = jnp.broadcast_to(jnp.max(top, axis=1, keepdims=True), shape)
+                total, weights = jnp.zeros(shape, jnp.float32), []
+                for lanes in blocks:
+                    weight = jnp.exp2((score_ref[span, rows, lanes] + bias[:, lanes] - top) * factor)
+                    total = total + weight
+                    weights.append(weight.astype(jnp.bfloat16))
+                result = jnp.dot(
+                    jnp.concatenate(weights, axis=1), values, preferred_element_type=jnp.float32
+                )
+                if not first:
+                    fade = jnp.exp2((before - top) * factor)
+                    total = total + sum_in[span, rows] * fade
+                    result = result + acc_in[span, rows] * fade
+            else:
+                top, total, result = top_in[span, rows], sum_in[span, rows], acc_in[span, rows]
             if not last:
                 top_ref[span, rows], sum_ref[span, rows], acc_ref[span, rows] = top, total, result
                 continue
@@ -222,9 +226,10 @@
             ).astype(jnp.bfloat16)
 
     def run(some, used):
-        score(some[0], used)
+        if used:
+            score(some[0], used)
         for i, span in enumerate(some):
-            if i + 1 < len(some):
+            if used and i + 1 < len(some):
                 score(some[i + 1], used)
             weigh(span, used)
 
@@ -240,7 +245,7 @@
             tests = [] if len(places) == spans else [[me == place for place in places]]
             if len(borders) > 1:
                 tests += [[(steps[n] != 0) == (n in inside)] for n in numbers if steps[n] is not None]
-            case = functools.partial(run, some, inside or numbers[:1])
+            case = functools.partial(run, some, inside)
             if tests:
                 tests = [functools.reduce(jnp.logical_or, test) for test in tests]
                 pl.when(functools.reduce(jnp.logical_and, tests))(case)
@@ -248,10 +253,12 @@
                 case()
 
 
-def collect(spans, own_ref, *refs):
-    q_refs, (q_all_ref, copy_ref) = refs[:spans], refs[spans:]
+def collect(spans, *refs):
     for k in range(spans):
-        q_all_ref[k] = q_refs[k][...]
+        refs[spans][k] = refs[k][...]
+
+
+def copy(own_ref, after_ref, copy_ref):
     copy_ref[...] = own_ref[...]
 
 
@@ -329,18 +336,24 @@
 
     sizes = (ty_count, tx_count)
     rows = groups * tok_rows
-    q_all, own_copy = pl.pallas_call(
+    own_copy = pl.pallas_call(
+        copy,
+        out_shape=jax.ShapeDtypeStruct(own.shape, bf16),
+        in_specs=[vmem()] * 2,
+        out_specs=vmem(),
+        compiler_params=params,
+        cost_estimate=SMALL,
+        name="copy",
+    )(own, q_here[1])
+    q_all = pl.pallas_call(
         functools.partial(collect, spans),
-        out_shape=[
-            jax.ShapeDtypeStruct((spans, *q_here[0].shape), bf16),
-            jax.ShapeDtypeStruct(own.shape, bf16),
-        ],
-        in_specs=[vmem()] * (1 + spans),
-        out_specs=[vmem()] * 2,
+        out_shape=jax.ShapeDtypeStruct((spans, *q_here[0].shape), bf16),
+        in_specs=[vmem()] * spans,
+        out_specs=vmem(),
         compiler_params=params,
+        cost_estimate=SMALL,
         name="collect",
-    )(own, *q_here)
-
+    )(*q_here)
     tiles = [own] + [swap(own if dim else own_copy, sizes, dim, pairs) for dim, _, pairs in swaps]
     kept = jax.ShapeDtypeStruct((spans, rows, HEAD_SIZE), jnp.float32)
     result = jax.ShapeDtypeStruct((spans, tok_rows, width), bf16)

time: 27.7 us -> 27.1 us (0.978)
  waiting for transfers between devices: 8.06 us -> 6.84 us
  starting transfers between devices: 13.9 us -> 14.4 us
    ppermute x9, waiting for transfers between devices: 7.54 us -> 6.32 us  [exchange(): return lax.ppermute(block, 'span', [(i, i ^ k) for i in range(spans)])]
    ppermute x3, starting transfers between devices: 1.72 us -> 2.22 us  [swap(): return lax.ppermute(block, ('ty', 'tx'), moves)]
    pallas_call x3 -> x4, Pallas kernels: 3.38 us -> 3.5 us  [stage(): pl.pallas_call(functools.partial(attend, spans, sizes, ways, numbers, cho...]
  transfers between devices with their start and end apart: 12 -> 12, of which waited for: 6 -> 7; matrix products, arithmetic and copies ran while one was open for 0% -> 0% of each run, Pallas kernels for 8% -> 12%
where the time goes in v7:
time: 27.1 us; the launch traced here: 26.9 us
  starting transfers between devices  14.4 us (53%)
  waiting for transfers between devices  6.84 us (25%)
  Pallas kernels  5.51 us (20%)
    ppermute x9, starting transfers between devices, exchange(): return lax.ppermute(block, 'span', [(i, i ^ k) for i in range(spans)])  12.2 us
    ppermute x9, waiting for transfers between devices, exchange(): return lax.ppermute(block, 'span', [(i, i ^ k) for i in range(spans)])  6.32 us
    pallas_call x4, Pallas kernels, stage(): pl.pallas_call(functools.partial(attend, spans, sizes, ways, numbers, cho...  3.5 us
    ppermute x3, starting transfers between devices, swap(): return lax.ppermute(block, ('ty', 'tx'), moves)  2.22 us
    pallas_call x1, Pallas kernels, shards(): pl.pallas_call(functools.partial(split, spans, sizes, ways), out_shape=[p...  1.16 us
    pallas_call x1, Pallas kernels, shards(): pl.pallas_call(functools.partial(join, places), out_shape=jax.ShapeDtypeS...  0.8 us
  transfers between devices with their start and end apart: 12, of which 7 were waited for; matrix products, arithmetic and copies ran while one was open for 0% of the time, Pallas kernels for 12%

profile of v7, /device:TPU:0, one launch (start us, length us, event | category | flops | bytes accessed | tf_op | source)
XLA Modules:
  0.0 26.9 jit_solution(698165414115119946)
XLA Ops:
  0.0 1.2 %split.1 = (bf16[2,128,128]{2,1,0:T(8,128)(2,1)S(1)}, bf16[2,128,128]{2,1,0:T(8,128)(2,1)S(1)}, bf16[2,128,128]{2,1,0:T(8,128)(2,1)S(1)}, bf16[2,128,128]{2,1,0:...) custom-call(s32[5]{0:T(128)} %bitcast.22, ...), custom_call_target="tpu_custom_call" | custom-call | tf_op jit(solution)/shard_map/split/pallas_call | solution.py:295
  1.2 3.0 %collective-permute-start.3 = (bf16[2,128,128]{2,1,0:T(8,128)(2,1)S(1)}, bf16[2,128,128]{2,1,0:T(8,128)(2,1)S(1)}, u32[]{:S(2)}, u32[]{:S(2)}) collective-permute-start(bf16[2,128,128]{2,1,0:T(8,128)(2,1)S(1)} %get-tuple-element.29), channel_id=1, source_target_pairs={{0,8},{8,0},{16,24},{24,16},{1,9},{9,1},{17,25},{25,17},{2,10},{10... | collective-permute-start | bytes 196616 | tf_op jit(solution)/shard_map/ppermute | solution.py:285
  4.2 1.5 %collective-permute-start.4 = (bf16[2,128,128]{2,1,0:T(8,128)(2,1)S(1)}, bf16[2,128,128]{2,1,0:T(8,128)(2,1)S(1)}, u32[]{:S(2)}, u32[]{:S(2)}) collective-permute-start(bf16[2,128,128]{2,1,0:T(8,128)(2,1)S(1)} %get-tuple-element.30), channel_id=1, source_target_pairs={{0,16},{8,24},{16,0},{24,8},{1,17},{9,25},{17,1},{25,9},{2,18},{10... | collective-permute-start | bytes 196616 | tf_op jit(solution)/shard_map/ppermute | solution.py:285
  5.7 0.0 collective-permute-start.5
  5.7 1.9 %collective-permute-start = (bf16[144,384]{1,0:T(8,128)(2,1)S(1)}, bf16[144,384]{1,0:T(8,128)(2,1)S(1)}, u32[]{:S(2)}, u32[]{:S(2)}) collective-permute-start(bf16[144,384]{1,0:T(8,128)(2,1)S(1)} %get-tuple-element.25), channel_id=1, source_target_pairs={{0,8},{8,0},{16,24},{24,16},{1,9},{9,1},{17,25},{25,17},{2,10},{10... | collective-permute-start | bytes 331784 | tf_op jit(solution)/shard_map/ppermute | solution.py:285
  7.7 1.5 %collective-permute-start.1 = (bf16[144,384]{1,0:T(8,128)(2,1)S(1)}, bf16[144,384]{1,0:T(8,128)(2,1)S(1)}, u32[]{:S(2)}, u32[]{:S(2)}) collective-permute-start(bf16[144,384]{1,0:T(8,128)(2,1)S(1)} %get-tuple-element.26), channel_id=1, source_target_pairs={{0,16},{8,24},{16,0},{24,8},{1,17},{9,25},{17,1},{25,9},{2,18},{10... | collective-permute-start | bytes 331784 | tf_op jit(solution)/shard_map/ppermute | solution.py:285
  9.2 0.6 %collective-permute-start.2 = (bf16[144,384]{1,0:T(8,128)(2,1)S(1)}, bf16[144,384]{1,0:T(8,128)(2,1)S(1)}, u32[]{:S(2)}, u32[]{:S(2)}) collective-permute-start(bf16[144,384]{1,0:T(8,128)(2,1)S(1)} %get-tuple-element.27), channel_id=1, source_target_pairs={{0,24},{8,16},{16,8},{24,0},{1,25},{9,17},{17,9},{25,1},{2,26},{10... | collective-permute-start | bytes 331784 | tf_op jit(solution)/shard_map/ppermute | solution.py:285
  9.8 1.3 %collective-permute-done.5 = bf16[2,128,128]{2,1,0:T(8,128)(2,1)S(1)} collective-permute-done((bf16[2,128,128]{2,1,0:T(8,128)(2,1)S(1)}, bf16[2,128,128]{2,1,0:T(8,128)(2,1)S(1)}, u32[]{:S(2)}, u32[]{:S(2)}) %collective-permute-start.5) | collective-permute-done | bytes 65568 | tf_op jit(solution)/shard_map/ppermute | solution.py:285
  11.1 1.6 %collective-permute-start.7 = (bf16[4,2,128,128]{3,2,1,0:T(8,128)(2,1)S(1)}, bf16[4,2,128,128]{3,2,1,0:T(8,128)(2,1)S(1)}, u32[]{:S(2)}, u32[]{:S(2)}) collective-permute-start(bf16[4,2,128,128]{3,2,1,0:T(8,128)(2,1)S(1)} %pad_maximum_fusion.own_ref.refs_1_), channel_id=1, source_target_pairs={{0,1},{1,0},{2,3},{3,2},{4,5},{5,4},{6,7},{7,6},{8,9},{9,8},{10,11... | collective-permute-start | bytes 786440 | tf_op jit(solution)/shard_map/ppermute | solution.py:54
  12.8 0.6 %collective-permute-start.8 = (bf16[4,2,128,128]{3,2,1,0:T(8,128)(2,1)S(1)}, bf16[4,2,128,128]{3,2,1,0:T(8,128)(2,1)S(1)}, u32[]{:S(2)}, u32[]{:S(2)}) collective-permute-start(bf16[4,2,128,128]{3,2,1,0:T(8,128)(2,1)S(1)} %copy.7), channel_id=1, source_target_pairs={{0,4},{1,5},{2,6},{3,7},{4,0},{5,1},{6,2},{7,3},{8,12},{9,13},{10,... | collective-permute-start | bytes 786440 | tf_op jit(solution)/shard_map/ppermute | solution.py:54
  13.3 0.2 collective-permute-done.1.refs_2_
  13.5 1.3 %collective-permute-done.2.refs_3_ = bf16[144,384]{1,0:T(8,128)(2,1)S(1)} collective-permute-done((bf16[144,384]{1,0:T(8,128)(2,1)S(1)}, bf16[144,384]{1,0:T(8,128)(2,1)S(1)}, u32[]{:S(2)}, u32[]{:S(2)}) %collective-permute-start.2) | collective-permute-done | bytes 110624 | tf_op jit(solution)/shard_map/ppermute | solution.py:285
  14.9 1.0 %attend_0.1 = (f32[4,384,128]{2,1,0:T(8,128)S(1)}, f32[4,384,128]{2,1,0:T(8,128)S(1)}, f32[4,384,128]{2,1,0:T(8,128)S(1)}) custom-call(bf16[4,144,384]{2,1,0:T(8,128)(2,1)S(1)} %collect.1.refs_0_, bf16[4,2,128,128]{3,2,1,0:T(8,128)(2,1)S(1)} %pad_maximum_fusion.own_ref.refs_1_, f32[4,8,512]{2,1,0:T(8,128)S(1)} %get-tuple-element.32.refs_2_, ...), custom_call_target="tpu_custom_call" | custom-call | flops 10000000000 | bytes 4000000 | tf_op jit(solution)/shard_map/attend_0/pallas_call | solution.py:365
  15.9 1.1 %attend_1.1 = (f32[4,384,128]{2,1,0:T(8,128)S(1)}, f32[4,384,128]{2,1,0:T(8,128)S(1)}, f32[4,384,128]{2,1,0:T(8,128)S(1)}) custom-call(bf16[4,144,384]{2,1,0:T(8,128)(2,1)S(1)} %collect.1.refs_0_, bf16[4,2,128,128]{3,2,1,0:T(8,128)(2,1)S(1)} %collective-permute-done.8.refs_1_, f32[4,8,512]{2,1,0:T(8,128)S(1)} %get-tuple-element.32.refs_2_, ...), custom_call_target="tpu_custom_call" | custom-call | flops 1000000 | bytes 4000000 | tf_op jit(solution)/shard_map/attend_1/pallas_call | solution.py:365
  17.0 0.5 %collective-permute-done.7.refs_1_ = bf16[4,2,128,128]{3,2,1,0:T(8,128)(2,1)S(1)} collective-permute-done((bf16[4,2,128,128]{3,2,1,0:T(8,128)(2,1)S(1)}, bf16[4,2,128,128]{3,2,1,0:T(8,128)(2,1)S(1)}, u32[]{:S(2)}, u32[]{:S(2)}) %collective-permute-start.7) | collective-permute-done | bytes 262176 | tf_op jit(solution)/shard_map/ppermute | solution.py:54
  17.5 1.1 %attend_2.1 = (f32[4,384,128]{2,1,0:T(8,128)S(1)}, f32[4,384,128]{2,1,0:T(8,128)S(1)}, f32[4,384,128]{2,1,0:T(8,128)S(1)}) custom-call(bf16[4,144,384]{2,1,0:T(8,128)(2,1)S(1)} %collect.1.refs_0_, bf16[4,2,128,128]{3,2,1,0:T(8,128)(2,1)S(1)} %collective-permute-done.7.refs_1_, f32[4,8,512]{2,1,0:T(8,128)S(1)} %get-tuple-element.32.refs_2_, ...), custom_call_target="tpu_custom_call" | custom-call | flops 1000000 | bytes 4000000 | tf_op jit(solution)/shard_map/attend_2/pallas_call | solution.py:365
  18.6 0.3 %attend_last_0.1 = bf16[4,128,384]{2,1,0:T(8,128)(2,1)S(1)} custom-call(bf16[4,144,384]{2,1,0:T(8,128)(2,1)S(1)} %collect.1.refs_0_, bf16[4,2,128,128]{3,2,1,0:T(8,128)(2,1)S(1)} %collective-permute-done.6.refs_1_, f32[4,8,512]{2,1,0:T(8,128)S(1)} %get-tuple-element.32.refs_2_, f32[4,128,128]{2,1,0:T(8,128)S(1)} %get-tuple-element.33.refs_3_, ...), custom_call_target="tpu_custom_call" | custom-call | flops 1000000 | bytes 4000000 | tf_op jit(solution)/shard_map/attend_last_0/pallas_call | solution.py:365
  19.0 1.1 %collective-permute-start.10 = (bf16[128,384]{1,0:T(8,128)(2,1)S(1)}, bf16[128,384]{1,0:T(8,128)(2,1)S(1)}, u32[]{:S(2)}, u32[]{:S(2)}) collective-permute-start(bf16[128,384]{1,0:T(8,128)(2,1)S(1)} %get-tuple-element.44), channel_id=1, source_target_pairs={{0,24},{8,16},{16,8},{24,0},{1,25},{9,17},{17,9},{25,1},{2,26},{10... | collective-permute-start | bytes 294920 | tf_op jit(solution)/shard_map/ppermute | solution.py:285
  20.1 1.4 %collective-permute-start.11 = (bf16[128,384]{1,0:T(8,128)(2,1)S(1)}, bf16[128,384]{1,0:T(8,128)(2,1)S(1)}, u32[]{:S(2)}, u32[]{:S(2)}) collective-permute-start(bf16[128,384]{1,0:T(8,128)(2,1)S(1)} %get-tuple-element.43), channel_id=1, source_target_pairs={{0,16},{8,24},{16,0},{24,8},{1,17},{9,25},{17,1},{25,9},{2,18},{10... | collective-permute-start | bytes 294920 | tf_op jit(solution)/shard_map/ppermute | solution.py:285
  21.5 1.1 %collective-permute-start.9 = (bf16[128,384]{1,0:T(8,128)(2,1)S(1)}, bf16[128,384]{1,0:T(8,128)(2,1)S(1)}, u32[]{:S(2)}, u32[]{:S(2)}) collective-permute-start(bf16[128,384]{1,0:T(8,128)(2,1)S(1)} %get-tuple-element.45), channel_id=1, source_target_pairs={{0,8},{8,0},{16,24},{24,16},{1,9},{9,1},{17,25},{25,17},{2,10},{10... | collective-permute-start | bytes 294920 | tf_op jit(solution)/shard_map/ppermute | solution.py:285
  22.5 2.1 %collective-permute-done.10.refs_2_ = bf16[128,384]{1,0:T(8,128)(2,1)S(1)} collective-permute-done((bf16[128,384]{1,0:T(8,128)(2,1)S(1)}, bf16[128,384]{1,0:T(8,128)(2,1)S(1)}, u32[]{:S(2)}, u32[]{:S(2)}) %collective-permute-start.10) | collective-permute-done | bytes 98336 | tf_op jit(solution)/shard_map/ppermute | solution.py:285
  24.7 1.0 %collective-permute-done.11.refs_3_ = bf16[128,384]{1,0:T(8,128)(2,1)S(1)} collective-permute-done((bf16[128,384]{1,0:T(8,128)(2,1)S(1)}, bf16[128,384]{1,0:T(8,128)(2,1)S(1)}, u32[]{:S(2)}, u32[]{:S(2)}) %collective-permute-start.11) | collective-permute-done | bytes 98336 | tf_op jit(solution)/shard_map/ppermute | solution.py:285
  25.6 0.5 %collective-permute-done.9.refs_1_ = bf16[128,384]{1,0:T(8,128)(2,1)S(1)} collective-permute-done((bf16[128,384]{1,0:T(8,128)(2,1)S(1)}, bf16[128,384]{1,0:T(8,128)(2,1)S(1)}, u32[]{:S(2)}, u32[]{:S(2)}) %collective-permute-start.9) | collective-permute-done | bytes 98336 | tf_op jit(solution)/shard_map/ppermute | solution.py:285
  26.1 0.8 %join.1 = bf16[128,1536]{1,0:T(8,128)(2,1)} custom-call(bf16[128,384]{1,0:T(8,128)(2,1)S(1)} %get-tuple-element.46.refs_0_, bf16[128,384]{1,0:T(8,128)(2,1)S(1)} %collective-permute-done.9.refs_1_, bf16[128,384]{1,0:T(8,128)(2,1)S(1)} %collective-permute-done.10.refs_2_, bf16[128,384]{1,0:T(8,128)(2,1)S(1)} %collective-permute-done.11.refs_3_), custom_call_target="tpu_custom_call" | custom-call | tf_op jit(solution)/shard_map/join/pallas_call | solution.py:392
  (10 shorter events, 0.2 us)
Async XLA Ops:
  1.2 8.0 %collective-permute-start.3 = (bf16[2,128,128]{2,1,0:T(8,128)(2,1)S(1)}, bf16[2,128,128]{2,1,0:T(8,128)(2,1)S(1)}, u32[]{:S(2)}, u32[]{:S(2)}) collective-permute-start(bf16[2,128,128]{2,1,0:T(8,128)(2,1)S(1)} %get-tuple-element.29), channel_id=1, source_target_pairs={{0,8},{8,0},{16,24},{24,16},{1,9},{9,1},{17,25},{25,17},{2,10},{10... | collective-permute-start | bytes 196616 | tf_op jit(solution)/shard_map/ppermute | solution.py:285
  4.2 5.6 %collective-permute-start.4 = (bf16[2,128,128]{2,1,0:T(8,128)(2,1)S(1)}, bf16[2,128,128]{2,1,0:T(8,128)(2,1)S(1)}, u32[]{:S(2)}, u32[]{:S(2)}) collective-permute-start(bf16[2,128,128]{2,1,0:T(8,128)(2,1)S(1)} %get-tuple-element.30), channel_id=1, source_target_pairs={{0,16},{8,24},{16,0},{24,8},{1,17},{9,25},{17,1},{25,9},{2,18},{10... | collective-permute-start | bytes 196616 | tf_op jit(solution)/shard_map/ppermute | solution.py:285
  5.7 5.4 %collective-permute-start.5 = (bf16[2,128,128]{2,1,0:T(8,128)(2,1)S(1)}, bf16[2,128,128]{2,1,0:T(8,128)(2,1)S(1)}, u32[]{:S(2)}, u32[]{:S(2)}) collective-permute-start(bf16[2,128,128]{2,1,0:T(8,128)(2,1)S(1)} %get-tuple-element.31), channel_id=1, source_target_pairs={{0,24},{8,16},{16,8},{24,0},{1,25},{9,17},{17,9},{25,1},{2,26},{10... | collective-permute-start | bytes 196616 | tf_op jit(solution)/shard_map/ppermute | solution.py:285
  5.7 7.0 %collective-permute-start = (bf16[144,384]{1,0:T(8,128)(2,1)S(1)}, bf16[144,384]{1,0:T(8,128)(2,1)S(1)}, u32[]{:S(2)}, u32[]{:S(2)}) collective-permute-start(bf16[144,384]{1,0:T(8,128)(2,1)S(1)} %get-tuple-element.25), channel_id=1, source_target_pairs={{0,8},{8,0},{16,24},{24,16},{1,9},{9,1},{17,25},{25,17},{2,10},{10... | collective-permute-start | bytes 331784 | tf_op jit(solution)/shard_map/ppermute | solution.py:285
  7.7 5.9 %collective-permute-start.1 = (bf16[144,384]{1,0:T(8,128)(2,1)S(1)}, bf16[144,384]{1,0:T(8,128)(2,1)S(1)}, u32[]{:S(2)}, u32[]{:S(2)}) collective-permute-start(bf16[144,384]{1,0:T(8,128)(2,1)S(1)} %get-tuple-element.26), channel_id=1, source_target_pairs={{0,16},{8,24},{16,0},{24,8},{1,17},{9,25},{17,1},{25,9},{2,18},{10... | collective-permute-start | bytes 331784 | tf_op jit(solution)/shard_map/ppermute | solution.py:285
  9.2 5.6 %collective-permute-start.2 = (bf16[144,384]{1,0:T(8,128)(2,1)S(1)}, bf16[144,384]{1,0:T(8,128)(2,1)S(1)}, u32[]{:S(2)}, u32[]{:S(2)}) collective-permute-start(bf16[144,384]{1,0:T(8,128)(2,1)S(1)} %get-tuple-element.27), channel_id=1, source_target_pairs={{0,24},{8,16},{16,8},{24,0},{1,25},{9,17},{17,9},{25,1},{2,26},{10... | collective-permute-start | bytes 331784 | tf_op jit(solution)/shard_map/ppermute | solution.py:285
  11.1 6.4 %collective-permute-start.7 = (bf16[4,2,128,128]{3,2,1,0:T(8,128)(2,1)S(1)}, bf16[4,2,128,128]{3,2,1,0:T(8,128)(2,1)S(1)}, u32[]{:S(2)}, u32[]{:S(2)}) collective-permute-start(bf16[4,2,128,128]{3,2,1,0:T(8,128)(2,1)S(1)} %pad_maximum_fusion.own_ref.refs_1_), channel_id=1, source_target_pairs={{0,1},{1,0},{2,3},{3,2},{4,5},{5,4},{6,7},{7,6},{8,9},{9,8},{10,11... | collective-permute-start | bytes 786440 | tf_op jit(solution)/shard_map/ppermute | solution.py:54
  12.7 5.9 %collective-permute-start.6 = (bf16[4,2,128,128]{3,2,1,0:T(8,128)(2,1)S(1)}, bf16[4,2,128,128]{3,2,1,0:T(8,128)(2,1)S(1)}, u32[]{:S(2)}, u32[]{:S(2)}) collective-permute-start(bf16[4,2,128,128]{3,2,1,0:T(8,128)(2,1)S(1)} %pad_maximum_fusion.own_ref.refs_1_), channel_id=1, source_target_pairs={{0,4},{1,2},{2,1},{3,7},{4,0},{5,6},{6,5},{7,3},{8,12},{9,10},{10,... | collective-permute-start | bytes 786440 | tf_op jit(solution)/shard_map/ppermute | solution.py:54
  12.8 3.1 %collective-permute-start.8 = (bf16[4,2,128,128]{3,2,1,0:T(8,128)(2,1)S(1)}, bf16[4,2,128,128]{3,2,1,0:T(8,128)(2,1)S(1)}, u32[]{:S(2)}, u32[]{:S(2)}) collective-permute-start(bf16[4,2,128,128]{3,2,1,0:T(8,128)(2,1)S(1)} %copy.7), channel_id=1, source_target_pairs={{0,4},{1,5},{2,6},{3,7},{4,0},{5,1},{6,2},{7,3},{8,12},{9,13},{10,... | collective-permute-start | bytes 786440 | tf_op jit(solution)/shard_map/ppermute | solution.py:54
  19.0 5.7 %collective-permute-start.10 = (bf16[128,384]{1,0:T(8,128)(2,1)S(1)}, bf16[128,384]{1,0:T(8,128)(2,1)S(1)}, u32[]{:S(2)}, u32[]{:S(2)}) collective-permute-start(bf16[128,384]{1,0:T(8,128)(2,1)S(1)} %get-tuple-element.44), channel_id=1, source_target_pairs={{0,24},{8,16},{16,8},{24,0},{1,25},{9,17},{17,9},{25,1},{2,26},{10... | collective-permute-start | bytes 294920 | tf_op jit(solution)/shard_map/ppermute | solution.py:285
  20.1 5.5 %collective-permute-start.11 = (bf16[128,384]{1,0:T(8,128)(2,1)S(1)}, bf16[128,384]{1,0:T(8,128)(2,1)S(1)}, u32[]{:S(2)}, u32[]{:S(2)}) collective-permute-start(bf16[128,384]{1,0:T(8,128)(2,1)S(1)} %get-tuple-element.43), channel_id=1, source_target_pairs={{0,16},{8,24},{16,0},{24,8},{1,17},{9,25},{17,1},{25,9},{2,18},{10... | collective-permute-start | bytes 294920 | tf_op jit(solution)/shard_map/ppermute | solution.py:285
  21.5 4.6 %collective-permute-start.9 = (bf16[128,384]{1,0:T(8,128)(2,1)S(1)}, bf16[128,384]{1,0:T(8,128)(2,1)S(1)}, u32[]{:S(2)}, u32[]{:S(2)}) collective-permute-start(bf16[128,384]{1,0:T(8,128)(2,1)S(1)} %get-tuple-element.45), channel_id=1, source_target_pairs={{0,8},{8,0},{16,24},{24,16},{1,9},{9,1},{17,25},{25,17},{2,10},{10... | collective-permute-start | bytes 294920 | tf_op jit(solution)/shard_map/ppermute | solution.py:285

commit v8 on v7

--- a/solution.py
+++ b/solution.py
@@ -386,7 +386,7 @@
             outs[k] = done[k]
 
     home = [outs[0]] + [None] * (spans - 1)
-    places = [0, *range(1, spans - 2), *range(spans - 2, spans)[::-1]] if spans > 2 else list(range(spans))
+    places = [0, *range(2, spans), 1] if spans > 2 else list(range(spans))
     for k in order:
         home[k] = exchange(outs[k], k)
     attended = pl.pallas_call(

time: 27.1 us -> 26.9 us (level)
  waiting for transfers between devices: 6.84 us -> 6.48 us
    ppermute x9, waiting for transfers between devices: 6.32 us -> 5.96 us  [exchange(): return lax.ppermute(block, 'span', [(i, i ^ k) for i in range(spans)])]
where the time goes in v8:
time: 26.9 us; the launch traced here: 26.5 us
  starting transfers between devices  14.4 us (54%)
  waiting for transfers between devices  6.48 us (24%)
  Pallas kernels  5.51 us (20%)
    ppermute x9, starting transfers between devices, exchange(): return lax.ppermute(block, 'span', [(i, i ^ k) for i in range(spans)])  12.2 us
    ppermute x9, waiting for transfers between devices, exchange(): return lax.ppermute(block, 'span', [(i, i ^ k) for i in range(spans)])  5.96 us
    pallas_call x4, Pallas kernels, stage(): pl.pallas_call(functools.partial(attend, spans, sizes, ways, numbers, cho...  3.5 us
    ppermute x3, starting transfers between devices, swap(): return lax.ppermute(block, ('ty', 'tx'), moves)  2.22 us
    pallas_call x1, Pallas kernels, shards(): pl.pallas_call(functools.partial(split, spans, sizes, ways), out_shape=[p...  1.16 us
    pallas_call x1, Pallas kernels, shards(): pl.pallas_call(functools.partial(join, places), out_shape=jax.ShapeDtypeS...  0.8 us
  transfers between devices with their start and end apart: 12, of which 7 were waited for; matrix products, arithmetic and copies ran while one was open for 0% of the time, Pallas kernels for 12%

profile of v8, /device:TPU:0, one launch (start us, length us, event | category | flops | bytes accessed | tf_op | source)
XLA Modules:
  0.0 26.5 jit_solution(6352725319908398995)
XLA Ops:
  0.0 1.2 %split.1 = (bf16[2,128,128]{2,1,0:T(8,128)(2,1)S(1)}, bf16[2,128,128]{2,1,0:T(8,128)(2,1)S(1)}, bf16[2,128,128]{2,1,0:T(8,128)(2,1)S(1)}, bf16[2,128,128]{2,1,0:...) custom-call(s32[5]{0:T(128)} %bitcast.22, ...), custom_call_target="tpu_custom_call" | custom-call | tf_op jit(solution)/shard_map/split/pallas_call | solution.py:295
  1.2 3.0 %collective-permute-start.3 = (bf16[2,128,128]{2,1,0:T(8,128)(2,1)S(1)}, bf16[2,128,128]{2,1,0:T(8,128)(2,1)S(1)}, u32[]{:S(2)}, u32[]{:S(2)}) collective-permute-start(bf16[2,128,128]{2,1,0:T(8,128)(2,1)S(1)} %get-tuple-element.29), channel_id=1, source_target_pairs={{0,8},{8,0},{16,24},{24,16},{1,9},{9,1},{17,25},{25,17},{2,10},{10... | collective-permute-start | bytes 196616 | tf_op jit(solution)/shard_map/ppermute | solution.py:285
  4.2 1.5 %collective-permute-start.4 = (bf16[2,128,128]{2,1,0:T(8,128)(2,1)S(1)}, bf16[2,128,128]{2,1,0:T(8,128)(2,1)S(1)}, u32[]{:S(2)}, u32[]{:S(2)}) collective-permute-start(bf16[2,128,128]{2,1,0:T(8,128)(2,1)S(1)} %get-tuple-element.30), channel_id=1, source_target_pairs={{0,16},{8,24},{16,0},{24,8},{1,17},{9,25},{17,1},{25,9},{2,18},{10... | collective-permute-start | bytes 196616 | tf_op jit(solution)/shard_map/ppermute | solution.py:285
  5.7 0.0 collective-permute-start.5
  5.7 1.9 %collective-permute-start = (bf16[144,384]{1,0:T(8,128)(2,1)S(1)}, bf16[144,384]{1,0:T(8,128)(2,1)S(1)}, u32[]{:S(2)}, u32[]{:S(2)}) collective-permute-start(bf16[144,384]{1,0:T(8,128)(2,1)S(1)} %get-tuple-element.25), channel_id=1, source_target_pairs={{0,8},{8,0},{16,24},{24,16},{1,9},{9,1},{17,25},{25,17},{2,10},{10... | collective-permute-start | bytes 331784 | tf_op jit(solution)/shard_map/ppermute | solution.py:285
  7.7 1.5 %collective-permute-start.1 = (bf16[144,384]{1,0:T(8,128)(2,1)S(1)}, bf16[144,384]{1,0:T(8,128)(2,1)S(1)}, u32[]{:S(2)}, u32[]{:S(2)}) collective-permute-start(bf16[144,384]{1,0:T(8,128)(2,1)S(1)} %get-tuple-element.26), channel_id=1, source_target_pairs={{0,16},{8,24},{16,0},{24,8},{1,17},{9,25},{17,1},{25,9},{2,18},{10... | collective-permute-start | bytes 331784 | tf_op jit(solution)/shard_map/ppermute | solution.py:285
  9.2 0.6 %collective-permute-start.2 = (bf16[144,384]{1,0:T(8,128)(2,1)S(1)}, bf16[144,384]{1,0:T(8,128)(2,1)S(1)}, u32[]{:S(2)}, u32[]{:S(2)}) collective-permute-start(bf16[144,384]{1,0:T(8,128)(2,1)S(1)} %get-tuple-element.27), channel_id=1, source_target_pairs={{0,24},{8,16},{16,8},{24,0},{1,25},{9,17},{17,9},{25,1},{2,26},{10... | collective-permute-start | bytes 331784 | tf_op jit(solution)/shard_map/ppermute | solution.py:285
  9.8 1.3 %collective-permute-done.5 = bf16[2,128,128]{2,1,0:T(8,128)(2,1)S(1)} collective-permute-done((bf16[2,128,128]{2,1,0:T(8,128)(2,1)S(1)}, bf16[2,128,128]{2,1,0:T(8,128)(2,1)S(1)}, u32[]{:S(2)}, u32[]{:S(2)}) %collective-permute-start.5) | collective-permute-done | bytes 65568 | tf_op jit(solution)/shard_map/ppermute | solution.py:285
  11.1 1.6 %collective-permute-start.7 = (bf16[4,2,128,128]{3,2,1,0:T(8,128)(2,1)S(1)}, bf16[4,2,128,128]{3,2,1,0:T(8,128)(2,1)S(1)}, u32[]{:S(2)}, u32[]{:S(2)}) collective-permute-start(bf16[4,2,128,128]{3,2,1,0:T(8,128)(2,1)S(1)} %pad_maximum_fusion.own_ref.refs_1_), channel_id=1, source_target_pairs={{0,1},{1,0},{2,3},{3,2},{4,5},{5,4},{6,7},{7,6},{8,9},{9,8},{10,11... | collective-permute-start | bytes 786440 | tf_op jit(solution)/shard_map/ppermute | solution.py:54
  12.8 0.6 %collective-permute-start.8 = (bf16[4,2,128,128]{3,2,1,0:T(8,128)(2,1)S(1)}, bf16[4,2,128,128]{3,2,1,0:T(8,128)(2,1)S(1)}, u32[]{:S(2)}, u32[]{:S(2)}) collective-permute-start(bf16[4,2,128,128]{3,2,1,0:T(8,128)(2,1)S(1)} %copy.7), channel_id=1, source_target_pairs={{0,4},{1,5},{2,6},{3,7},{4,0},{5,1},{6,2},{7,3},{8,12},{9,13},{10,... | collective-permute-start | bytes 786440 | tf_op jit(solution)/shard_map/ppermute | solution.py:54
  13.3 0.2 collective-permute-done.1.refs_2_
  13.5 1.3 %collective-permute-done.2.refs_3_ = bf16[144,384]{1,0:T(8,128)(2,1)S(1)} collective-permute-done((bf16[144,384]{1,0:T(8,128)(2,1)S(1)}, bf16[144,384]{1,0:T(8,128)(2,1)S(1)}, u32[]{:S(2)}, u32[]{:S(2)}) %collective-permute-start.2) | collective-permute-done | bytes 110624 | tf_op jit(solution)/shard_map/ppermute | solution.py:285
  14.9 1.0 %attend_0.1 = (f32[4,384,128]{2,1,0:T(8,128)S(1)}, f32[4,384,128]{2,1,0:T(8,128)S(1)}, f32[4,384,128]{2,1,0:T(8,128)S(1)}) custom-call(bf16[4,144,384]{2,1,0:T(8,128)(2,1)S(1)} %collect.1.refs_0_, bf16[4,2,128,128]{3,2,1,0:T(8,128)(2,1)S(1)} %pad_maximum_fusion.own_ref.refs_1_, f32[4,8,512]{2,1,0:T(8,128)S(1)} %get-tuple-element.32.refs_2_, ...), custom_call_target="tpu_custom_call" | custom-call | flops 10000000000 | bytes 4000000 | tf_op jit(solution)/shard_map/attend_0/pallas_call | solution.py:365
  15.9 1.1 %attend_1.1 = (f32[4,384,128]{2,1,0:T(8,128)S(1)}, f32[4,384,128]{2,1,0:T(8,128)S(1)}, f32[4,384,128]{2,1,0:T(8,128)S(1)}) custom-call(bf16[4,144,384]{2,1,0:T(8,128)(2,1)S(1)} %collect.1.refs_0_, bf16[4,2,128,128]{3,2,1,0:T(8,128)(2,1)S(1)} %collective-permute-done.8.refs_1_, f32[4,8,512]{2,1,0:T(8,128)S(1)} %get-tuple-element.32.refs_2_, ...), custom_call_target="tpu_custom_call" | custom-call | flops 1000000 | bytes 4000000 | tf_op jit(solution)/shard_map/attend_1/pallas_call | solution.py:365
  17.0 0.5 %collective-permute-done.7.refs_1_ = bf16[4,2,128,128]{3,2,1,0:T(8,128)(2,1)S(1)} collective-permute-done((bf16[4,2,128,128]{3,2,1,0:T(8,128)(2,1)S(1)}, bf16[4,2,128,128]{3,2,1,0:T(8,128)(2,1)S(1)}, u32[]{:S(2)}, u32[]{:S(2)}) %collective-permute-start.7) | collective-permute-done | bytes 262176 | tf_op jit(solution)/shard_map/ppermute | solution.py:54
  17.5 1.1 %attend_2.1 = (f32[4,384,128]{2,1,0:T(8,128)S(1)}, f32[4,384,128]{2,1,0:T(8,128)S(1)}, f32[4,384,128]{2,1,0:T(8,128)S(1)}) custom-call(bf16[4,144,384]{2,1,0:T(8,128)(2,1)S(1)} %collect.1.refs_0_, bf16[4,2,128,128]{3,2,1,0:T(8,128)(2,1)S(1)} %collective-permute-done.7.refs_1_, f32[4,8,512]{2,1,0:T(8,128)S(1)} %get-tuple-element.32.refs_2_, ...), custom_call_target="tpu_custom_call" | custom-call | flops 1000000 | bytes 4000000 | tf_op jit(solution)/shard_map/attend_2/pallas_call | solution.py:365
  18.6 0.3 %attend_last_0.1 = bf16[4,128,384]{2,1,0:T(8,128)(2,1)S(1)} custom-call(bf16[4,144,384]{2,1,0:T(8,128)(2,1)S(1)} %collect.1.refs_0_, bf16[4,2,128,128]{3,2,1,0:T(8,128)(2,1)S(1)} %collective-permute-done.6.refs_1_, f32[4,8,512]{2,1,0:T(8,128)S(1)} %get-tuple-element.32.refs_2_, f32[4,128,128]{2,1,0:T(8,128)S(1)} %get-tuple-element.33.refs_3_, ...), custom_call_target="tpu_custom_call" | custom-call | flops 1000000 | bytes 4000000 | tf_op jit(solution)/shard_map/attend_last_0/pallas_call | solution.py:365
  19.0 1.1 %collective-permute-start.10 = (bf16[128,384]{1,0:T(8,128)(2,1)S(1)}, bf16[128,384]{1,0:T(8,128)(2,1)S(1)}, u32[]{:S(2)}, u32[]{:S(2)}) collective-permute-start(bf16[128,384]{1,0:T(8,128)(2,1)S(1)} %get-tuple-element.44), channel_id=1, source_target_pairs={{0,24},{8,16},{16,8},{24,0},{1,25},{9,17},{17,9},{25,1},{2,26},{10... | collective-permute-start | bytes 294920 | tf_op jit(solution)/shard_map/ppermute | solution.py:285
  20.1 1.0 %collective-permute-start.11 = (bf16[128,384]{1,0:T(8,128)(2,1)S(1)}, bf16[128,384]{1,0:T(8,128)(2,1)S(1)}, u32[]{:S(2)}, u32[]{:S(2)}) collective-permute-start(bf16[128,384]{1,0:T(8,128)(2,1)S(1)} %get-tuple-element.43), channel_id=1, source_target_pairs={{0,8},{8,0},{16,24},{24,16},{1,9},{9,1},{17,25},{25,17},{2,10},{10... | collective-permute-start | bytes 294920 | tf_op jit(solution)/shard_map/ppermute | solution.py:285
  21.1 1.4 %collective-permute-start.9 = (bf16[128,384]{1,0:T(8,128)(2,1)S(1)}, bf16[128,384]{1,0:T(8,128)(2,1)S(1)}, u32[]{:S(2)}, u32[]{:S(2)}) collective-permute-start(bf16[128,384]{1,0:T(8,128)(2,1)S(1)} %get-tuple-element.45), channel_id=1, source_target_pairs={{0,16},{8,24},{16,0},{24,8},{1,17},{9,25},{17,1},{25,9},{2,18},{10... | collective-permute-start | bytes 294920 | tf_op jit(solution)/shard_map/ppermute | solution.py:285
  22.5 2.0 %collective-permute-done.10.refs_2_ = bf16[128,384]{1,0:T(8,128)(2,1)S(1)} collective-permute-done((bf16[128,384]{1,0:T(8,128)(2,1)S(1)}, bf16[128,384]{1,0:T(8,128)(2,1)S(1)}, u32[]{:S(2)}, u32[]{:S(2)}) %collective-permute-start.10) | collective-permute-done | bytes 98336 | tf_op jit(solution)/shard_map/ppermute | solution.py:285
  24.6 0.2 collective-permute-done.11.refs_3_
  24.8 1.0 %collective-permute-done.9.refs_1_ = bf16[128,384]{1,0:T(8,128)(2,1)S(1)} collective-permute-done((bf16[128,384]{1,0:T(8,128)(2,1)S(1)}, bf16[128,384]{1,0:T(8,128)(2,1)S(1)}, u32[]{:S(2)}, u32[]{:S(2)}) %collective-permute-start.9) | collective-permute-done | bytes 98336 | tf_op jit(solution)/shard_map/ppermute | solution.py:285
  25.7 0.8 %join.1 = bf16[128,1536]{1,0:T(8,128)(2,1)} custom-call(bf16[128,384]{1,0:T(8,128)(2,1)S(1)} %get-tuple-element.46.refs_0_, bf16[128,384]{1,0:T(8,128)(2,1)S(1)} %collective-permute-done.9.refs_1_, bf16[128,384]{1,0:T(8,128)(2,1)S(1)} %collective-permute-done.10.refs_2_, bf16[128,384]{1,0:T(8,128)(2,1)S(1)} %collective-permute-done.11.refs_3_), custom_call_target="tpu_custom_call" | custom-call | tf_op jit(solution)/shard_map/join/pallas_call | solution.py:392
  (10 shorter events, 0.2 us)
Async XLA Ops:
  1.2 8.0 %collective-permute-start.3 = (bf16[2,128,128]{2,1,0:T(8,128)(2,1)S(1)}, bf16[2,128,128]{2,1,0:T(8,128)(2,1)S(1)}, u32[]{:S(2)}, u32[]{:S(2)}) collective-permute-start(bf16[2,128,128]{2,1,0:T(8,128)(2,1)S(1)} %get-tuple-element.29), channel_id=1, source_target_pairs={{0,8},{8,0},{16,24},{24,16},{1,9},{9,1},{17,25},{25,17},{2,10},{10... | collective-permute-start | bytes 196616 | tf_op jit(solution)/shard_map/ppermute | solution.py:285
  4.2 5.6 %collective-permute-start.4 = (bf16[2,128,128]{2,1,0:T(8,128)(2,1)S(1)}, bf16[2,128,128]{2,1,0:T(8,128)(2,1)S(1)}, u32[]{:S(2)}, u32[]{:S(2)}) collective-permute-start(bf16[2,128,128]{2,1,0:T(8,128)(2,1)S(1)} %get-tuple-element.30), channel_id=1, source_target_pairs={{0,16},{8,24},{16,0},{24,8},{1,17},{9,25},{17,1},{25,9},{2,18},{10... | collective-permute-start | bytes 196616 | tf_op jit(solution)/shard_map/ppermute | solution.py:285
  5.7 5.4 %collective-permute-start.5 = (bf16[2,128,128]{2,1,0:T(8,128)(2,1)S(1)}, bf16[2,128,128]{2,1,0:T(8,128)(2,1)S(1)}, u32[]{:S(2)}, u32[]{:S(2)}) collective-permute-start(bf16[2,128,128]{2,1,0:T(8,128)(2,1)S(1)} %get-tuple-element.31), channel_id=1, source_target_pairs={{0,24},{8,16},{16,8},{24,0},{1,25},{9,17},{17,9},{25,1},{2,26},{10... | collective-permute-start | bytes 196616 | tf_op jit(solution)/shard_map/ppermute | solution.py:285
  5.7 7.0 %collective-permute-start = (bf16[144,384]{1,0:T(8,128)(2,1)S(1)}, bf16[144,384]{1,0:T(8,128)(2,1)S(1)}, u32[]{:S(2)}, u32[]{:S(2)}) collective-permute-start(bf16[144,384]{1,0:T(8,128)(2,1)S(1)} %get-tuple-element.25), channel_id=1, source_target_pairs={{0,8},{8,0},{16,24},{24,16},{1,9},{9,1},{17,25},{25,17},{2,10},{10... | collective-permute-start | bytes 331784 | tf_op jit(solution)/shard_map/ppermute | solution.py:285
  7.7 5.9 %collective-permute-start.1 = (bf16[144,384]{1,0:T(8,128)(2,1)S(1)}, bf16[144,384]{1,0:T(8,128)(2,1)S(1)}, u32[]{:S(2)}, u32[]{:S(2)}) collective-permute-start(bf16[144,384]{1,0:T(8,128)(2,1)S(1)} %get-tuple-element.26), channel_id=1, source_target_pairs={{0,16},{8,24},{16,0},{24,8},{1,17},{9,25},{17,1},{25,9},{2,18},{10... | collective-permute-start | bytes 331784 | tf_op jit(solution)/shard_map/ppermute | solution.py:285
  9.2 5.6 %collective-permute-start.2 = (bf16[144,384]{1,0:T(8,128)(2,1)S(1)}, bf16[144,384]{1,0:T(8,128)(2,1)S(1)}, u32[]{:S(2)}, u32[]{:S(2)}) collective-permute-start(bf16[144,384]{1,0:T(8,128)(2,1)S(1)} %get-tuple-element.27), channel_id=1, source_target_pairs={{0,24},{8,16},{16,8},{24,0},{1,25},{9,17},{17,9},{25,1},{2,26},{10... | collective-permute-start | bytes 331784 | tf_op jit(solution)/shard_map/ppermute | solution.py:285
  11.1 6.4 %collective-permute-start.7 = (bf16[4,2,128,128]{3,2,1,0:T(8,128)(2,1)S(1)}, bf16[4,2,128,128]{3,2,1,0:T(8,128)(2,1)S(1)}, u32[]{:S(2)}, u32[]{:S(2)}) collective-permute-start(bf16[4,2,128,128]{3,2,1,0:T(8,128)(2,1)S(1)} %pad_maximum_fusion.own_ref.refs_1_), channel_id=1, source_target_pairs={{0,1},{1,0},{2,3},{3,2},{4,5},{5,4},{6,7},{7,6},{8,9},{9,8},{10,11... | collective-permute-start | bytes 786440 | tf_op jit(solution)/shard_map/ppermute | solution.py:54
  12.7 5.9 %collective-permute-start.6 = (bf16[4,2,128,128]{3,2,1,0:T(8,128)(2,1)S(1)}, bf16[4,2,128,128]{3,2,1,0:T(8,128)(2,1)S(1)}, u32[]{:S(2)}, u32[]{:S(2)}) collective-permute-start(bf16[4,2,128,128]{3,2,1,0:T(8,128)(2,1)S(1)} %pad_maximum_fusion.own_ref.refs_1_), channel_id=1, source_target_pairs={{0,4},{1,2},{2,1},{3,7},{4,0},{5,6},{6,5},{7,3},{8,12},{9,10},{10,... | collective-permute-start | bytes 786440 | tf_op jit(solution)/shard_map/ppermute | solution.py:54
  12.8 3.1 %collective-permute-start.8 = (bf16[4,2,128,128]{3,2,1,0:T(8,128)(2,1)S(1)}, bf16[4,2,128,128]{3,2,1,0:T(8,128)(2,1)S(1)}, u32[]{:S(2)}, u32[]{:S(2)}) collective-permute-start(bf16[4,2,128,128]{3,2,1,0:T(8,128)(2,1)S(1)} %copy.7), channel_id=1, source_target_pairs={{0,4},{1,5},{2,6},{3,7},{4,0},{5,1},{6,2},{7,3},{8,12},{9,13},{10,... | collective-permute-start | bytes 786440 | tf_op jit(solution)/shard_map/ppermute | solution.py:54
  19.0 5.6 %collective-permute-start.10 = (bf16[128,384]{1,0:T(8,128)(2,1)S(1)}, bf16[128,384]{1,0:T(8,128)(2,1)S(1)}, u32[]{:S(2)}, u32[]{:S(2)}) collective-permute-start(bf16[128,384]{1,0:T(8,128)(2,1)S(1)} %get-tuple-element.44), channel_id=1, source_target_pairs={{0,24},{8,16},{16,8},{24,0},{1,25},{9,17},{17,9},{25,1},{2,26},{10... | collective-permute-start | bytes 294920 | tf_op jit(solution)/shard_map/ppermute | solution.py:285
  20.1 4.7 %collective-permute-start.11 = (bf16[128,384]{1,0:T(8,128)(2,1)S(1)}, bf16[128,384]{1,0:T(8,128)(2,1)S(1)}, u32[]{:S(2)}, u32[]{:S(2)}) collective-permute-start(bf16[128,384]{1,0:T(8,128)(2,1)S(1)} %get-tuple-element.43), channel_id=1, source_target_pairs={{0,8},{8,0},{16,24},{24,16},{1,9},{9,1},{17,25},{25,17},{2,10},{10... | collective-permute-start | bytes 294920 | tf_op jit(solution)/shard_map/ppermute | solution.py:285
  21.1 4.6 %collective-permute-start.9 = (bf16[128,384]{1,0:T(8,128)(2,1)S(1)}, bf16[128,384]{1,0:T(8,128)(2,1)S(1)}, u32[]{:S(2)}, u32[]{:S(2)}) collective-permute-start(bf16[128,384]{1,0:T(8,128)(2,1)S(1)} %get-tuple-element.45), channel_id=1, source_target_pairs={{0,16},{8,24},{16,0},{24,8},{1,17},{9,25},{17,1},{25,9},{2,18},{10... | collective-permute-start | bytes 294920 | tf_op jit(solution)/shard_map/ppermute | solution.py:285

commit v9 on v8

--- a/solution.py
+++ b/solution.py
@@ -226,6 +226,7 @@
             ).astype(jnp.bfloat16)
 
     def run(some, used):
+        some = some[::-1]
         if used:
             score(some[0], used)
         for i, span in enumerate(some):

time: 26.9 us -> 26.7 us (level)
  no operation moved by 1% of the time
where the time goes in v9:
time: 26.7 us; the launch traced here: 26.5 us
  starting transfers between devices  14.4 us (54%)
  waiting for transfers between devices  6.55 us (25%)
  Pallas kernels  5.44 us (20%)
    ppermute x9, starting transfers between devices, exchange(): return lax.ppermute(block, 'span', [(i, i ^ k) for i in range(spans)])  12.2 us
    ppermute x9, waiting for transfers between devices, exchange(): return lax.ppermute(block, 'span', [(i, i ^ k) for i in range(spans)])  5.97 us
    pallas_call x4, Pallas kernels, stage(): pl.pallas_call(functools.partial(attend, spans, sizes, ways, numbers, cho...  3.43 us
    ppermute x3, starting transfers between devices, swap(): return lax.ppermute(block, ('ty', 'tx'), moves)  2.22 us
    pallas_call x1, Pallas kernels, shards(): pl.pallas_call(functools.partial(split, spans, sizes, ways), out_shape=[p...  1.16 us
    pallas_call x1, Pallas kernels, shards(): pl.pallas_call(functools.partial(join, places), out_shape=jax.ShapeDtypeS...  0.8 us
    ppermute x3, waiting for transfers between devices, swap(): return lax.ppermute(block, ('ty', 'tx'), moves)  0.58 us
  transfers between devices with their start and end apart: 12, of which 7 were waited for; matrix products, arithmetic and copies ran while one was open for 0% of the time, Pallas kernels for 12%

profile of v9, /device:TPU:0, one launch (start us, length us, event | category | flops | bytes accessed | tf_op | source)
XLA Modules:
  0.0 26.5 jit_solution(5994565533300766636)
XLA Ops:
  0.0 1.2 %split.1 = (bf16[2,128,128]{2,1,0:T(8,128)(2,1)S(1)}, bf16[2,128,128]{2,1,0:T(8,128)(2,1)S(1)}, bf16[2,128,128]{2,1,0:T(8,128)(2,1)S(1)}, bf16[2,128,128]{2,1,0:...) custom-call(s32[5]{0:T(128)} %bitcast.22, ...), custom_call_target="tpu_custom_call" | custom-call | tf_op jit(solution)/shard_map/split/pallas_call | solution.py:296
  1.2 3.0 %collective-permute-start.3 = (bf16[2,128,128]{2,1,0:T(8,128)(2,1)S(1)}, bf16[2,128,128]{2,1,0:T(8,128)(2,1)S(1)}, u32[]{:S(2)}, u32[]{:S(2)}) collective-permute-start(bf16[2,128,128]{2,1,0:T(8,128)(2,1)S(1)} %get-tuple-element.29), channel_id=1, source_target_pairs={{0,8},{8,0},{16,24},{24,16},{1,9},{9,1},{17,25},{25,17},{2,10},{10... | collective-permute-start | bytes 196616 | tf_op jit(solution)/shard_map/ppermute | solution.py:286
  4.2 1.5 %collective-permute-start.4 = (bf16[2,128,128]{2,1,0:T(8,128)(2,1)S(1)}, bf16[2,128,128]{2,1,0:T(8,128)(2,1)S(1)}, u32[]{:S(2)}, u32[]{:S(2)}) collective-permute-start(bf16[2,128,128]{2,1,0:T(8,128)(2,1)S(1)} %get-tuple-element.30), channel_id=1, source_target_pairs={{0,16},{8,24},{16,0},{24,8},{1,17},{9,25},{17,1},{25,9},{2,18},{10... | collective-permute-start | bytes 196616 | tf_op jit(solution)/shard_map/ppermute | solution.py:286
  5.7 0.0 collective-permute-start.5
  5.7 1.9 %collective-permute-start = (bf16[144,384]{1,0:T(8,128)(2,1)S(1)}, bf16[144,384]{1,0:T(8,128)(2,1)S(1)}, u32[]{:S(2)}, u32[]{:S(2)}) collective-permute-start(bf16[144,384]{1,0:T(8,128)(2,1)S(1)} %get-tuple-element.25), channel_id=1, source_target_pairs={{0,8},{8,0},{16,24},{24,16},{1,9},{9,1},{17,25},{25,17},{2,10},{10... | collective-permute-start | bytes 331784 | tf_op jit(solution)/shard_map/ppermute | solution.py:286
  7.7 1.5 %collective-permute-start.1 = (bf16[144,384]{1,0:T(8,128)(2,1)S(1)}, bf16[144,384]{1,0:T(8,128)(2,1)S(1)}, u32[]{:S(2)}, u32[]{:S(2)}) collective-permute-start(bf16[144,384]{1,0:T(8,128)(2,1)S(1)} %get-tuple-element.26), channel_id=1, source_target_pairs={{0,16},{8,24},{16,0},{24,8},{1,17},{9,25},{17,1},{25,9},{2,18},{10... | collective-permute-start | bytes 331784 | tf_op jit(solution)/shard_map/ppermute | solution.py:286
  9.2 0.6 %collective-permute-start.2 = (bf16[144,384]{1,0:T(8,128)(2,1)S(1)}, bf16[144,384]{1,0:T(8,128)(2,1)S(1)}, u32[]{:S(2)}, u32[]{:S(2)}) collective-permute-start(bf16[144,384]{1,0:T(8,128)(2,1)S(1)} %get-tuple-element.27), channel_id=1, source_target_pairs={{0,24},{8,16},{16,8},{24,0},{1,25},{9,17},{17,9},{25,1},{2,26},{10... | collective-permute-start | bytes 331784 | tf_op jit(solution)/shard_map/ppermute | solution.py:286
  9.8 1.3 %collective-permute-done.5 = bf16[2,128,128]{2,1,0:T(8,128)(2,1)S(1)} collective-permute-done((bf16[2,128,128]{2,1,0:T(8,128)(2,1)S(1)}, bf16[2,128,128]{2,1,0:T(8,128)(2,1)S(1)}, u32[]{:S(2)}, u32[]{:S(2)}) %collective-permute-start.5) | collective-permute-done | bytes 65568 | tf_op jit(solution)/shard_map/ppermute | solution.py:286
  11.1 1.6 %collective-permute-start.7 = (bf16[4,2,128,128]{3,2,1,0:T(8,128)(2,1)S(1)}, bf16[4,2,128,128]{3,2,1,0:T(8,128)(2,1)S(1)}, u32[]{:S(2)}, u32[]{:S(2)}) collective-permute-start(bf16[4,2,128,128]{3,2,1,0:T(8,128)(2,1)S(1)} %pad_maximum_fusion.own_ref.refs_1_), channel_id=1, source_target_pairs={{0,1},{1,0},{2,3},{3,2},{4,5},{5,4},{6,7},{7,6},{8,9},{9,8},{10,11... | collective-permute-start | bytes 786440 | tf_op jit(solution)/shard_map/ppermute | solution.py:54
  12.8 0.6 %collective-permute-start.8 = (bf16[4,2,128,128]{3,2,1,0:T(8,128)(2,1)S(1)}, bf16[4,2,128,128]{3,2,1,0:T(8,128)(2,1)S(1)}, u32[]{:S(2)}, u32[]{:S(2)}) collective-permute-start(bf16[4,2,128,128]{3,2,1,0:T(8,128)(2,1)S(1)} %copy.7), channel_id=1, source_target_pairs={{0,4},{1,5},{2,6},{3,7},{4,0},{5,1},{6,2},{7,3},{8,12},{9,13},{10,... | collective-permute-start | bytes 786440 | tf_op jit(solution)/shard_map/ppermute | solution.py:54
  13.3 0.2 collective-permute-done.1.refs_2_
  13.5 1.3 %collective-permute-done.2.refs_3_ = bf16[144,384]{1,0:T(8,128)(2,1)S(1)} collective-permute-done((bf16[144,384]{1,0:T(8,128)(2,1)S(1)}, bf16[144,384]{1,0:T(8,128)(2,1)S(1)}, u32[]{:S(2)}, u32[]{:S(2)}) %collective-permute-start.2) | collective-permute-done | bytes 110624 | tf_op jit(solution)/shard_map/ppermute | solution.py:286
  14.9 1.0 %attend_0.1 = (f32[4,384,128]{2,1,0:T(8,128)S(1)}, f32[4,384,128]{2,1,0:T(8,128)S(1)}, f32[4,384,128]{2,1,0:T(8,128)S(1)}) custom-call(bf16[4,144,384]{2,1,0:T(8,128)(2,1)S(1)} %collect.1.refs_0_, bf16[4,2,128,128]{3,2,1,0:T(8,128)(2,1)S(1)} %pad_maximum_fusion.own_ref.refs_1_, f32[4,8,512]{2,1,0:T(8,128)S(1)} %get-tuple-element.32.refs_2_, ...), custom_call_target="tpu_custom_call" | custom-call | flops 10000000000 | bytes 4000000 | tf_op jit(solution)/shard_map/attend_0/pallas_call | solution.py:366
  15.9 1.1 %attend_1.1 = (f32[4,384,128]{2,1,0:T(8,128)S(1)}, f32[4,384,128]{2,1,0:T(8,128)S(1)}, f32[4,384,128]{2,1,0:T(8,128)S(1)}) custom-call(bf16[4,144,384]{2,1,0:T(8,128)(2,1)S(1)} %collect.1.refs_0_, bf16[4,2,128,128]{3,2,1,0:T(8,128)(2,1)S(1)} %collective-permute-done.8.refs_1_, f32[4,8,512]{2,1,0:T(8,128)S(1)} %get-tuple-element.32.refs_2_, ...), custom_call_target="tpu_custom_call" | custom-call | flops 1000000 | bytes 4000000 | tf_op jit(solution)/shard_map/attend_1/pallas_call | solution.py:366
  16.9 0.6 %collective-permute-done.7.refs_1_ = bf16[4,2,128,128]{3,2,1,0:T(8,128)(2,1)S(1)} collective-permute-done((bf16[4,2,128,128]{3,2,1,0:T(8,128)(2,1)S(1)}, bf16[4,2,128,128]{3,2,1,0:T(8,128)(2,1)S(1)}, u32[]{:S(2)}, u32[]{:S(2)}) %collective-permute-start.7) | collective-permute-done | bytes 262176 | tf_op jit(solution)/shard_map/ppermute | solution.py:54
  17.5 1.1 %attend_2.1 = (f32[4,384,128]{2,1,0:T(8,128)S(1)}, f32[4,384,128]{2,1,0:T(8,128)S(1)}, f32[4,384,128]{2,1,0:T(8,128)S(1)}) custom-call(bf16[4,144,384]{2,1,0:T(8,128)(2,1)S(1)} %collect.1.refs_0_, bf16[4,2,128,128]{3,2,1,0:T(8,128)(2,1)S(1)} %collective-permute-done.7.refs_1_, f32[4,8,512]{2,1,0:T(8,128)S(1)} %get-tuple-element.32.refs_2_, ...), custom_call_target="tpu_custom_call" | custom-call | flops 1000000 | bytes 4000000 | tf_op jit(solution)/shard_map/attend_2/pallas_call | solution.py:366
  18.6 0.3 %attend_last_0.1 = bf16[4,128,384]{2,1,0:T(8,128)(2,1)S(1)} custom-call(bf16[4,144,384]{2,1,0:T(8,128)(2,1)S(1)} %collect.1.refs_0_, bf16[4,2,128,128]{3,2,1,0:T(8,128)(2,1)S(1)} %collective-permute-done.6.refs_1_, f32[4,8,512]{2,1,0:T(8,128)S(1)} %get-tuple-element.32.refs_2_, f32[4,128,128]{2,1,0:T(8,128)S(1)} %get-tuple-element.33.refs_3_, ...), custom_call_target="tpu_custom_call" | custom-call | flops 1000000 | bytes 4000000 | tf_op jit(solution)/shard_map/attend_last_0/pallas_call | solution.py:366
  19.0 1.1 %collective-permute-start.10 = (bf16[128,384]{1,0:T(8,128)(2,1)S(1)}, bf16[128,384]{1,0:T(8,128)(2,1)S(1)}, u32[]{:S(2)}, u32[]{:S(2)}) collective-permute-start(bf16[128,384]{1,0:T(8,128)(2,1)S(1)} %get-tuple-element.44), channel_id=1, source_target_pairs={{0,24},{8,16},{16,8},{24,0},{1,25},{9,17},{17,9},{25,1},{2,26},{10... | collective-permute-start | bytes 294920 | tf_op jit(solution)/shard_map/ppermute | solution.py:286
  20.1 1.0 %collective-permute-start.11 = (bf16[128,384]{1,0:T(8,128)(2,1)S(1)}, bf16[128,384]{1,0:T(8,128)(2,1)S(1)}, u32[]{:S(2)}, u32[]{:S(2)}) collective-permute-start(bf16[128,384]{1,0:T(8,128)(2,1)S(1)} %get-tuple-element.43), channel_id=1, source_target_pairs={{0,8},{8,0},{16,24},{24,16},{1,9},{9,1},{17,25},{25,17},{2,10},{10... | collective-permute-start | bytes 294920 | tf_op jit(solution)/shard_map/ppermute | solution.py:286
  21.1 1.4 %collective-permute-start.9 = (bf16[128,384]{1,0:T(8,128)(2,1)S(1)}, bf16[128,384]{1,0:T(8,128)(2,1)S(1)}, u32[]{:S(2)}, u32[]{:S(2)}) collective-permute-start(bf16[128,384]{1,0:T(8,128)(2,1)S(1)} %get-tuple-element.45), channel_id=1, source_target_pairs={{0,16},{8,24},{16,0},{24,8},{1,17},{9,25},{17,1},{25,9},{2,18},{10... | collective-permute-start | bytes 294920 | tf_op jit(solution)/shard_map/ppermute | solution.py:286
  22.5 2.0 %collective-permute-done.10.refs_2_ = bf16[128,384]{1,0:T(8,128)(2,1)S(1)} collective-permute-done((bf16[128,384]{1,0:T(8,128)(2,1)S(1)}, bf16[128,384]{1,0:T(8,128)(2,1)S(1)}, u32[]{:S(2)}, u32[]{:S(2)}) %collective-permute-start.10) | collective-permute-done | bytes 98336 | tf_op jit(solution)/shard_map/ppermute | solution.py:286
  24.6 0.2 collective-permute-done.11.refs_3_
  24.8 1.0 %collective-permute-done.9.refs_1_ = bf16[128,384]{1,0:T(8,128)(2,1)S(1)} collective-permute-done((bf16[128,384]{1,0:T(8,128)(2,1)S(1)}, bf16[128,384]{1,0:T(8,128)(2,1)S(1)}, u32[]{:S(2)}, u32[]{:S(2)}) %collective-permute-start.9) | collective-permute-done | bytes 98336 | tf_op jit(solution)/shard_map/ppermute | solution.py:286
  25.7 0.8 %join.1 = bf16[128,1536]{1,0:T(8,128)(2,1)} custom-call(bf16[128,384]{1,0:T(8,128)(2,1)S(1)} %get-tuple-element.46.refs_0_, bf16[128,384]{1,0:T(8,128)(2,1)S(1)} %collective-permute-done.9.refs_1_, bf16[128,384]{1,0:T(8,128)(2,1)S(1)} %collective-permute-done.10.refs_2_, bf16[128,384]{1,0:T(8,128)(2,1)S(1)} %collective-permute-done.11.refs_3_), custom_call_target="tpu_custom_call" | custom-call | tf_op jit(solution)/shard_map/join/pallas_call | solution.py:393
  (10 shorter events, 0.2 us)
Async XLA Ops:
  1.2 8.0 %collective-permute-start.3 = (bf16[2,128,128]{2,1,0:T(8,128)(2,1)S(1)}, bf16[2,128,128]{2,1,0:T(8,128)(2,1)S(1)}, u32[]{:S(2)}, u32[]{:S(2)}) collective-permute-start(bf16[2,128,128]{2,1,0:T(8,128)(2,1)S(1)} %get-tuple-element.29), channel_id=1, source_target_pairs={{0,8},{8,0},{16,24},{24,16},{1,9},{9,1},{17,25},{25,17},{2,10},{10... | collective-permute-start | bytes 196616 | tf_op jit(solution)/shard_map/ppermute | solution.py:286
  4.2 5.6 %collective-permute-start.4 = (bf16[2,128,128]{2,1,0:T(8,128)(2,1)S(1)}, bf16[2,128,128]{2,1,0:T(8,128)(2,1)S(1)}, u32[]{:S(2)}, u32[]{:S(2)}) collective-permute-start(bf16[2,128,128]{2,1,0:T(8,128)(2,1)S(1)} %get-tuple-element.30), channel_id=1, source_target_pairs={{0,16},{8,24},{16,0},{24,8},{1,17},{9,25},{17,1},{25,9},{2,18},{10... | collective-permute-start | bytes 196616 | tf_op jit(solution)/shard_map/ppermute | solution.py:286
  5.7 5.4 %collective-permute-start.5 = (bf16[2,128,128]{2,1,0:T(8,128)(2,1)S(1)}, bf16[2,128,128]{2,1,0:T(8,128)(2,1)S(1)}, u32[]{:S(2)}, u32[]{:S(2)}) collective-permute-start(bf16[2,128,128]{2,1,0:T(8,128)(2,1)S(1)} %get-tuple-element.31), channel_id=1, source_target_pairs={{0,24},{8,16},{16,8},{24,0},{1,25},{9,17},{17,9},{25,1},{2,26},{10... | collective-permute-start | bytes 196616 | tf_op jit(solution)/shard_map/ppermute | solution.py:286
  5.7 7.0 %collective-permute-start = (bf16[144,384]{1,0:T(8,128)(2,1)S(1)}, bf16[144,384]{1,0:T(8,128)(2,1)S(1)}, u32[]{:S(2)}, u32[]{:S(2)}) collective-permute-start(bf16[144,384]{1,0:T(8,128)(2,1)S(1)} %get-tuple-element.25), channel_id=1, source_target_pairs={{0,8},{8,0},{16,24},{24,16},{1,9},{9,1},{17,25},{25,17},{2,10},{10... | collective-permute-start | bytes 331784 | tf_op jit(solution)/shard_map/ppermute | solution.py:286
  7.7 5.9 %collective-permute-start.1 = (bf16[144,384]{1,0:T(8,128)(2,1)S(1)}, bf16[144,384]{1,0:T(8,128)(2,1)S(1)}, u32[]{:S(2)}, u32[]{:S(2)}) collective-permute-start(bf16[144,384]{1,0:T(8,128)(2,1)S(1)} %get-tuple-element.26), channel_id=1, source_target_pairs={{0,16},{8,24},{16,0},{24,8},{1,17},{9,25},{17,1},{25,9},{2,18},{10... | collective-permute-start | bytes 331784 | tf_op jit(solution)/shard_map/ppermute | solution.py:286
  9.2 5.6 %collective-permute-start.2 = (bf16[144,384]{1,0:T(8,128)(2,1)S(1)}, bf16[144,384]{1,0:T(8,128)(2,1)S(1)}, u32[]{:S(2)}, u32[]{:S(2)}) collective-permute-start(bf16[144,384]{1,0:T(8,128)(2,1)S(1)} %get-tuple-element.27), channel_id=1, source_target_pairs={{0,24},{8,16},{16,8},{24,0},{1,25},{9,17},{17,9},{25,1},{2,26},{10... | collective-permute-start | bytes 331784 | tf_op jit(solution)/shard_map/ppermute | solution.py:286
  11.1 6.4 %collective-permute-start.7 = (bf16[4,2,128,128]{3,2,1,0:T(8,128)(2,1)S(1)}, bf16[4,2,128,128]{3,2,1,0:T(8,128)(2,1)S(1)}, u32[]{:S(2)}, u32[]{:S(2)}) collective-permute-start(bf16[4,2,128,128]{3,2,1,0:T(8,128)(2,1)S(1)} %pad_maximum_fusion.own_ref.refs_1_), channel_id=1, source_target_pairs={{0,1},{1,0},{2,3},{3,2},{4,5},{5,4},{6,7},{7,6},{8,9},{9,8},{10,11... | collective-permute-start | bytes 786440 | tf_op jit(solution)/shard_map/ppermute | solution.py:54
  12.7 5.9 %collective-permute-start.6 = (bf16[4,2,128,128]{3,2,1,0:T(8,128)(2,1)S(1)}, bf16[4,2,128,128]{3,2,1,0:T(8,128)(2,1)S(1)}, u32[]{:S(2)}, u32[]{:S(2)}) collective-permute-start(bf16[4,2,128,128]{3,2,1,0:T(8,128)(2,1)S(1)} %pad_maximum_fusion.own_ref.refs_1_), channel_id=1, source_target_pairs={{0,4},{1,2},{2,1},{3,7},{4,0},{5,6},{6,5},{7,3},{8,12},{9,10},{10,... | collective-permute-start | bytes 786440 | tf_op jit(solution)/shard_map/ppermute | solution.py:54
  12.8 3.1 %collective-permute-start.8 = (bf16[4,2,128,128]{3,2,1,0:T(8,128)(2,1)S(1)}, bf16[4,2,128,128]{3,2,1,0:T(8,128)(2,1)S(1)}, u32[]{:S(2)}, u32[]{:S(2)}) collective-permute-start(bf16[4,2,128,128]{3,2,1,0:T(8,128)(2,1)S(1)} %copy.7), channel_id=1, source_target_pairs={{0,4},{1,5},{2,6},{3,7},{4,0},{5,1},{6,2},{7,3},{8,12},{9,13},{10,... | collective-permute-start | bytes 786440 | tf_op jit(solution)/shard_map/ppermute | solution.py:54
  19.0 5.6 %collective-permute-start.10 = (bf16[128,384]{1,0:T(8,128)(2,1)S(1)}, bf16[128,384]{1,0:T(8,128)(2,1)S(1)}, u32[]{:S(2)}, u32[]{:S(2)}) collective-permute-start(bf16[128,384]{1,0:T(8,128)(2,1)S(1)} %get-tuple-element.44), channel_id=1, source_target_pairs={{0,24},{8,16},{16,8},{24,0},{1,25},{9,17},{17,9},{25,1},{2,26},{10... | collective-permute-start | bytes 294920 | tf_op jit(solution)/shard_map/ppermute | solution.py:286
  20.1 4.7 %collective-permute-start.11 = (bf16[128,384]{1,0:T(8,128)(2,1)S(1)}, bf16[128,384]{1,0:T(8,128)(2,1)S(1)}, u32[]{:S(2)}, u32[]{:S(2)}) collective-permute-start(bf16[128,384]{1,0:T(8,128)(2,1)S(1)} %get-tuple-element.43), channel_id=1, source_target_pairs={{0,8},{8,0},{16,24},{24,16},{1,9},{9,1},{17,25},{25,17},{2,10},{10... | collective-permute-start | bytes 294920 | tf_op jit(solution)/shard_map/ppermute | solution.py:286
  21.1 4.6 %collective-permute-start.9 = (bf16[128,384]{1,0:T(8,128)(2,1)S(1)}, bf16[128,384]{1,0:T(8,128)(2,1)S(1)}, u32[]{:S(2)}, u32[]{:S(2)}) collective-permute-start(bf16[128,384]{1,0:T(8,128)(2,1)S(1)} %get-tuple-element.45), channel_id=1, source_target_pairs={{0,16},{8,24},{16,0},{24,8},{1,17},{9,25},{17,1},{25,9},{2,18},{10... | collective-permute-start | bytes 294920 | tf_op jit(solution)/shard_map/ppermute | solution.py:286
